TPU v7x, 32 devices: a whole 2x2x4 slice. The times are simulated.
32 devices in a mesh: groups: 2 (over x), pts: 16 (over z, y, core).
Axes of the slice: x: 2, y: 2, z: 4, core: 2. Of those that a mesh axis runs over, the one named last changes fastest.
Arguments:
- points: bfloat16 [8192, 512], P(('groups', 'pts')), parts along dimension 0, may hold values from -6 to 6
- labels: int32 [8192], P(('groups', 'pts')), parts along dimension 0, may hold values from 0 to 15
- centres: bfloat16 [32768, 512], P(('groups', 'pts')), parts along dimension 0, may hold values from -6 to 6
- tri_inverse: bfloat16 [32768, 16384], P(('groups', 'pts')), parts along dimension 0, as said below
- beta: bfloat16 [32768, 16], P(('groups', 'pts')), parts along dimension 0, may hold values from -0.01171875 to 0.01171875
- bias: float32 [32], P('groups'), parts along dimension 0, may hold values from -3.2 to -2.2
Outputs:
- gradient: float32 [32768, 16], P(('groups', 'pts')), parts along dimension 0
- logits: float32 [8192, 16], P(('groups', 'pts')), parts along dimension 0
There are 2 independent parts, one for each index of `groups`. A program takes and returns all parts, laid end to end along the dimension named above; each array names one. Nothing has to cross between parts.
Inputs may be any that keep to these rules, and one draw needn't show every extreme that they name: `tri_inverse`: upper triangular: entries below the diagonal are zero; the diagonal lies between 0.6 and 1.4.
All inputs are finite; a program needn't handle non-finite values.
Results may differ from a plain program's by a relative error of at most 0.0039.
Values may be sent and summed in bfloat16 or wider, within the bound.
No kernel may reach another device: no remote copies, remote signals or barrier semaphores. Data moves between devices by JAX's collectives and lax.ppermute only.
A program may use at most 128 MiB of HBM per device.

v0:
```python
import math

import jax
import jax.numpy as jnp
from jax import lax
from jax.sharding import PartitionSpec as P


def cube_kernel(point_block, centre_block):
    inner = lax.dot_general(
        point_block, centre_block, (((1,), (1,)), ((), ())), preferred_element_type=jnp.float32
    )
    factor = 1.0 / math.sqrt(point_block.shape[1])
    return ((inner * factor + 1.0) ** 3).astype(jnp.bfloat16)


def on_device(points, labels, centres, tri_inverse, beta, bias):
    local_points = points.shape[0]
    local_centres = centres.shape[0]
    class_count = beta.shape[1]
    packing = 128 // class_count
    dense_centres = local_centres // packing
    total_points = local_points * lax.axis_size("pts")
    beta_dense = beta.reshape(dense_centres, 128)
    beta_part = lax.all_gather(beta_dense, "pts", axis=0, tiled=True)
    narrow = beta_part.reshape(beta_part.shape[0] * packing, class_count)
    columns = tri_inverse
    alpha_sum = jnp.dot(columns, narrow, preferred_element_type=jnp.float32)
    alpha_local = alpha_sum.astype(jnp.bfloat16)
    alpha_dense = alpha_local.reshape(dense_centres, 128)
    classes_row = jnp.arange(class_count, dtype=jnp.int32)
    onehot = (labels[:, None] == classes_row[None, :]).astype(jnp.float32)
    parts_in = (
        lax.all_gather(centres, "pts", axis=0, tiled=True),
        lax.all_gather(alpha_dense, "pts", axis=0, tiled=True),
    )
    kernel_tile = cube_kernel(points, parts_in[0])
    narrow = parts_in[1].reshape(parts_in[1].shape[0] * packing, class_count)
    logit_sum = jnp.dot(kernel_tile, narrow, preferred_element_type=jnp.float32)
    logits = logit_sum + bias[None, :]
    resid = (jax.nn.sigmoid(logits) - onehot).astype(jnp.bfloat16)
    resid_dense = resid.reshape(local_points // packing, 128)
    parts_in = (
        lax.all_gather(points, "pts", axis=0, tiled=True),
        lax.all_gather(resid_dense, "pts", axis=0, tiled=True),
    )
    kernel_tile = cube_kernel(parts_in[0], centres)
    narrow = parts_in[1].reshape(parts_in[1].shape[0] * packing, class_count)
    grad_sum = lax.dot_general(
        kernel_tile, narrow, (((0,), (0,)), ((), ())), preferred_element_type=jnp.float32
    )
    grad_dense = grad_sum.reshape(dense_centres, 128)
    grad_kernel = (
        grad_dense.reshape(local_centres, class_count) * (1.0 / math.sqrt(total_points))
    ).astype(jnp.bfloat16)
    columns = tri_inverse
    term = lax.dot_general(
        columns, grad_kernel, (((0,), (0,)), ((), ())), preferred_element_type=jnp.float32
    )
    gradient_dense = lax.psum_scatter(
        term.reshape(lax.axis_size("pts") * dense_centres, 128),
        "pts",
        scatter_dimension=0,
        tiled=True,
    )
    return (gradient_dense.reshape(local_centres, class_count), logits)


def solution(mesh):
    return jax.shard_map(
        on_device,
        mesh=mesh,
        in_specs=(
            P(("groups", "pts"), None),
            P(("groups", "pts")),
            P(("groups", "pts"), None),
            P(("groups", "pts"), None),
            P(("groups", "pts"), None),
            P("groups"),
        ),
        out_specs=(P(("groups", "pts"), None), P(("groups", "pts"), None)),
        check_vma=False,
    )
```

profile of v0, /device:TPU:0, one launch (start us, length us, event | category | flops | bytes accessed | tf_op | source)
XLA Modules:
  0.0 295.1 jit_solution(16298011855423108095)
XLA Ops:
  7.2 0.7 all-gather.5.cloned.1.call-update
  7.9 0.7 all-gather.3.cloned.1.call-update
  8.7 0.9 copy.8
  9.6 0.2 reshape.30
  9.8 26.2 %all_gather.17 = bf16[2048,128]{1,0:T(8,128)(2,1)S(1)} all-gather(bf16[128,128]{1,0:T(8,128)(2,1)S(1)} %reshape.30), channel_id=1, replica_groups=mesh['groups'=2,'pts'=16] {'pts'}, dimensions={0}, use_global_device_ids=true | all-gather | bytes 557056 | tf_op jit(solution)/shard_map/all_gather | solution.py:25
  36.0 4.0 %reshape.31 = bf16[16384,16]{1,0:T(8,128)(2,1)} reshape(bf16[2048,128]{1,0:T(8,128)(2,1)S(1)} %all_gather.17) | data formatting | bytes 1048576 | tf_op jit(solution)/shard_map/reshape | solution.py:26
  40.0 15.4 %convolution_convert_fusion = bf16[1024,16]{0,1:T(8,128)(2,1)S(1)} fusion(bf16[1024,16384]{1,0:T(8,128)(2,1)} %param.9, bf16[16384,16]{1,0:T(8,128)(2,1)} %reshape.31), kind=kOutput, calls=%fused_computation.11 | convolution fusion | flops 536887296 | bytes 34111488 | tf_op jit(solution)/shard_map/dot_general | solution.py:28
  55.4 0.2 copy.9
  55.6 0.2 reshape.32
  55.8 20.0 %all_gather.18 = bf16[2048,128]{1,0:T(8,128)(2,1)S(1)} all-gather(bf16[128,128]{1,0:T(8,128)(2,1)S(1)} %reshape.32), channel_id=1, replica_groups=mesh['groups'=2,'pts'=16] {'pts'}, dimensions={0}, use_global_device_ids=true | all-gather | bytes 557056 | tf_op jit(solution)/shard_map/all_gather | solution.py:35
  75.8 4.0 %reshape.33 = bf16[16384,16]{1,0:T(8,128)(2,1)} reshape(bf16[2048,128]{1,0:T(8,128)(2,1)S(1)} %all_gather.18) | data formatting | bytes 1048576 | tf_op jit(solution)/shard_map/reshape | solution.py:38
  79.8 62.1 %all-gather.5.cloned.1.call-done = bf16[16384,512]{1,0:T(8,128)(2,1)} async-done(((bf16[1024,512]{1,0:T(8,128)(2,1)}), bf16[16384,512]{1,0:T(8,128)(2,1)}) %all-gather.5.cloned.1.call-update) | async-done | bytes 16777232 | tf_op jit(solution)/shard_map/all_gather | solution.py:34
  141.9 11.7 %subtract_convert_fusion = (bf16[256,16]{0,1:T(8,128)(2,1)S(1)}, f32[256,16]{0,1:T(8,128)}) fusion(s32[256]{0:T(256)S(1)} %copy-done.2, f32[16]{0:T(128)S(1)} %copy-done.3, bf16[16384,16]{1,0:T(8,128)(2,1)} %reshape.33, bf16[256,512]{1,0:T(8,128)(2,1)S(1)} %copy-done.1, bf16[16384,512]{1,0:T(8,128)(2,1)} %all-gather.5.cloned.1.call-done), kind=kOutput, calls=%fused_computation.13 | convolution fusion | flops 4450189312 | bytes 17589312 | tf_op jit(solution)/shard_map/dot_general | solution.py:39
  153.6 0.1 copy.10
  153.8 19.5 %all_gather.19 = bf16[512,128]{1,0:T(8,128)(2,1)S(1)} all-gather(bf16[32,128]{1,0:T(8,128)(2,1)S(1)} %reshape.34), channel_id=1, replica_groups=mesh['groups'=2,'pts'=16] {'pts'}, dimensions={0}, use_global_device_ids=true | all-gather | bytes 139264 | tf_op jit(solution)/shard_map/all_gather | solution.py:45
  173.3 0.7 reshape.35
  174.0 19.6 %all-gather.3.cloned.1.call-done = bf16[4096,512]{1,0:T(8,128)(2,1)} async-done(((bf16[256,512]{1,0:T(8,128)(2,1)}), bf16[4096,512]{1,0:T(8,128)(2,1)}) %all-gather.3.cloned.1.call-update) | async-done | bytes 4194320 | tf_op jit(solution)/shard_map/all_gather | solution.py:44
  193.6 12.9 %fusion.10 = bf16[1024,16]{1,0:T(8,128)(2,1)S(1)} fusion(bf16[4096,16]{1,0:T(8,128)(2,1)S(1)} %reshape.35, bf16[4096,512]{1,0:T(8,128)(2,1)} %all-gather.3.cloned.1.call-done, bf16[1024,512]{1,0:T(8,128)(2,1)S(1)} %copy-done), kind=kOutput, calls=%fused_computation.10 | convolution fusion | flops 4450189312 | bytes 5406720 | tf_op jit(solution)/shard_map/dot_general | solution.py:49
  206.5 13.1 %convolution_bitcast_fusion = f32[16384,16]{0,1:T(8,128)S(1)} fusion(bf16[1024,16]{1,0:T(8,128)(2,1)S(1)} %fusion.10, bf16[1024,16384]{1,0:T(8,128)(2,1)} %param.9), kind=kOutput, calls=%fused_computation.5 | convolution fusion | flops 536870912 | bytes 34635776 | tf_op jit(solution)/shard_map/dot_general | solution.py:57
  219.6 4.6 %copy.11 = f32[16384,16]{1,0:T(8,128)} copy(f32[16384,16]{0,1:T(8,128)S(1)} %convolution_bitcast_fusion) | data formatting | bytes 2097152 | tf_op jit(solution)/shard_map/dot_general | solution.py:57
  224.2 6.5 %reshape.36 = f32[2048,128]{1,0:T(8,128)} reshape(f32[16384,16]{1,0:T(8,128)} %copy.11) | data formatting | bytes 2097152 | tf_op jit(solution)/shard_map/reshape | solution.py:61
  230.7 56.0 %reduce-scatter.2.cloned.1.call-done = f32[128,128]{1,0:T(8,128)} async-done(((f32[2048,128]{1,0:T(8,128)}), f32[128,128]{1,0:T(8,128)}) %reduce-scatter.2.cloned.1.call-update) | async-done | bytes 65552 | tf_op jit(solution)/shard_map/reduce_scatter | solution.py:60
  286.7 1.0 reshape.37
  287.7 0.8 copy.12
  (13 shorter events, 0.3 us)
Async XLA Ops:
  7.2 134.7 %all-gather.5.cloned.1.call-start = ((), (), s32[]{:S(2)}) async-start(), calls=%async_computation.2 | async-start | bytes 17825792 | tf_op jit(solution)/shard_map/all_gather | solution.py:34
  7.9 185.7 %all-gather.3.cloned.1.call-start = ((), (), s32[]{:S(2)}) async-start(), calls=%async_computation.1 | async-start | bytes 4456448 | tf_op jit(solution)/shard_map/all_gather | solution.py:44
  8.6 278.0 %reduce-scatter.2.cloned.1.call-start = ((), (), s32[]{:S(2)}) async-start(), calls=%async_computation.3 | async-start | bytes 1114112 | tf_op jit(solution)/shard_map/reduce_scatter | solution.py:60
  40.0 101.9 %copy-start.1 = (bf16[256,512]{1,0:T(8,128)(2,1)S(1)}, bf16[256,512]{1,0:T(8,128)(2,1)}, u32[]{:S(2)}) copy-start(bf16[256,512]{1,0:T(8,128)(2,1)} %param.6) | copy-start | bytes 786436
  40.0 101.9 %copy-start.2 = (s32[256]{0:T(256)S(1)}, s32[256]{0:T(256)}, u32[]{:S(2)}) copy-start(s32[256]{0:T(256)} %param.7) | copy-start | bytes 3076
  40.0 101.9 %copy-start.3 = (f32[16]{0:T(128)S(1)}, f32[16]{0:T(128)}, u32[]{:S(2)}) copy-start(f32[16]{0:T(128)} %param.11) | copy-start | bytes 196
  79.8 113.8 %copy-start = (bf16[1024,512]{1,0:T(8,128)(2,1)S(1)}, bf16[1024,512]{1,0:T(8,128)(2,1)}, u32[]{:S(2)}) copy-start(bf16[1024,512]{1,0:T(8,128)(2,1)} %param.8) | copy-start | bytes 3145732
Sparse Core Ops, SparseCore 0:
  10.2 131.6 all-gather.4
  144.0 49.5 all-gather.2
  230.8 55.8 reduce-scatter.1
where the time goes:
time: 295 us
  waiting for transfers between devices  139 us (47%)
  blocking collectives  65.7 us (22%)
  matrix products  53.1 us (18%)
  local copies, waits for them, and re-layouts  23.3 us (8%)
  between operations  13.8 us (5%)
    all_gather x1, waiting for transfers between devices, on_device(): lax.all_gather(centres, 'pts', axis=0, tiled=True)  62.1 us
    reduce_scatter x1, waiting for transfers between devices, on_device(): lax.psum_scatter(term.reshape(lax.axis_size('pts') * dense_centres, 128),...  56 us
    all_gather x1, blocking collectives, on_device(): beta_part = lax.all_gather(beta_dense, 'pts', axis=0, tiled=True)  26.2 us
    all_gather x1, blocking collectives, on_device(): lax.all_gather(alpha_dense, 'pts', axis=0, tiled=True)  20 us
    all_gather x1, waiting for transfers between devices, on_device(): lax.all_gather(points, 'pts', axis=0, tiled=True)  19.6 us
    all_gather x1, blocking collectives, on_device(): lax.all_gather(resid_dense, 'pts', axis=0, tiled=True)  19.5 us
    dot_general x1, matrix products, on_device(): alpha_sum = jnp.dot(columns, narrow, preferred_element_type=jnp.float32)  15.4 us
    dot_general x1, matrix products, on_device(): lax.dot_general(columns, grad_kernel, (((0,), (0,)), ((), ())), preferred...  13.1 us
  transfers between devices with their start and end apart: 3, of which 3 were waited for; matrix products, arithmetic and copies ran while one was open for 13% of the time, Pallas kernels for 0%

commit v1 on v0

v1 whole, which is shorter than its diff:
```python
import math

import jax
import jax.numpy as jnp
from jax import lax
from jax.experimental import pallas as pl
from jax.experimental.pallas import tpu as pltpu
from jax.sharding import PartitionSpec as P

BF16 = jnp.bfloat16
F32 = jnp.float32
ROWS_BY_ROWS = (((1,), (1,)), ((), ()))
MIB = 1 << 20
IN_FLIGHT = 3


def params(mib):
    return pltpu.CompilerParams(vmem_limit_bytes=mib * MIB)


def in_vmem():
    return pl.BlockSpec(memory_space=pltpu.VMEM)


def anywhere():
    return pl.BlockSpec(memory_space=pl.ANY)


def in_smem():
    return pl.BlockSpec(memory_space=pltpu.SMEM)


def cost(flops, bytes_accessed):
    return pl.CostEstimate(flops=int(flops), bytes_accessed=int(bytes_accessed), transcendentals=0)


def alpha_step(me, offsets, coeffs, tri, total, last):
    rows = tri.shape[0]
    count, classes, width = coeffs.shape
    ahead = min(IN_FLIGHT, count)

    def body(*refs):
        me_ref, tri_ref, coeff_ref = refs[:3]
        out_ref, held_ref, sems = refs[-3:]
        copies = [
            pltpu.make_async_copy(
                tri_ref.at[:, pl.ds(pl.multiple_of((me_ref[0] ^ offset) * width, width), width)],
                held_ref.at[at],
                sems.at[at],
            )
            for at, offset in enumerate(offsets)
        ]
        for copy in copies[:ahead]:
            copy.start()
        acc = None if total is None else refs[3][...]
        for at in range(count):
            copies[at].wait()
            if at + ahead < count:
                copies[at + ahead].start()
            term = lax.dot_general(coeff_ref[at], held_ref[at], ROWS_BY_ROWS, preferred_element_type=F32)
            acc = term if acc is None else acc + term
        out_ref[...] = acc.astype(out_ref.dtype)

    operands = (me, tri, coeffs) + (() if total is None else (total,))
    return pl.pallas_call(
        body,
        out_shape=[
            jax.ShapeDtypeStruct((classes, rows), BF16 if last else F32),
            pltpu.VMEM((count, rows, width), BF16),
        ],
        in_specs=[in_smem(), anywhere()] + [in_vmem()] * (len(operands) - 2),
        out_specs=[in_vmem(), in_vmem()],
        scratch_shapes=[pltpu.SemaphoreType.DMA((count,))],
        compiler_params=params(8),
        cost_estimate=cost(2 * rows * count * width * 128, 2 * rows * count * width),
        name="alpha_step",
    )(*operands)


def gradient_terms(grad, blocks, first, count):
    classes, rows = grad.shape
    width = blocks.shape[2]

    def body(grad_ref, block_ref, out_ref):
        for at in range(count):
            out_ref[at] = jnp.dot(grad_ref[...], block_ref[first + at], preferred_element_type=F32)

    return pl.pallas_call(
        body,
        out_shape=jax.ShapeDtypeStruct((count, classes, width), F32),
        in_specs=[in_vmem(), in_vmem()],
        out_specs=in_vmem(),
        compiler_params=params(8),
        cost_estimate=cost(2 * rows * count * width * 128, 1024),
        name="gradient_terms",
    )(grad, pltpu.with_memory_space_constraint(blocks, pltpu.VMEM))


def kernel_tile(points, centre_blocks, after):
    block, features = points[0].shape
    local = sum(piece.shape[0] for piece in centre_blocks[0])
    factor = 1.0 / math.sqrt(features)
    pieces = [piece for pieces in centre_blocks for piece in pieces]
    total = len(points) * block

    def body(*refs):
        point_refs, piece_refs, out_ref = refs[: len(points)], refs[len(points) : -2], refs[-1]
        row = 0
        for piece_ref in piece_refs:
            which, first, rows = row // local, row % local, piece_ref.shape[0]
            for at, point_ref in enumerate(point_refs):
                inner = lax.dot_general(
                    piece_ref[...], point_ref[...], ROWS_BY_ROWS, preferred_element_type=F32
                )
                value = inner * factor + 1.0
                out_ref[which, first : first + rows, at * block : (at + 1) * block] = (
                    value * value * value
                ).astype(BF16)
            row += rows

    return pl.pallas_call(
        body,
        out_shape=pltpu.VMEM((len(centre_blocks), local, total), BF16),
        in_specs=[in_vmem()] * (len(points) + len(pieces)) + [anywhere()],
        out_specs=in_vmem(),
        compiler_params=params(8),
        cost_estimate=cost(2 * total * len(centre_blocks) * local * features, 1024),
        name="kernel_tile",
    )(*points, *pieces, after)


def partial_logits(tiles, alphas):
    classes = alphas[0].shape[0]
    sizes = [row[0].shape[2] for row in tiles]
    flat = [tile for row in tiles for tile in row]
    counts = [tile.shape[0] for tile in tiles[0]]

    def body(*refs):
        alpha_refs, tile_refs, out_ref = refs[: len(alphas)], refs[len(alphas) : -1], refs[-1]
        for part, size in enumerate(sizes):
            first = sum(sizes[:part])
            acc = None
            index = 0
            for which, count in enumerate(counts):
                tile_ref = tile_refs[part * len(counts) + which]
                for at in range(count):
                    term = jnp.dot(alpha_refs[index][...], tile_ref[at], preferred_element_type=F32)
                    acc = term if acc is None else acc + term
                    index += 1
            out_ref[:, first : first + size] = acc

    return pl.pallas_call(
        body,
        out_shape=jax.ShapeDtypeStruct((classes, sum(sizes)), F32),
        in_specs=[in_vmem()] * (len(alphas) + len(flat)),
        out_specs=in_vmem(),
        compiler_params=params(8),
        cost_estimate=cost(2 * sum(tile.size for tile in flat) * 128, 1024),
        name="partial_logits",
    )(*alphas, *flat)


def kernel_gradient(logit_sum, received, order, bias, onehots, hot_order, tiles):
    flat = [tile for row in tiles for tile in row]
    n_parts = len(tiles[0])
    local = flat[0].shape[1]
    sizes = [row[0].shape[2] for row in tiles]
    classes, total = logit_sum.shape
    block = total // len(order)

    def body(sum_ref, received_ref, bias_ref, onehot_ref, *refs):
        tile_refs, out_refs, (logits_ref, resid_ref) = refs[: len(flat)], refs[len(flat) : -2], refs[-2:]
        for at, source in enumerate(order):
            here = slice(at * block, (at + 1) * block)
            there = slice(source * block, (source + 1) * block)
            logits = sum_ref[:, here] + received_ref[:, there] + bias_ref[:, :1]
            if at == 0:
                logits_ref[...] = logits
            resid_ref[:, here] = (jax.nn.sigmoid(logits) - onehot_ref[hot_order[at]].astype(F32)).astype(BF16)
        for parity, out_ref in enumerate(out_refs):
            for which in range(n_parts):
                acc = None
                for part, size in enumerate(sizes):
                    first = sum(sizes[:part])
                    term = lax.dot_general(
                        resid_ref[:, first : first + size],
                        tile_refs[part * n_parts + which][parity],
                        ROWS_BY_ROWS,
                        preferred_element_type=F32,
                    )
                    acc = term if acc is None else acc + term
                out_ref[which] = acc

    return pl.pallas_call(
        body,
        out_shape=[jax.ShapeDtypeStruct((n_parts, classes, local), F32)] * 2
        + [jax.ShapeDtypeStruct((classes, block), F32)],
        in_specs=[in_vmem()] * (4 + len(flat)),
        out_specs=[in_vmem()] * 3,
        scratch_shapes=[pltpu.VMEM((classes, total), BF16)],
        compiler_params=params(8),
        cost_estimate=cost(2 * sum(tile.size for tile in flat) * 128, 1024),
        name="kernel_gradient",
    )(logit_sum, received, bias, onehots, *flat)


def on_device(points, labels, centres, tri_inverse, beta, bias):
    devices = lax.axis_size("pts")
    local_centres, classes = beta.shape
    total_points = points.shape[0] * devices
    outer = [1 << bit for bit in range(2, devices.bit_length() - 1)]

    def swap(array, mask):
        return lax.ppermute(array, "pts", [(index, index ^ mask) for index in range(devices)])

    tri_inverse = pltpu.with_memory_space_constraint(tri_inverse, pltpu.HBM)
    me = lax.axis_index("pts").astype(jnp.int32).reshape(1)
    bias_column = jnp.broadcast_to(bias[:, None], (classes, 128))
    class_column = jnp.arange(classes, dtype=jnp.int32)[:, None]
    onehot = (labels[None, :] == class_column).astype(BF16)

    half = local_centres // 2
    centres_2 = [swap(centres[:half], 2)]
    stack = jnp.concatenate([beta.T, onehot], axis=1)[None]
    far = [0]
    for mask in reversed(outer):
        stack = jnp.concatenate([stack, swap(stack, mask)])
        far = far + [offset ^ mask for offset in far]
    count = len(far)
    points_late, stack = lax.optimization_barrier((points, stack))
    onehots = stack[:, :, local_centres:]
    coeffs = stack[:, :, :local_centres]
    received = swap(coeffs, 2)
    near, distant = swap(points_late, outer[0]), swap(points_late, outer[-1])
    alpha, tri_0 = alpha_step(me, far, coeffs, tri_inverse, None, False)
    centres_late, received, near = lax.optimization_barrier((centres, received, near))
    centres_2 = centres_2 + [swap(centres_late[half:], 2)]
    near_2 = [offset ^ 2 for offset in far]
    alpha, tri_2 = alpha_step(me, near_2, received, tri_inverse, alpha, False)
    received = swap(jnp.concatenate([coeffs, received]), 1)
    received, distant = lax.optimization_barrier((received, distant))
    far_points = {0: points, outer[0]: near, outer[-1]: distant}
    for mask in outer[1:-1]:
        far_points[mask] = swap(points_late, mask)
    for offset in far:
        if offset not in far_points:
            low = offset & -offset
            far_points[offset] = swap(far_points[offset ^ low], low)
    near_13 = [offset ^ 1 for offset in far + near_2]
    alpha, tri_13 = alpha_step(me, near_13, received, tri_inverse, alpha, True)

    point_blocks = [far_points[offset] for offset in far]
    point_parts = [[at for at, offset in enumerate(far) if offset < outer[-1]]]
    point_parts = point_parts + [[at for at in range(count) if at not in point_parts[0]]]
    far_parts = [far[at] for part in point_parts for at in part]
    *centres_2, latest = lax.optimization_barrier((*centres_2, alpha))
    centres_3 = [swap(piece, 1) for piece in centres_2]
    centre_parts = [[[centres], [swap(centres, 1)]], [centres_2, centres_3]]
    tiles = []
    for part in point_parts:
        row = []
        for centre_part in centre_parts:
            latest = kernel_tile([point_blocks[at] for at in part], centre_part, latest)
            row.append(latest)
        tiles.append(row)
    alpha_2 = swap(alpha, 2)
    alpha_1 = swap(alpha, 1)
    alpha_3 = swap(alpha_2, 1)
    logit_sum = partial_logits(tiles, (alpha, alpha_1, alpha_2, alpha_3))

    block = points.shape[0]
    for mask in outer:
        received = swap(logit_sum, mask)
        order = [far_parts.index(offset ^ mask) for offset in far_parts]
        if mask != outer[-1]:
            moved = [received[:, source * block : (source + 1) * block] for source in order]
            logit_sum = logit_sum + jnp.concatenate(moved, axis=1)
    keep, send, logits = kernel_gradient(logit_sum, received, order, bias_column, onehots, [far.index(offset) for offset in far_parts], tiles)

    received = swap(send, 1)
    received_2 = swap(keep[1] + received[1], 2)
    grad = ((keep[0] + received[0] + received_2) * (1.0 / math.sqrt(total_points))).astype(BF16)

    term_3 = gradient_terms(grad, tri_13, count, count)
    received_3 = swap(term_3, 1)
    term_2 = gradient_terms(grad, tri_2, 0, count)
    received_2 = swap(term_2 + received_3, 2)
    term_1 = gradient_terms(grad, tri_13, 0, count)
    received_1 = swap(term_1, 1)
    term_0 = gradient_terms(grad, tri_0, 0, count)
    total = term_0 + received_1 + received_2
    held = list(far)
    for mask in outer:
        keep = [at for at, offset in enumerate(held) if not offset & mask]
        send = [held.index(held[at] ^ mask) for at in keep]
        received = swap(jnp.stack([total[at] for at in send]), mask)
        total = jnp.stack([total[at] for at in keep]) + received
        held = [held[at] for at in keep]
    return (total[0].T, logits.T)


def solution(mesh):
    return jax.shard_map(
        on_device,
        mesh=mesh,
        in_specs=(
            P(("groups", "pts"), None),
            P(("groups", "pts")),
            P(("groups", "pts"), None),
            P(("groups", "pts"), None),
            P(("groups", "pts"), None),
            P("groups"),
        ),
        out_specs=(P(("groups", "pts"), None), P(("groups", "pts"), None)),
        check_vma=False,
    )
```

time: 295 us -> 99.4 us (0.34)
  waiting for transfers between devices: 139 us -> 37.4 us
  blocking collectives: 65.7 us -> 0 us
  matrix products: 53.1 us -> 0 us
  Pallas kernels: 0 us -> 29.9 us
  starting transfers between devices: 0.11 us -> 24.1 us
  local copies, waits for them, and re-layouts: 23.3 us -> 3.9 us
  between operations: 13.8 us -> 0.84 us
  other arithmetic: 0 us -> 2.97 us
    all_gather x2 -> x0, waiting for transfers between devices: 81.7 us -> none  [the longest x1 62.1 us: on_device(): lax.all_gather(centres, 'pts', axis=0, tiled=True)]
    all_gather x3 -> x0, blocking collectives: 65.7 us -> none  [the longest x1 26.2 us: on_device(): beta_part = lax.all_gather(beta_dense, 'pts', axis=0, tiled=True)]
    reduce_scatter x1 -> x0, waiting for transfers between devices: 56 us -> none  [on_device(): lax.psum_scatter(term.reshape(lax.axis_size('pts') * dense_centres, 128),...]
    dot_general x4 -> x0, matrix products: 53.1 us -> none  [the longest x1 15.4 us: on_device(): alpha_sum = jnp.dot(columns, narrow, preferred_element_type=jnp.float32)]
    ppermute x0 -> x24, waiting for transfers between devices: none -> 37.4 us  [swap(): lax.ppermute(array, 'pts', [(index, index ^ mask) for index in range(devi...]
    pallas_call x0 -> x13, Pallas kernels: none -> 29.9 us  [the longest x3 16.2 us: alpha_step(): pl.pallas_call(body, out_shape=[jax.ShapeDtypeStruct((classes, rows), BF1...]
    ppermute x0 -> x24, starting transfers between devices: none -> 24.1 us  [swap(): lax.ppermute(array, 'pts', [(index, index ^ mask) for index in range(devi...]
    reshape x8 -> x0, local copies, waits for them, and re-layouts: 16.6 us -> none  [the longest x1 6.45 us: on_device(): term.reshape(lax.axis_size('pts') * dense_centres, 128)]
  transfers between devices with their start and end apart: 3 -> 24, of which waited for: 3 -> 12; matrix products, arithmetic and copies ran while one was open for 13% -> 5% of each run, Pallas kernels for 0% -> 25%
where the time goes in v1:
time: 99.4 us; the launch traced here: 99.1 us
  waiting for transfers between devices  37.4 us (38%)
  Pallas kernels  29.9 us (30%)
  starting transfers between devices  24.1 us (24%)
  local copies, waits for them, and re-layouts  3.9 us (4%)
  other arithmetic  2.97 us (3%)
    ppermute x24, waiting for transfers between devices, swap(): lax.ppermute(array, 'pts', [(index, index ^ mask) for index in range(devi...  37.4 us
    ppermute x24, starting transfers between devices, swap(): lax.ppermute(array, 'pts', [(index, index ^ mask) for index in range(devi...  24.1 us
    pallas_call x3, Pallas kernels, alpha_step(): pl.pallas_call(body, out_shape=[jax.ShapeDtypeStruct((classes, rows), BF1...  16.2 us
    pallas_call x4, Pallas kernels, kernel_tile(): pl.pallas_call(body, out_shape=pltpu.VMEM((len(centre_blocks), local, tot...  5.26 us
    pallas_call x4, Pallas kernels, gradient_terms(): pl.pallas_call(body, out_shape=jax.ShapeDtypeStruct((count, classes, widt...  4.79 us
    pallas_call x1, Pallas kernels, kernel_gradient(): pl.pallas_call(body, out_shape=[jax.ShapeDtypeStruct((n_parts, classes, l...  2.29 us
  transfers between devices with their start and end apart: 24, of which 12 were waited for; matrix products, arithmetic and copies ran while one was open for 5% of the time, Pallas kernels for 25%

profile of v1, /device:TPU:0, one launch (start us, length us, event | category | flops | bytes accessed | tf_op | source)
XLA Modules:
  0.0 99.1 jit_solution(15600307058456444290)
XLA Ops:
  2.1 4.0 %collective-permute-start = (bf16[1,16,1280]{2,1,0:T(8,128)(2,1)S(1)}, bf16[1,16,1280]{2,1,0:T(8,128)(2,1)S(1)}, u32[]{:S(2)}, u32[]{:S(2)}) collective-permute-start(bf16[1,16,1280]{2,1,0:T(8,128)(2,1)S(1)} %maximum_bitcast_fusion), channel_id=1, source_target_pairs={{0,8},{1,9},{2,10},{3,11},{4,12},{5,13},{6,14},{7,15},{8,0},{9,1},... | collective-permute-start | bytes 122888 | tf_op jit(solution)/shard_map/ppermute | solution.py:214
  6.1 2.4 %collective-permute-done = bf16[1,16,1280]{2,1,0:T(8,128)(2,1)S(1)} collective-permute-done((bf16[1,16,1280]{2,1,0:T(8,128)(2,1)S(1)}, bf16[1,16,1280]{2,1,0:T(8,128)(2,1)S(1)}, u32[]{:S(2)}, u32[]{:S(2)}) %collective-permute-start) | collective-permute-done | bytes 40992 | tf_op jit(solution)/shard_map/ppermute | solution.py:214
  8.5 1.5 %collective-permute-start.1 = (bf16[2,16,1280]{2,1,0:T(8,128)(2,1)S(1)}, bf16[2,16,1280]{2,1,0:T(8,128)(2,1)S(1)}, u32[]{:S(2)}, u32[]{:S(2)}) collective-permute-start(bf16[2,16,1280]{2,1,0:T(8,128)(2,1)S(1)} %pad_maximum_fusion.2), channel_id=1, source_target_pairs={{0,4},{1,5},{2,6},{3,7},{4,0},{5,1},{6,2},{7,3},{8,12},{9,13},{10,... | collective-permute-start | bytes 245768 | tf_op jit(solution)/shard_map/ppermute | solution.py:214
  10.1 3.0 %collective-permute-done.1 = bf16[2,16,1280]{2,1,0:T(8,128)(2,1)S(1)} collective-permute-done((bf16[2,16,1280]{2,1,0:T(8,128)(2,1)S(1)}, bf16[2,16,1280]{2,1,0:T(8,128)(2,1)S(1)}, u32[]{:S(2)}, u32[]{:S(2)}) %collective-permute-start.1) | collective-permute-done | bytes 81952 | tf_op jit(solution)/shard_map/ppermute | solution.py:214
  13.1 1.5 %collective-permute-start.3 = (bf16[256,512]{1,0:T(8,128)(2,1)}, bf16[256,512]{1,0:T(8,128)(2,1)S(1)}, u32[]{:S(2)}, u32[]{:S(2)}) collective-permute-start(bf16[256,512]{1,0:T(8,128)(2,1)} %refs_0_.3), channel_id=1, source_target_pairs={{0,4},{1,5},{2,6},{3,7},{4,0},{5,1},{6,2},{7,3},{8,12},{9,13},{10,... | collective-permute-start | bytes 786440 | tf_op jit(solution)/shard_map/ppermute | solution.py:214
  14.6 1.6 %collective-permute-start.2 = (bf16[4,16,1024]{2,1,0:T(8,128)(2,1)S(1)}, bf16[4,16,1024]{2,1,0:T(8,128)(2,1)S(1)}, u32[]{:S(2)}, u32[]{:S(2)}) collective-permute-start(bf16[4,16,1024]{2,1,0:T(8,128)(2,1)S(1)} %slice.48.refs_2_), channel_id=1, source_target_pairs={{0,2},{1,3},{2,0},{3,1},{4,6},{5,7},{6,4},{7,5},{8,10},{9,11},{10,... | collective-permute-start | bytes 393224 | tf_op jit(solution)/shard_map/ppermute | solution.py:214
  16.2 1.9 %slice.49 = bf16[512,512]{1,0:T(8,128)(2,1)} slice(bf16[1024,512]{1,0:T(8,128)(2,1)} %refs_2_.3), slice={[0:512], [0:512]} | slice | bytes 1048576 | tf_op jit(solution)/shard_map/slice | solution.py:223
  18.6 2.9 %collective-permute-start.5 = (bf16[256,512]{1,0:T(8,128)(2,1)}, bf16[256,512]{1,0:T(8,128)(2,1)S(1)}, u32[]{:S(2)}, u32[]{:S(2)}) collective-permute-start(bf16[256,512]{1,0:T(8,128)(2,1)} %refs_0_.3), channel_id=1, source_target_pairs={{0,8},{1,9},{2,10},{3,11},{4,12},{5,13},{6,14},{7,15},{8,0},{9,1},... | collective-permute-start | bytes 786440 | tf_op jit(solution)/shard_map/ppermute | solution.py:214
  21.5 1.9 %slice.50 = bf16[512,512]{1,0:T(8,128)(2,1)} slice(bf16[1024,512]{1,0:T(8,128)(2,1)} %refs_2_.3), slice={[512:1024], [0:512]} | slice | bytes 1048576 | tf_op jit(solution)/shard_map/slice | solution.py:237
  23.4 1.5 %collective-permute-start.11 = (bf16[512,512]{1,0:T(8,128)(2,1)}, bf16[512,512]{1,0:T(8,128)(2,1)S(1)}, u32[]{:S(2)}, u32[]{:S(2)}) collective-permute-start(bf16[512,512]{1,0:T(8,128)(2,1)} %slice.50), channel_id=1, source_target_pairs={{0,2},{1,3},{2,0},{3,1},{4,6},{5,7},{6,4},{7,5},{8,10},{9,11},{10,... | collective-permute-start | bytes 1572872 | tf_op jit(solution)/shard_map/ppermute | solution.py:214
  25.7 4.5 %alpha_step.3 = (f32[16,1024]{1,0:T(8,128)S(1)}, bf16[4,1024,1024]{2,1,0:T(8,128)(2,1)S(1)}) custom-call(s32[1]{0:T(128)} %bitcast.refs_0_, bf16[1024,16384]{1,0:T(8,128)(2,1)} %refs_1_.5, bf16[4,16,1024]{2,1,0:T(8,128)(2,1)S(1)} %slice.48.refs_2_), custom_call_target="tpu_custom_call" | custom-call | flops 1073741824 | bytes 8388608 | tf_op jit(solution)/shard_map/alpha_step/pallas_call | solution.py:65
  30.2 4.4 %alpha_step.4 = (f32[16,1024]{1,0:T(8,128)S(1)}, bf16[4,1024,1024]{2,1,0:T(8,128)(2,1)S(1)}) custom-call(s32[1]{0:T(128)} %bitcast.refs_0_, bf16[1024,16384]{1,0:T(8,128)(2,1)} %refs_1_.5, bf16[4,16,1024]{2,1,0:T(8,128)(2,1)S(1)} %collective-permute-done.2.refs_2_, f32[16,1024]{1,0:T(8,128)S(1)} %get-tuple-element.25.refs_3_), custom_call_target="tpu_custom_call" | custom-call | flops 1073741824 | bytes 8388608 | tf_op jit(solution)/shard_map/alpha_step/pallas_call | solution.py:65
  34.7 7.2 %alpha_step.5 = (bf16[16,1024]{1,0:T(8,128)(2,1)S(1)}, bf16[8,1024,1024]{2,1,0:T(8,128)(2,1)S(1)}) custom-call(s32[1]{0:T(128)} %bitcast.refs_0_, bf16[1024,16384]{1,0:T(8,128)(2,1)} %refs_1_.5, bf16[8,16,1024]{2,1,0:T(8,128)(2,1)S(1)} %collective-permute-done.4.refs_2_, f32[16,1024]{1,0:T(8,128)S(1)} %get-tuple-element.26.refs_3_), custom_call_target="tpu_custom_call" | custom-call | flops 2147483648 | bytes 16777216 | tf_op jit(solution)/shard_map/alpha_step/pallas_call | solution.py:65
  42.0 1.9 %collective-permute-done.11.refs_3_ = bf16[512,512]{1,0:T(8,128)(2,1)S(1)} collective-permute-done((bf16[512,512]{1,0:T(8,128)(2,1)}, bf16[512,512]{1,0:T(8,128)(2,1)S(1)}, u32[]{:S(2)}, u32[]{:S(2)}) %collective-permute-start.11) | collective-permute-done | bytes 524320 | tf_op jit(solution)/shard_map/ppermute | solution.py:214
  45.5 3.6 %collective-permute-done.7.refs_2_ = bf16[16,1024]{1,0:T(8,128)(2,1)S(1)} collective-permute-done((bf16[16,1024]{1,0:T(8,128)(2,1)S(1)}, bf16[16,1024]{1,0:T(8,128)(2,1)S(1)}, u32[]{:S(2)}, u32[]{:S(2)}) %collective-permute-start.7) | collective-permute-done | bytes 32800 | tf_op jit(solution)/shard_map/ppermute | solution.py:214
  57.6 3.3 %collective-permute-done.15 = f32[16,1024]{1,0:T(8,128)S(1)} collective-permute-done((f32[16,1024]{1,0:T(8,128)S(1)}, f32[16,1024]{1,0:T(8,128)S(1)}, u32[]{:S(2)}, u32[]{:S(2)}) %collective-permute-start.15) | collective-permute-done | bytes 65568 | tf_op jit(solution)/shard_map/ppermute | solution.py:214
  60.9 3.0 %collective-permute-start.16 = (f32[16,1024]{1,0:T(8,128)S(1)}, f32[16,1024]{1,0:T(8,128)S(1)}, u32[]{:S(2)}, u32[]{:S(2)}) collective-permute-start(f32[16,1024]{1,0:T(8,128)S(1)} %maximum_add_fusion.sum_ref), channel_id=1, source_target_pairs={{0,8},{1,9},{2,10},{3,11},{4,12},{5,13},{6,14},{7,15},{8,0},{9,1},... | collective-permute-start | bytes 196616 | tf_op jit(solution)/shard_map/ppermute | solution.py:214
  63.9 2.9 %collective-permute-done.16.received_ref = f32[16,1024]{1,0:T(8,128)S(1)} collective-permute-done((f32[16,1024]{1,0:T(8,128)S(1)}, f32[16,1024]{1,0:T(8,128)S(1)}, u32[]{:S(2)}, u32[]{:S(2)}) %collective-permute-start.16) | collective-permute-done | bytes 65568 | tf_op jit(solution)/shard_map/ppermute | solution.py:214
  66.9 2.3 %kernel_gradient.1 = (f32[2,16,1024]{2,1,0:T(8,128)S(1)}, f32[2,16,1024]{2,1,0:T(8,128)S(1)}, f32[16,256]{1,0:T(8,128)}) custom-call(f32[16,1024]{1,0:T(8,128)S(1)} %maximum_add_fusion.sum_ref, f32[16,1024]{1,0:T(8,128)S(1)} %collective-permute-done.16.received_ref, f32[16,128]{1,0:T(8,128)S(1)} %broadcast_in_dim.5.bias_ref, ...), custom_call_target="tpu_custom_call" | custom-call | flops 1073741824 | bytes 1024 | tf_op jit(solution)/shard_map/kernel_gradient/pallas_call | solution.py:194
  71.2 3.8 %collective-permute-done.18 = f32[16,1024]{1,0:T(8,128)S(1)} collective-permute-done((f32[16,1024]{1,0:T(8,128)S(1)}, f32[16,1024]{1,0:T(8,128)S(1)}, u32[]{:S(2)}, u32[]{:S(2)}) %collective-permute-start.18) | collective-permute-done | bytes 65568 | tf_op jit(solution)/shard_map/ppermute | solution.py:214
  80.9 6.5 %collective-permute-done.21 = f32[4,16,1024]{2,1,0:T(8,128)S(1)} collective-permute-done((f32[4,16,1024]{2,1,0:T(8,128)S(1)}, f32[4,16,1024]{2,1,0:T(8,128)S(1)}, u32[]{:S(2)}, u32[]{:S(2)}) %collective-permute-start.21) | collective-permute-done | bytes 262176 | tf_op jit(solution)/shard_map/ppermute | solution.py:214
  87.9 4.6 %collective-permute-done.22 = f32[2,16,1024]{2,1,0:T(8,128)S(1)} collective-permute-done((f32[2,16,1024]{2,1,0:T(8,128)S(1)}, f32[2,16,1024]{2,1,0:T(8,128)S(1)}, u32[]{:S(2)}, u32[]{:S(2)}) %collective-permute-start.22) | collective-permute-done | bytes 131104 | tf_op jit(solution)/shard_map/ppermute | solution.py:214
  92.5 2.4 %collective-permute-start.23 = (f32[1,16,1024]{2,1,0:T(8,128)S(1)}, f32[1,16,1024]{2,1,0:T(8,128)S(1)}, u32[]{:S(2)}, u32[]{:S(2)}) collective-permute-start(f32[1,16,1024]{2,1,0:T(8,128)S(1)} %slice.69), channel_id=1, source_target_pairs={{0,8},{1,9},{2,10},{3,11},{4,12},{5,13},{6,14},{7,15},{8,0},{9,1},... | collective-permute-start | bytes 196616 | tf_op jit(solution)/shard_map/ppermute | solution.py:214
  94.9 3.5 %collective-permute-done.23 = f32[1,16,1024]{2,1,0:T(8,128)S(1)} collective-permute-done((f32[1,16,1024]{2,1,0:T(8,128)S(1)}, f32[1,16,1024]{2,1,0:T(8,128)S(1)}, u32[]{:S(2)}, u32[]{:S(2)}) %collective-permute-start.23) | collective-permute-done | bytes 65568 | tf_op jit(solution)/shard_map/ppermute | solution.py:214
  (63 shorter events, 21.8 us)
Async XLA Ops:
  2.1 6.5 %collective-permute-start = (bf16[1,16,1280]{2,1,0:T(8,128)(2,1)S(1)}, bf16[1,16,1280]{2,1,0:T(8,128)(2,1)S(1)}, u32[]{:S(2)}, u32[]{:S(2)}) collective-permute-start(bf16[1,16,1280]{2,1,0:T(8,128)(2,1)S(1)} %maximum_bitcast_fusion), channel_id=1, source_target_pairs={{0,8},{1,9},{2,10},{3,11},{4,12},{5,13},{6,14},{7,15},{8,0},{9,1},... | collective-permute-start | bytes 122888 | tf_op jit(solution)/shard_map/ppermute | solution.py:214
  8.5 4.5 %collective-permute-start.1 = (bf16[2,16,1280]{2,1,0:T(8,128)(2,1)S(1)}, bf16[2,16,1280]{2,1,0:T(8,128)(2,1)S(1)}, u32[]{:S(2)}, u32[]{:S(2)}) collective-permute-start(bf16[2,16,1280]{2,1,0:T(8,128)(2,1)S(1)} %pad_maximum_fusion.2), channel_id=1, source_target_pairs={{0,4},{1,5},{2,6},{3,7},{4,0},{5,1},{6,2},{7,3},{8,12},{9,13},{10,... | collective-permute-start | bytes 245768 | tf_op jit(solution)/shard_map/ppermute | solution.py:214
  13.1 8.5 %collective-permute-start.3 = (bf16[256,512]{1,0:T(8,128)(2,1)}, bf16[256,512]{1,0:T(8,128)(2,1)S(1)}, u32[]{:S(2)}, u32[]{:S(2)}) collective-permute-start(bf16[256,512]{1,0:T(8,128)(2,1)} %refs_0_.3), channel_id=1, source_target_pairs={{0,4},{1,5},{2,6},{3,7},{4,0},{5,1},{6,2},{7,3},{8,12},{9,13},{10,... | collective-permute-start | bytes 786440 | tf_op jit(solution)/shard_map/ppermute | solution.py:214
  14.6 6.9 %collective-permute-start.2 = (bf16[4,16,1024]{2,1,0:T(8,128)(2,1)S(1)}, bf16[4,16,1024]{2,1,0:T(8,128)(2,1)S(1)}, u32[]{:S(2)}, u32[]{:S(2)}) collective-permute-start(bf16[4,16,1024]{2,1,0:T(8,128)(2,1)S(1)} %slice.48.refs_2_), channel_id=1, source_target_pairs={{0,2},{1,3},{2,0},{3,1},{4,6},{5,7},{6,4},{7,5},{8,10},{9,11},{10,... | collective-permute-start | bytes 393224 | tf_op jit(solution)/shard_map/ppermute | solution.py:214
  16.2 32.9 %collective-permute-start.9 = (bf16[1024,512]{1,0:T(8,128)(2,1)}, bf16[1024,512]{1,0:T(8,128)(2,1)S(1)}, u32[]{:S(2)}, u32[]{:S(2)}) collective-permute-start(bf16[1024,512]{1,0:T(8,128)(2,1)} %refs_2_.3), channel_id=1, source_target_pairs={{0,1},{1,0},{2,3},{3,2},{4,5},{5,4},{6,7},{7,6},{8,9},{9,8},{10,11... | collective-permute-start | bytes 3145736 | tf_op jit(solution)/shard_map/ppermute | solution.py:214
  18.1 23.9 %collective-permute-start.10 = (bf16[512,512]{1,0:T(8,128)(2,1)}, bf16[512,512]{1,0:T(8,128)(2,1)S(1)}, u32[]{:S(2)}, u32[]{:S(2)}) collective-permute-start(bf16[512,512]{1,0:T(8,128)(2,1)} %slice.49), channel_id=1, source_target_pairs={{0,2},{1,3},{2,0},{3,1},{4,6},{5,7},{6,4},{7,5},{8,10},{9,11},{10,... | collective-permute-start | bytes 1572872 | tf_op jit(solution)/shard_map/ppermute | solution.py:214
  18.6 16.0 %collective-permute-start.5 = (bf16[256,512]{1,0:T(8,128)(2,1)}, bf16[256,512]{1,0:T(8,128)(2,1)S(1)}, u32[]{:S(2)}, u32[]{:S(2)}) collective-permute-start(bf16[256,512]{1,0:T(8,128)(2,1)} %refs_0_.3), channel_id=1, source_target_pairs={{0,8},{1,9},{2,10},{3,11},{4,12},{5,13},{6,14},{7,15},{8,0},{9,1},... | collective-permute-start | bytes 786440 | tf_op jit(solution)/shard_map/ppermute | solution.py:214
  23.4 20.5 %collective-permute-start.11 = (bf16[512,512]{1,0:T(8,128)(2,1)}, bf16[512,512]{1,0:T(8,128)(2,1)S(1)}, u32[]{:S(2)}, u32[]{:S(2)}) collective-permute-start(bf16[512,512]{1,0:T(8,128)(2,1)} %slice.50), channel_id=1, source_target_pairs={{0,2},{1,3},{2,0},{3,1},{4,6},{5,7},{6,4},{7,5},{8,10},{9,11},{10,... | collective-permute-start | bytes 1572872 | tf_op jit(solution)/shard_map/ppermute | solution.py:214
  25.7 9.0 %collective-permute-start.4 = (bf16[8,16,1024]{2,1,0:T(8,128)(2,1)}, bf16[8,16,1024]{2,1,0:T(8,128)(2,1)S(1)}, u32[]{:S(2)}, u32[]{:S(2)}) collective-permute-start(bf16[8,16,1024]{2,1,0:T(8,128)(2,1)} %pad_maximum_fusion), channel_id=1, source_target_pairs={{0,1},{1,0},{2,3},{3,2},{4,5},{5,4},{6,7},{7,6},{8,9},{9,8},{10,11... | collective-permute-start | bytes 786440 | tf_op jit(solution)/shard_map/ppermute | solution.py:214
  43.9 7.0 %collective-permute-start.12 = (bf16[512,512]{1,0:T(8,128)(2,1)S(1)}, bf16[512,512]{1,0:T(8,128)(2,1)S(1)}, u32[]{:S(2)}, u32[]{:S(2)}) collective-permute-start(bf16[512,512]{1,0:T(8,128)(2,1)S(1)} %collective-permute-done.10.refs_2_), channel_id=1, source_target_pairs={{0,1},{1,0},{2,3},{3,2},{4,5},{5,4},{6,7},{7,6},{8,9},{9,8},{10,11... | collective-permute-start | bytes 1572872 | tf_op jit(solution)/shard_map/ppermute | solution.py:214
  43.9 7.0 %collective-permute-start.13 = (bf16[512,512]{1,0:T(8,128)(2,1)S(1)}, bf16[512,512]{1,0:T(8,128)(2,1)S(1)}, u32[]{:S(2)}, u32[]{:S(2)}) collective-permute-start(bf16[512,512]{1,0:T(8,128)(2,1)S(1)} %collective-permute-done.11.refs_3_), channel_id=1, source_target_pairs={{0,1},{1,0},{2,3},{3,2},{4,5},{5,4},{6,7},{7,6},{8,9},{9,8},{10,11... | collective-permute-start | bytes 1572872 | tf_op jit(solution)/shard_map/ppermute | solution.py:214
  44.4 8.2 %collective-permute-start.14 = (bf16[256,512]{1,0:T(8,128)(2,1)S(1)}, bf16[256,512]{1,0:T(8,128)(2,1)S(1)}, u32[]{:S(2)}, u32[]{:S(2)}) collective-permute-start(bf16[256,512]{1,0:T(8,128)(2,1)S(1)} %collective-permute-done.5.refs_0_), channel_id=1, source_target_pairs={{0,4},{1,5},{2,6},{3,7},{4,0},{5,1},{6,2},{7,3},{8,12},{9,13},{10,... | collective-permute-start | bytes 786440 | tf_op jit(solution)/shard_map/ppermute | solution.py:214
  45.2 3.9 %collective-permute-start.7 = (bf16[16,1024]{1,0:T(8,128)(2,1)S(1)}, bf16[16,1024]{1,0:T(8,128)(2,1)S(1)}, u32[]{:S(2)}, u32[]{:S(2)}) collective-permute-start(bf16[16,1024]{1,0:T(8,128)(2,1)S(1)} %get-tuple-element.30.refs_4_.refs_0_), channel_id=1, source_target_pairs={{0,2},{1,3},{2,0},{3,1},{4,6},{5,7},{6,4},{7,5},{8,10},{9,11},{10,... | collective-permute-start | bytes 98312 | tf_op jit(solution)/shard_map/ppermute | solution.py:214
  49.1 6.2 %collective-permute-start.6 = (bf16[16,1024]{1,0:T(8,128)(2,1)S(1)}, bf16[16,1024]{1,0:T(8,128)(2,1)S(1)}, u32[]{:S(2)}, u32[]{:S(2)}) collective-permute-start(bf16[16,1024]{1,0:T(8,128)(2,1)S(1)} %get-tuple-element.30.refs_4_.refs_0_), channel_id=1, source_target_pairs={{0,1},{1,0},{2,3},{3,2},{4,5},{5,4},{6,7},{7,6},{8,9},{9,8},{10,11... | collective-permute-start | bytes 98312 | tf_op jit(solution)/shard_map/ppermute | solution.py:214
  49.1 6.2 %collective-permute-start.8 = (bf16[16,1024]{1,0:T(8,128)(2,1)S(1)}, bf16[16,1024]{1,0:T(8,128)(2,1)S(1)}, u32[]{:S(2)}, u32[]{:S(2)}) collective-permute-start(bf16[16,1024]{1,0:T(8,128)(2,1)S(1)} %collective-permute-done.7.refs_2_), channel_id=1, source_target_pairs={{0,1},{1,0},{2,3},{3,2},{4,5},{5,4},{6,7},{7,6},{8,9},{9,8},{10,11... | collective-permute-start | bytes 98312 | tf_op jit(solution)/shard_map/ppermute | solution.py:214
  56.6 4.3 %collective-permute-start.15 = (f32[16,1024]{1,0:T(8,128)S(1)}, f32[16,1024]{1,0:T(8,128)S(1)}, u32[]{:S(2)}, u32[]{:S(2)}) collective-permute-start(f32[16,1024]{1,0:T(8,128)S(1)} %partial_logits.1), channel_id=1, source_target_pairs={{0,4},{1,5},{2,6},{3,7},{4,0},{5,1},{6,2},{7,3},{8,12},{9,13},{10,... | collective-permute-start | bytes 196616 | tf_op jit(solution)/shard_map/ppermute | solution.py:214
  60.9 5.9 %collective-permute-start.16 = (f32[16,1024]{1,0:T(8,128)S(1)}, f32[16,1024]{1,0:T(8,128)S(1)}, u32[]{:S(2)}, u32[]{:S(2)}) collective-permute-start(f32[16,1024]{1,0:T(8,128)S(1)} %maximum_add_fusion.sum_ref), channel_id=1, source_target_pairs={{0,8},{1,9},{2,10},{3,11},{4,12},{5,13},{6,14},{7,15},{8,0},{9,1},... | collective-permute-start | bytes 196616 | tf_op jit(solution)/shard_map/ppermute | solution.py:214
  69.2 1.4 %collective-permute-start.17 = (f32[2,16,1024]{2,1,0:T(8,128)S(1)}, f32[2,16,1024]{2,1,0:T(8,128)S(1)}, u32[]{:S(2)}, u32[]{:S(2)}) collective-permute-start(f32[2,16,1024]{2,1,0:T(8,128)S(1)} %get-tuple-element.35), channel_id=1, source_target_pairs={{0,1},{1,0},{2,3},{3,2},{4,5},{5,4},{6,7},{7,6},{8,9},{9,8},{10,11... | collective-permute-start | bytes 393224 | tf_op jit(solution)/shard_map/ppermute | solution.py:214
  70.6 4.3 %collective-permute-start.18 = (f32[16,1024]{1,0:T(8,128)S(1)}, f32[16,1024]{1,0:T(8,128)S(1)}, u32[]{:S(2)}, u32[]{:S(2)}) collective-permute-start(f32[16,1024]{1,0:T(8,128)S(1)} %fusion.1), channel_id=1, source_target_pairs={{0,2},{1,3},{2,0},{3,1},{4,6},{5,7},{6,4},{7,5},{8,10},{9,11},{10,... | collective-permute-start | bytes 196616 | tf_op jit(solution)/shard_map/ppermute | solution.py:214
  76.1 2.9 %collective-permute-start.20 = (f32[4,16,1024]{2,1,0:T(8,128)S(1)}, f32[4,16,1024]{2,1,0:T(8,128)S(1)}, u32[]{:S(2)}, u32[]{:S(2)}) collective-permute-start(f32[4,16,1024]{2,1,0:T(8,128)S(1)} %gradient_terms.7), channel_id=1, source_target_pairs={{0,1},{1,0},{2,3},{3,2},{4,5},{5,4},{6,7},{7,6},{8,9},{9,8},{10,11... | collective-permute-start | bytes 786440 | tf_op jit(solution)/shard_map/ppermute | solution.py:214
  77.4 3.5 %collective-permute-start.19 = (f32[4,16,1024]{2,1,0:T(8,128)S(1)}, f32[4,16,1024]{2,1,0:T(8,128)S(1)}, u32[]{:S(2)}, u32[]{:S(2)}) collective-permute-start(f32[4,16,1024]{2,1,0:T(8,128)S(1)} %gradient_terms.5), channel_id=1, source_target_pairs={{0,1},{1,0},{2,3},{3,2},{4,5},{5,4},{6,7},{7,6},{8,9},{9,8},{10,11... | collective-permute-start | bytes 786440 | tf_op jit(solution)/shard_map/ppermute | solution.py:214
  79.1 8.3 %collective-permute-start.21 = (f32[4,16,1024]{2,1,0:T(8,128)S(1)}, f32[4,16,1024]{2,1,0:T(8,128)S(1)}, u32[]{:S(2)}, u32[]{:S(2)}) collective-permute-start(f32[4,16,1024]{2,1,0:T(8,128)S(1)} %add.40), channel_id=1, source_target_pairs={{0,2},{1,3},{2,0},{3,1},{4,6},{5,7},{6,4},{7,5},{8,10},{9,11},{10,... | collective-permute-start | bytes 786440 | tf_op jit(solution)/shard_map/ppermute | solution.py:214
  87.5 5.0 %collective-permute-start.22 = (f32[2,16,1024]{2,1,0:T(8,128)S(1)}, f32[2,16,1024]{2,1,0:T(8,128)S(1)}, u32[]{:S(2)}, u32[]{:S(2)}) collective-permute-start(f32[2,16,1024]{2,1,0:T(8,128)S(1)} %stack.9), channel_id=1, source_target_pairs={{0,4},{1,5},{2,6},{3,7},{4,0},{5,1},{6,2},{7,3},{8,12},{9,13},{10,... | collective-permute-start | bytes 393224 | tf_op jit(solution)/shard_map/ppermute | solution.py:214
  92.5 5.9 %collective-permute-start.23 = (f32[1,16,1024]{2,1,0:T(8,128)S(1)}, f32[1,16,1024]{2,1,0:T(8,128)S(1)}, u32[]{:S(2)}, u32[]{:S(2)}) collective-permute-start(f32[1,16,1024]{2,1,0:T(8,128)S(1)} %slice.69), channel_id=1, source_target_pairs={{0,8},{1,9},{2,10},{3,11},{4,12},{5,13},{6,14},{7,15},{8,0},{9,1},... | collective-permute-start | bytes 196616 | tf_op jit(solution)/shard_map/ppermute | solution.py:214
  (3 other events, 42.8 us)

commit v2 on v1

v2 whole, which is shorter than its diff:
```python
import math

import jax
import jax.numpy as jnp
from jax import lax
from jax.experimental import pallas as pl
from jax.experimental.pallas import tpu as pltpu
from jax.sharding import PartitionSpec as P

BF16 = jnp.bfloat16
F32 = jnp.float32
ROWS_BY_ROWS = (((1,), (1,)), ((), ()))
MIB = 1 << 20
IN_FLIGHT = 3


def params(mib):
    return pltpu.CompilerParams(vmem_limit_bytes=mib * MIB)


def in_vmem():
    return pl.BlockSpec(memory_space=pltpu.VMEM)


def anywhere():
    return pl.BlockSpec(memory_space=pl.ANY)


def in_smem():
    return pl.BlockSpec(memory_space=pltpu.SMEM)


def cost(flops, bytes_accessed):
    return pl.CostEstimate(flops=int(flops), bytes_accessed=int(bytes_accessed), transcendentals=0)


def alpha_sum(me, tri, brought, known, total, after):
    offsets, betas = brought
    rows = tri.shape[0]
    classes, width = betas.shape[1:]
    count = len(offsets)
    ahead = min(IN_FLIGHT, count)
    last = total is not None

    def body(me_ref, tri_ref, after_ref, beta_ref, *refs):
        known_refs, (out_ref, held_ref, sems) = refs[:-3], refs[-3:]
        copies = [
            pltpu.make_async_copy(
                tri_ref.at[:, pl.ds(pl.multiple_of((me_ref[0] ^ offset) * width, width), width)],
                held_ref.at[at],
                sems.at[at],
            )
            for at, offset in enumerate(offsets)
        ]
        for copy in copies[:ahead]:
            copy.start()
        acc = None
        if last:
            total_ref, block_ref, known_beta_ref = known_refs
            acc = total_ref[...]
            for at in range(known_beta_ref.shape[0]):
                acc = acc + lax.dot_general(
                    known_beta_ref[at], block_ref[known[1] + at], ROWS_BY_ROWS, preferred_element_type=F32
                )
        for at in range(count):
            copies[at].wait()
            if at + ahead < count:
                copies[at + ahead].start()
            if at < betas.shape[0]:
                term = lax.dot_general(beta_ref[at], held_ref[at], ROWS_BY_ROWS, preferred_element_type=F32)
                acc = term if acc is None else acc + term
        out_ref[...] = acc.astype(out_ref.dtype)

    operands = (me, tri, after, betas)
    if last:
        operands += (total, pltpu.with_memory_space_constraint(known[0], pltpu.VMEM), known[2])
    return pl.pallas_call(
        body,
        out_shape=[
            jax.ShapeDtypeStruct((classes, rows), BF16 if last else F32),
            pltpu.VMEM((count, rows, width), BF16),
        ],
        in_specs=[in_smem(), anywhere(), anywhere()] + [in_vmem()] * (len(operands) - 3),
        out_specs=[in_vmem(), in_vmem()],
        scratch_shapes=[pltpu.SemaphoreType.DMA((count,))],
        compiler_params=params(8),
        cost_estimate=cost(2 * rows * count * width * 128, 2 * rows * count * width),
        name="alpha_sum",
    )(*operands)


def gradient_terms(grad, blocks, first, count):
    classes, rows = grad.shape
    width = blocks.shape[2]

    def body(grad_ref, block_ref, out_ref):
        for at in range(count):
            out_ref[at] = jnp.dot(grad_ref[...], block_ref[first + at], preferred_element_type=F32)

    return pl.pallas_call(
        body,
        out_shape=jax.ShapeDtypeStruct((count, classes, width), F32),
        in_specs=[in_vmem(), in_vmem()],
        out_specs=in_vmem(),
        compiler_params=params(8),
        cost_estimate=cost(2 * rows * count * width * 128, 1024),
        name="gradient_terms",
    )(grad, pltpu.with_memory_space_constraint(blocks, pltpu.VMEM))


def kernel_tile(block, points, centre_blocks, after):
    count, _, features = points.shape
    local = sum(piece.shape[0] for piece in centre_blocks[0])
    factor = 1.0 / math.sqrt(features)
    pieces = [piece for pieces in centre_blocks for piece in pieces]
    total = count * block

    def body(point_ref, *refs):
        piece_refs, out_ref = refs[:-2], refs[-1]
        row = 0
        for piece_ref in piece_refs:
            which, first, rows = row // local, row % local, piece_ref.shape[0]
            for at in range(count):
                inner = lax.dot_general(
                    piece_ref[...], point_ref[at, :block], ROWS_BY_ROWS, preferred_element_type=F32
                )
                value = inner * factor + 1.0
                out_ref[which, first : first + rows, at * block : (at + 1) * block] = (
                    value * value * value
                ).astype(BF16)
            row += rows

    return pl.pallas_call(
        body,
        out_shape=pltpu.VMEM((len(centre_blocks), local, total), BF16),
        in_specs=[in_vmem()] * (1 + len(pieces)) + [anywhere()],
        out_specs=in_vmem(),
        compiler_params=params(8),
        cost_estimate=cost(2 * total * len(centre_blocks) * local * features, 1024),
        name="kernel_tile",
    )(points, *pieces, after)


def partial_logits(tiles, alphas):
    classes = alphas[0].shape[0]
    sizes = [row[0].shape[2] for row in tiles]
    flat = [tile for row in tiles for tile in row]
    counts = [tile.shape[0] for tile in tiles[0]]

    def body(*refs):
        alpha_refs, tile_refs, out_ref = refs[: len(alphas)], refs[len(alphas) : -1], refs[-1]
        for part, size in enumerate(sizes):
            first = sum(sizes[:part])
            acc = None
            index = 0
            for which, count in enumerate(counts):
                tile_ref = tile_refs[part * len(counts) + which]
                for at in range(count):
                    term = jnp.dot(alpha_refs[index][...], tile_ref[at], preferred_element_type=F32)
                    acc = term if acc is None else acc + term
                    index += 1
            out_ref[:, first : first + size] = acc

    return pl.pallas_call(
        body,
        out_shape=jax.ShapeDtypeStruct((classes, sum(sizes)), F32),
        in_specs=[in_vmem()] * (len(alphas) + len(flat)),
        out_specs=in_vmem(),
        compiler_params=params(8),
        cost_estimate=cost(2 * sum(tile.size for tile in flat) * 128, 1024),
        name="partial_logits",
    )(*alphas, *flat)


def kernel_gradient(logit_sum, received, order, bias, points, tiles):
    flat = [tile for row in tiles for tile in row]
    n_parts = len(tiles[0])
    local = flat[0].shape[1]
    sizes = [row[0].shape[2] for row in tiles]
    classes, total = logit_sum.shape
    block = total // len(order)

    def body(sum_ref, received_ref, bias_ref, *refs):
        point_refs, tile_refs = refs[: len(points)], refs[len(points) : len(points) + len(flat)]
        *out_refs, logits_ref, resid_ref = refs[len(points) + len(flat) :]
        for at, source in enumerate(order):
            here = slice(at * block, (at + 1) * block)
            there = slice(source * block, (source + 1) * block)
            logits = sum_ref[:, here] + received_ref[:, there] + bias_ref[:, :1]
            if at == 0:
                logits_ref[...] = logits
            held = point_refs[at // points[0].shape[0]]
            onehot = held[at % points[0].shape[0], block : block + classes, :block].astype(F32)
            resid_ref[:, here] = (jax.nn.sigmoid(logits) - onehot).astype(BF16)
        for parity, out_ref in enumerate(out_refs):
            for which in range(n_parts):
                acc = None
                for part, size in enumerate(sizes):
                    first = sum(sizes[:part])
                    term = lax.dot_general(
                        resid_ref[:, first : first + size],
                        tile_refs[part * n_parts + which][parity],
                        ROWS_BY_ROWS,
                        preferred_element_type=F32,
                    )
                    acc = term if acc is None else acc + term
                out_ref[which] = acc

    return pl.pallas_call(
        body,
        out_shape=[jax.ShapeDtypeStruct((n_parts, classes, local), F32)] * 2
        + [jax.ShapeDtypeStruct((classes, block), F32)],
        in_specs=[in_vmem()] * (3 + len(points) + len(flat)),
        out_specs=[in_vmem()] * 3,
        scratch_shapes=[pltpu.VMEM((classes, total), BF16)],
        compiler_params=params(8),
        cost_estimate=cost(2 * sum(tile.size for tile in flat) * 128, 1024),
        name="kernel_gradient",
    )(logit_sum, received, bias, *points, *flat)


def on_device(points, labels, centres, tri_inverse, beta, bias):
    devices = lax.axis_size("pts")
    local_centres, classes = beta.shape
    total_points = points.shape[0] * devices
    outer = [1 << bit for bit in range(2, devices.bit_length() - 1)]

    def swap(array, mask):
        return lax.ppermute(array, "pts", [(index, index ^ mask) for index in range(devices)])

    tri_inverse = pltpu.with_memory_space_constraint(tri_inverse, pltpu.HBM)
    me = lax.axis_index("pts").astype(jnp.int32).reshape(1)
    bias_column = jnp.broadcast_to(bias[:, None], (classes, 128))
    class_column = jnp.arange(classes, dtype=jnp.int32)[:, None]
    onehot = (labels[None, :] == class_column).astype(BF16)

    block, features = points.shape
    points = jnp.concatenate([points, jnp.pad(onehot, ((0, 0), (0, features - block)))])[None]
    half = local_centres // 2
    centre_halves = [centres[:half], centres[half:]]
    centres_2 = [swap(centre_halves[0], 2)]
    coeffs = beta.T[None]
    far = [0]
    for mask in reversed(outer):
        coeffs = jnp.concatenate([coeffs, swap(coeffs, mask)])
        far = far + [offset ^ mask for offset in far]
        if mask != outer[0]:
            points, coeffs = lax.optimization_barrier((points, coeffs))
            points = jnp.concatenate([points, swap(points, mask)])
    count = len(far)
    coeffs_2 = swap(coeffs, 2)
    near_2 = [offset ^ 2 for offset in far]
    near_13 = [offset ^ 1 for offset in far + near_2]
    alpha, tri_02 = alpha_sum(me, tri_inverse, (far + near_2, coeffs), None, None, coeffs)
    later, coeffs_2, alpha, centres_2[0] = lax.optimization_barrier((centre_halves[1], coeffs_2, alpha, centres_2[0]))
    centres_2.append(swap(later, 2))
    coeffs_13 = swap(jnp.concatenate([coeffs, coeffs_2]), 1)
    alpha, tri_13 = alpha_sum(me, tri_inverse, (near_13, coeffs_13), (tri_02, count, coeffs_2), alpha, points)
    points = [points, swap(points, outer[0])]

    alpha_2 = swap(alpha, 2)
    near_centres = [[centres], [swap(centres, 1)]]
    tile_00 = kernel_tile(block, points[0], near_centres, alpha)
    alpha_2, tile_00, points[1] = lax.optimization_barrier((alpha_2, tile_00, points[1]))
    alpha_1 = swap(alpha, 1)
    alpha_3 = swap(alpha_2, 1)
    *centres_2, alpha = lax.optimization_barrier((*centres_2, alpha))
    far_centres = [centres_2, [swap(piece, 1) for piece in centres_2]]
    tile_01 = kernel_tile(block, points[0], far_centres, tile_00)
    tile_10 = kernel_tile(block, points[1], near_centres, tile_01)
    tile_11 = kernel_tile(block, points[1], far_centres, tile_10)
    tiles = [[tile_00, tile_01], [tile_10, tile_11]]
    logit_sum = partial_logits(tiles, (alpha, alpha_1, alpha_2, alpha_3))

    for mask in outer:
        received = swap(logit_sum, mask)
        order = [far.index(offset ^ mask) for offset in far]
        if mask != outer[-1]:
            moved = [received[:, source * block : (source + 1) * block] for source in order]
            logit_sum = logit_sum + jnp.concatenate(moved, axis=1)
    keep, send, logits = kernel_gradient(logit_sum, received, order, bias_column, points, tiles)

    received = swap(send, 1)
    received_2 = swap(keep[1] + received[1], 2)
    grad = ((keep[0] + received[0] + received_2) * (1.0 / math.sqrt(total_points))).astype(BF16)

    term_3 = gradient_terms(grad, tri_13, count, count)
    received_3 = swap(term_3, 1)
    term_2 = gradient_terms(grad, tri_02, count, count)
    received_2 = swap(term_2 + received_3, 2)
    term_1 = gradient_terms(grad, tri_13, 0, count)
    received_1 = swap(term_1, 1)
    term_0 = gradient_terms(grad, tri_02, 0, count)
    total = term_0 + received_1 + received_2
    gradient = total[0]
    for at, offset in enumerate(far[1:], 1):
        gradient = gradient + swap(total[at], offset)
    return (gradient.T, logits.T)


def solution(mesh):
    return jax.shard_map(
        on_device,
        mesh=mesh,
        in_specs=(
            P(("groups", "pts"), None),
            P(("groups", "pts")),
            P(("groups", "pts"), None),
            P(("groups", "pts"), None),
            P(("groups", "pts"), None),
            P("groups"),
        ),
        out_specs=(P(("groups", "pts"), None), P(("groups", "pts"), None)),
        check_vma=False,
    )
```

time: 99.4 us -> 86.6 us (0.87)
  waiting for transfers between devices: 37.4 us -> 29 us
  local copies, waits for them, and re-layouts: 3.9 us -> 1.43 us
  other arithmetic: 2.97 us -> 0.83 us
  starting transfers between devices: 24.1 us -> 26.1 us
  Pallas kernels: 29.9 us -> 28.2 us
    ppermute x24, waiting for transfers between devices: 37.4 us -> 29 us  [swap(): lax.ppermute(array, 'pts', [(index, index ^ mask) for index in range(devi...]
    slice x5 -> x1, local copies, waits for them, and re-layouts: 3.8 us -> 1.27 us  [on_device(): centre_halves = [centres[:half], centres[half:]]]
    ppermute x24, starting transfers between devices: 24.1 us -> 26.1 us  [swap(): lax.ppermute(array, 'pts', [(index, index ^ mask) for index in range(devi...]
    pallas_call x3 -> x2, Pallas kernels: 16.2 us -> 14.5 us  [alpha_sum(): pl.pallas_call(body, out_shape=[jax.ShapeDtypeStruct((classes, rows), BF1...]
  transfers between devices with their start and end apart: 24 -> 24, of which waited for: 12 -> 11; matrix products, arithmetic and copies ran while one was open for 5% -> 2% of each run, Pallas kernels for 25% -> 27%
where the time goes in v2:
time: 86.6 us; the launch traced here: 86.4 us
  waiting for transfers between devices  29 us (33%)
  Pallas kernels  28.2 us (33%)
  starting transfers between devices  26.1 us (30%)
  local copies, waits for them, and re-layouts  1.43 us (2%)
  between operations  0.89 us (1%)
    ppermute x24, waiting for transfers between devices, swap(): lax.ppermute(array, 'pts', [(index, index ^ mask) for index in range(devi...  29 us
    ppermute x24, starting transfers between devices, swap(): lax.ppermute(array, 'pts', [(index, index ^ mask) for index in range(devi...  26.1 us
    pallas_call x2, Pallas kernels, alpha_sum(): pl.pallas_call(body, out_shape=[jax.ShapeDtypeStruct((classes, rows), BF1...  14.5 us
    pallas_call x4, Pallas kernels, kernel_tile(): pl.pallas_call(body, out_shape=pltpu.VMEM((len(centre_blocks), local, tot...  5.26 us
    pallas_call x4, Pallas kernels, gradient_terms(): pl.pallas_call(body, out_shape=jax.ShapeDtypeStruct((count, classes, widt...  4.79 us
    pallas_call x1, Pallas kernels, kernel_gradient(): pl.pallas_call(body, out_shape=[jax.ShapeDtypeStruct((n_parts, classes, l...  2.29 us
  transfers between devices with their start and end apart: 24, of which 11 were waited for; matrix products, arithmetic and copies ran while one was open for 2% of the time, Pallas kernels for 27%

profile of v2, /device:TPU:0, one launch (start us, length us, event | category | flops | bytes accessed | tf_op | source)
XLA Modules:
  0.0 86.4 jit_solution(17298809951484661055)
XLA Ops:
  0.7 4.1 %collective-permute-start = (bf16[1,16,1024]{2,1,0:T(8,128)(2,1)}, bf16[1,16,1024]{2,1,0:T(8,128)(2,1)S(1)}, u32[]{:S(2)}, u32[]{:S(2)}) collective-permute-start(bf16[1,16,1024]{2,1,0:T(8,128)(2,1)} %bitcast.35), channel_id=1, source_target_pairs={{0,8},{1,9},{2,10},{3,11},{4,12},{5,13},{6,14},{7,15},{8,0},{9,1},... | collective-permute-start | bytes 98312 | tf_op jit(solution)/shard_map/ppermute | solution.py:229
  6.0 1.6 %collective-permute-start.3 = (bf16[512,512]{1,0:T(8,128)(2,1)S(1)}, bf16[512,512]{1,0:T(8,128)(2,1)S(1)}, u32[]{:S(2)}, u32[]{:S(2)}) collective-permute-start(bf16[512,512]{1,0:T(8,128)(2,1)S(1)} %get-tuple-element.40), channel_id=1, source_target_pairs={{0,2},{1,3},{2,0},{3,1},{4,6},{5,7},{6,4},{7,5},{8,10},{9,11},{10,... | collective-permute-start | bytes 1572872 | tf_op jit(solution)/shard_map/ppermute | solution.py:229
  7.7 1.6 %collective-permute-start.1 = (bf16[2,16,1024]{2,1,0:T(8,128)(2,1)S(1)}, bf16[2,16,1024]{2,1,0:T(8,128)(2,1)S(1)}, u32[]{:S(2)}, u32[]{:S(2)}) collective-permute-start(bf16[2,16,1024]{2,1,0:T(8,128)(2,1)S(1)} %pad_maximum_fusion.1), channel_id=1, source_target_pairs={{0,4},{1,5},{2,6},{3,7},{4,0},{5,1},{6,2},{7,3},{8,12},{9,13},{10,... | collective-permute-start | bytes 196616 | tf_op jit(solution)/shard_map/ppermute | solution.py:229
  9.4 2.3 %collective-permute-start.5 = (bf16[1,272,512]{2,1,0:T(8,128)(2,1)S(1)}, bf16[1,272,512]{2,1,0:T(8,128)(2,1)S(1)}, u32[]{:S(2)}, u32[]{:S(2)}) collective-permute-start(bf16[1,272,512]{2,1,0:T(8,128)(2,1)S(1)} %maximum_bitcast_fusion), channel_id=1, source_target_pairs={{0,8},{1,9},{2,10},{3,11},{4,12},{5,13},{6,14},{7,15},{8,0},{9,1},... | collective-permute-start | bytes 835592 | tf_op jit(solution)/shard_map/ppermute | solution.py:229
  13.3 6.5 %alpha_sum.2 = (f32[16,1024]{1,0:T(8,128)S(1)}, bf16[8,1024,1024]{2,1,0:T(8,128)(2,1)S(1)}) custom-call(s32[1]{0:T(128)} %bitcast.4.me_ref, bf16[1024,16384]{1,0:T(8,128)(2,1)} %tri_ref.3, bf16[4,16,1024]{2,1,0:T(8,128)(2,1)S(1)} %constant_dynamic-update-slice_fusion.after_ref.beta_ref, ...), custom_call_target="tpu_custom_call" | custom-call | flops 2147483648 | bytes 16777216 | tf_op jit(solution)/shard_map/alpha_sum/pallas_call | solution.py:77
  19.8 3.5 %collective-permute-done.2.refs_2_ = bf16[4,16,1024]{2,1,0:T(8,128)(2,1)S(1)} collective-permute-done((bf16[4,16,1024]{2,1,0:T(8,128)(2,1)S(1)}, bf16[4,16,1024]{2,1,0:T(8,128)(2,1)S(1)}, u32[]{:S(2)}, u32[]{:S(2)}) %collective-permute-start.2) | collective-permute-done | bytes 131104 | tf_op jit(solution)/shard_map/ppermute | solution.py:229
  23.2 1.5 %collective-permute-start.4 = (bf16[512,512]{1,0:T(8,128)(2,1)S(1)}, bf16[512,512]{1,0:T(8,128)(2,1)S(1)}, u32[]{:S(2)}, u32[]{:S(2)}) collective-permute-start(bf16[512,512]{1,0:T(8,128)(2,1)S(1)} %get-tuple-element.24), channel_id=1, source_target_pairs={{0,2},{1,3},{2,0},{3,1},{4,6},{5,7},{6,4},{7,5},{8,10},{9,11},{10,... | collective-permute-start | bytes 1572872 | tf_op jit(solution)/shard_map/ppermute | solution.py:229
  24.9 1.6 %collective-permute-start.10 = (bf16[2,272,512]{2,1,0:T(8,128)(2,1)S(1)}, bf16[2,272,512]{2,1,0:T(8,128)(2,1)S(1)}, u32[]{:S(2)}, u32[]{:S(2)}) collective-permute-start(bf16[2,272,512]{2,1,0:T(8,128)(2,1)S(1)} %constant_dynamic-update-slice_fusion.2.after_ref.point_ref.refs_0_), channel_id=1, source_target_pairs={{0,4},{1,5},{2,6},{3,7},{4,0},{5,1},{6,2},{7,3},{8,12},{9,13},{10,... | collective-permute-start | bytes 1671176 | tf_op jit(solution)/shard_map/ppermute | solution.py:229
  26.6 8.1 %alpha_sum.3 = (bf16[16,1024]{1,0:T(8,128)(2,1)S(1)}, bf16[8,1024,1024]{2,1,0:T(8,128)(2,1)S(1)}) custom-call(s32[1]{0:T(128)} %bitcast.4.me_ref, bf16[1024,16384]{1,0:T(8,128)(2,1)} %tri_ref.3, bf16[2,272,512]{2,1,0:T(8,128)(2,1)S(1)} %constant_dynamic-update-slice_fusion.2.after_ref.point_ref.refs_0_, ...), custom_call_target="tpu_custom_call" | custom-call | flops 2147483648 | bytes 16777216 | tf_op jit(solution)/shard_map/alpha_sum/pallas_call | solution.py:77
  34.7 2.1 %collective-permute-done.4.refs_1_ = bf16[512,512]{1,0:T(8,128)(2,1)S(1)} collective-permute-done((bf16[512,512]{1,0:T(8,128)(2,1)S(1)}, bf16[512,512]{1,0:T(8,128)(2,1)S(1)}, u32[]{:S(2)}, u32[]{:S(2)}) %collective-permute-start.4) | collective-permute-done | bytes 524320 | tf_op jit(solution)/shard_map/ppermute | solution.py:229
  37.3 1.5 %collective-permute-start.8 = (bf16[16,1024]{1,0:T(8,128)(2,1)S(1)}, bf16[16,1024]{1,0:T(8,128)(2,1)S(1)}, u32[]{:S(2)}, u32[]{:S(2)}) collective-permute-start(bf16[16,1024]{1,0:T(8,128)(2,1)S(1)} %get-tuple-element.30.refs_2_.refs_0_), channel_id=1, source_target_pairs={{0,2},{1,3},{2,0},{3,1},{4,6},{5,7},{6,4},{7,5},{8,10},{9,11},{10,... | collective-permute-start | bytes 98312 | tf_op jit(solution)/shard_map/ppermute | solution.py:229
  45.2 1.4 %partial_logits.1 = f32[16,1024]{1,0:T(8,128)S(1)} custom-call(bf16[16,1024]{1,0:T(8,128)(2,1)S(1)} %get-tuple-element.30.refs_2_.refs_0_, bf16[16,1024]{1,0:T(8,128)(2,1)S(1)} %collective-permute-done.7.refs_1_, bf16[16,1024]{1,0:T(8,128)(2,1)S(1)} %collective-permute-done.8.refs_2_, bf16[16,1024]{1,0:T(8,128)(2,1)S(1)} %collective-permute-done.11.refs_3_, ...), custom_call_target="tpu_custom_call" | custom-call | flops 1073741824 | bytes 1024 | tf_op jit(solution)/shard_map/partial_logits/pallas_call | solution.py:164
  46.6 1.6 %collective-permute-start.14 = (f32[16,1024]{1,0:T(8,128)S(1)}, f32[16,1024]{1,0:T(8,128)S(1)}, u32[]{:S(2)}, u32[]{:S(2)}) collective-permute-start(f32[16,1024]{1,0:T(8,128)S(1)} %partial_logits.1), channel_id=1, source_target_pairs={{0,4},{1,5},{2,6},{3,7},{4,0},{5,1},{6,2},{7,3},{8,12},{9,13},{10,... | collective-permute-start | bytes 196616 | tf_op jit(solution)/shard_map/ppermute | solution.py:229
  48.2 2.9 %collective-permute-done.14 = f32[16,1024]{1,0:T(8,128)S(1)} collective-permute-done((f32[16,1024]{1,0:T(8,128)S(1)}, f32[16,1024]{1,0:T(8,128)S(1)}, u32[]{:S(2)}, u32[]{:S(2)}) %collective-permute-start.14) | collective-permute-done | bytes 65568 | tf_op jit(solution)/shard_map/ppermute | solution.py:229
  51.4 6.2 %collective-permute-done.15.received_ref = f32[16,1024]{1,0:T(8,128)S(1)} collective-permute-done((f32[16,1024]{1,0:T(8,128)S(1)}, f32[16,1024]{1,0:T(8,128)S(1)}, u32[]{:S(2)}, u32[]{:S(2)}) %collective-permute-start.15) | collective-permute-done | bytes 65568 | tf_op jit(solution)/shard_map/ppermute | solution.py:229
  57.6 2.3 %kernel_gradient.1 = (f32[2,16,1024]{2,1,0:T(8,128)S(1)}, f32[2,16,1024]{2,1,0:T(8,128)S(1)}, f32[16,256]{1,0:T(8,128)}) custom-call(f32[16,1024]{1,0:T(8,128)S(1)} %maximum_add_fusion.sum_ref, f32[16,1024]{1,0:T(8,128)S(1)} %collective-permute-done.15.received_ref, f32[16,128]{1,0:T(8,128)S(1)} %broadcast_in_dim.16.bias_ref, ...), custom_call_target="tpu_custom_call" | custom-call | flops 1073741824 | bytes 1024 | tf_op jit(solution)/shard_map/kernel_gradient/pallas_call | solution.py:209
  59.9 1.4 %collective-permute-done.16 = f32[2,16,1024]{2,1,0:T(8,128)S(1)} collective-permute-done((f32[2,16,1024]{2,1,0:T(8,128)S(1)}, f32[2,16,1024]{2,1,0:T(8,128)S(1)}, u32[]{:S(2)}, u32[]{:S(2)}) %collective-permute-start.16) | collective-permute-done | bytes 131104 | tf_op jit(solution)/shard_map/ppermute | solution.py:229
  61.3 1.6 %collective-permute-start.17 = (f32[16,1024]{1,0:T(8,128)S(1)}, f32[16,1024]{1,0:T(8,128)S(1)}, u32[]{:S(2)}, u32[]{:S(2)}) collective-permute-start(f32[16,1024]{1,0:T(8,128)S(1)} %fusion.4), channel_id=1, source_target_pairs={{0,2},{1,3},{2,0},{3,1},{4,6},{5,7},{6,4},{7,5},{8,10},{9,11},{10,... | collective-permute-start | bytes 196616 | tf_op jit(solution)/shard_map/ppermute | solution.py:229
  62.8 2.8 %collective-permute-done.17 = f32[16,1024]{1,0:T(8,128)S(1)} collective-permute-done((f32[16,1024]{1,0:T(8,128)S(1)}, f32[16,1024]{1,0:T(8,128)S(1)}, u32[]{:S(2)}, u32[]{:S(2)}) %collective-permute-start.17) | collective-permute-done | bytes 65568 | tf_op jit(solution)/shard_map/ppermute | solution.py:229
  69.8 1.6 %collective-permute-start.20 = (f32[4,16,1024]{2,1,0:T(8,128)S(1)}, f32[4,16,1024]{2,1,0:T(8,128)S(1)}, u32[]{:S(2)}, u32[]{:S(2)}) collective-permute-start(f32[4,16,1024]{2,1,0:T(8,128)S(1)} %add.43), channel_id=1, source_target_pairs={{0,2},{1,3},{2,0},{3,1},{4,6},{5,7},{6,4},{7,5},{8,10},{9,11},{10,... | collective-permute-start | bytes 786440 | tf_op jit(solution)/shard_map/ppermute | solution.py:229
  72.6 5.5 %collective-permute-done.20 = f32[4,16,1024]{2,1,0:T(8,128)S(1)} collective-permute-done((f32[4,16,1024]{2,1,0:T(8,128)S(1)}, f32[4,16,1024]{2,1,0:T(8,128)S(1)}, u32[]{:S(2)}, u32[]{:S(2)}) %collective-permute-start.20) | collective-permute-done | bytes 262176 | tf_op jit(solution)/shard_map/ppermute | solution.py:229
  78.2 1.4 %collective-permute-start.22 = (f32[16,1024]{1,0:T(8,128)S(1)}, f32[16,1024]{1,0:T(8,128)S(1)}, u32[]{:S(2)}, u32[]{:S(2)}) collective-permute-start(f32[16,1024]{1,0:T(8,128)S(1)} %get-tuple-element.44), channel_id=1, source_target_pairs={{0,4},{1,5},{2,6},{3,7},{4,0},{5,1},{6,2},{7,3},{8,12},{9,13},{10,... | collective-permute-start | bytes 196616 | tf_op jit(solution)/shard_map/ppermute | solution.py:229
  79.6 3.0 %collective-permute-start.23 = (f32[16,1024]{1,0:T(8,128)S(1)}, f32[16,1024]{1,0:T(8,128)S(1)}, u32[]{:S(2)}, u32[]{:S(2)}) collective-permute-start(f32[16,1024]{1,0:T(8,128)S(1)} %get-tuple-element.43), channel_id=1, source_target_pairs={{0,12},{1,13},{2,14},{3,15},{4,8},{5,9},{6,10},{7,11},{8,4},{9,5},... | collective-permute-start | bytes 196616 | tf_op jit(solution)/shard_map/ppermute | solution.py:229
  82.6 2.4 %collective-permute-done.21 = f32[16,1024]{1,0:T(8,128)S(1)} collective-permute-done((f32[16,1024]{1,0:T(8,128)S(1)}, f32[16,1024]{1,0:T(8,128)S(1)}, u32[]{:S(2)}, u32[]{:S(2)}) %collective-permute-start.21) | collective-permute-done | bytes 65568 | tf_op jit(solution)/shard_map/ppermute | solution.py:229
  (65 shorter events, 17.2 us)
Async XLA Ops:
  0.7 7.0 %collective-permute-start = (bf16[1,16,1024]{2,1,0:T(8,128)(2,1)}, bf16[1,16,1024]{2,1,0:T(8,128)(2,1)S(1)}, u32[]{:S(2)}, u32[]{:S(2)}) collective-permute-start(bf16[1,16,1024]{2,1,0:T(8,128)(2,1)} %bitcast.35), channel_id=1, source_target_pairs={{0,8},{1,9},{2,10},{3,11},{4,12},{5,13},{6,14},{7,15},{8,0},{9,1},... | collective-permute-start | bytes 98312 | tf_op jit(solution)/shard_map/ppermute | solution.py:229
  4.8 34.1 %collective-permute-start.9 = (bf16[1024,512]{1,0:T(8,128)(2,1)}, bf16[1024,512]{1,0:T(8,128)(2,1)S(1)}, u32[]{:S(2)}, u32[]{:S(2)}) collective-permute-start(bf16[1024,512]{1,0:T(8,128)(2,1)} %refs_0_.3), channel_id=1, source_target_pairs={{0,1},{1,0},{2,3},{3,2},{4,5},{5,4},{6,7},{7,6},{8,9},{9,8},{10,11... | collective-permute-start | bytes 3145736 | tf_op jit(solution)/shard_map/ppermute | solution.py:229
  6.0 17.2 %collective-permute-start.3 = (bf16[512,512]{1,0:T(8,128)(2,1)S(1)}, bf16[512,512]{1,0:T(8,128)(2,1)S(1)}, u32[]{:S(2)}, u32[]{:S(2)}) collective-permute-start(bf16[512,512]{1,0:T(8,128)(2,1)S(1)} %get-tuple-element.40), channel_id=1, source_target_pairs={{0,2},{1,3},{2,0},{3,1},{4,6},{5,7},{6,4},{7,5},{8,10},{9,11},{10,... | collective-permute-start | bytes 1572872 | tf_op jit(solution)/shard_map/ppermute | solution.py:229
  7.7 4.3 %collective-permute-start.1 = (bf16[2,16,1024]{2,1,0:T(8,128)(2,1)S(1)}, bf16[2,16,1024]{2,1,0:T(8,128)(2,1)S(1)}, u32[]{:S(2)}, u32[]{:S(2)}) collective-permute-start(bf16[2,16,1024]{2,1,0:T(8,128)(2,1)S(1)} %pad_maximum_fusion.1), channel_id=1, source_target_pairs={{0,4},{1,5},{2,6},{3,7},{4,0},{5,1},{6,2},{7,3},{8,12},{9,13},{10,... | collective-permute-start | bytes 196616 | tf_op jit(solution)/shard_map/ppermute | solution.py:229
  9.4 15.5 %collective-permute-start.5 = (bf16[1,272,512]{2,1,0:T(8,128)(2,1)S(1)}, bf16[1,272,512]{2,1,0:T(8,128)(2,1)S(1)}, u32[]{:S(2)}, u32[]{:S(2)}) collective-permute-start(bf16[1,272,512]{2,1,0:T(8,128)(2,1)S(1)} %maximum_bitcast_fusion), channel_id=1, source_target_pairs={{0,8},{1,9},{2,10},{3,11},{4,12},{5,13},{6,14},{7,15},{8,0},{9,1},... | collective-permute-start | bytes 835592 | tf_op jit(solution)/shard_map/ppermute | solution.py:229
  12.1 11.2 %collective-permute-start.2 = (bf16[4,16,1024]{2,1,0:T(8,128)(2,1)S(1)}, bf16[4,16,1024]{2,1,0:T(8,128)(2,1)S(1)}, u32[]{:S(2)}, u32[]{:S(2)}) collective-permute-start(bf16[4,16,1024]{2,1,0:T(8,128)(2,1)S(1)} %constant_dynamic-update-slice_fusion.after_ref.beta_ref), channel_id=1, source_target_pairs={{0,2},{1,3},{2,0},{3,1},{4,6},{5,7},{6,4},{7,5},{8,10},{9,11},{10,... | collective-permute-start | bytes 393224 | tf_op jit(solution)/shard_map/ppermute | solution.py:229
  23.2 13.6 %collective-permute-start.4 = (bf16[512,512]{1,0:T(8,128)(2,1)S(1)}, bf16[512,512]{1,0:T(8,128)(2,1)S(1)}, u32[]{:S(2)}, u32[]{:S(2)}) collective-permute-start(bf16[512,512]{1,0:T(8,128)(2,1)S(1)} %get-tuple-element.24), channel_id=1, source_target_pairs={{0,2},{1,3},{2,0},{3,1},{4,6},{5,7},{6,4},{7,5},{8,10},{9,11},{10,... | collective-permute-start | bytes 1572872 | tf_op jit(solution)/shard_map/ppermute | solution.py:229
  24.8 1.8 %collective-permute-start.6 = (bf16[8,16,1024]{2,1,0:T(8,128)(2,1)S(1)}, bf16[8,16,1024]{2,1,0:T(8,128)(2,1)S(1)}, u32[]{:S(2)}, u32[]{:S(2)}) collective-permute-start(bf16[8,16,1024]{2,1,0:T(8,128)(2,1)S(1)} %pad_maximum_fusion), channel_id=1, source_target_pairs={{0,1},{1,0},{2,3},{3,2},{4,5},{5,4},{6,7},{7,6},{8,9},{9,8},{10,11... | collective-permute-start | bytes 786440 | tf_op jit(solution)/shard_map/ppermute | solution.py:229
  24.9 16.3 %collective-permute-start.10 = (bf16[2,272,512]{2,1,0:T(8,128)(2,1)S(1)}, bf16[2,272,512]{2,1,0:T(8,128)(2,1)S(1)}, u32[]{:S(2)}, u32[]{:S(2)}) collective-permute-start(bf16[2,272,512]{2,1,0:T(8,128)(2,1)S(1)} %constant_dynamic-update-slice_fusion.2.after_ref.point_ref.refs_0_), channel_id=1, source_target_pairs={{0,4},{1,5},{2,6},{3,7},{4,0},{5,1},{6,2},{7,3},{8,12},{9,13},{10,... | collective-permute-start | bytes 1671176 | tf_op jit(solution)/shard_map/ppermute | solution.py:229
  36.8 4.4 %collective-permute-start.12 = (bf16[512,512]{1,0:T(8,128)(2,1)S(1)}, bf16[512,512]{1,0:T(8,128)(2,1)S(1)}, u32[]{:S(2)}, u32[]{:S(2)}) collective-permute-start(bf16[512,512]{1,0:T(8,128)(2,1)S(1)} %collective-permute-done.3.refs_0_), channel_id=1, source_target_pairs={{0,1},{1,0},{2,3},{3,2},{4,5},{5,4},{6,7},{7,6},{8,9},{9,8},{10,11... | collective-permute-start | bytes 1572872 | tf_op jit(solution)/shard_map/ppermute | solution.py:229
  36.8 4.4 %collective-permute-start.13 = (bf16[512,512]{1,0:T(8,128)(2,1)S(1)}, bf16[512,512]{1,0:T(8,128)(2,1)S(1)}, u32[]{:S(2)}, u32[]{:S(2)}) collective-permute-start(bf16[512,512]{1,0:T(8,128)(2,1)S(1)} %collective-permute-done.4.refs_1_), channel_id=1, source_target_pairs={{0,1},{1,0},{2,3},{3,2},{4,5},{5,4},{6,7},{7,6},{8,9},{9,8},{10,11... | collective-permute-start | bytes 1572872 | tf_op jit(solution)/shard_map/ppermute | solution.py:229
  37.3 3.9 %collective-permute-start.8 = (bf16[16,1024]{1,0:T(8,128)(2,1)S(1)}, bf16[16,1024]{1,0:T(8,128)(2,1)S(1)}, u32[]{:S(2)}, u32[]{:S(2)}) collective-permute-start(bf16[16,1024]{1,0:T(8,128)(2,1)S(1)} %get-tuple-element.30.refs_2_.refs_0_), channel_id=1, source_target_pairs={{0,2},{1,3},{2,0},{3,1},{4,6},{5,7},{6,4},{7,5},{8,10},{9,11},{10,... | collective-permute-start | bytes 98312 | tf_op jit(solution)/shard_map/ppermute | solution.py:229
  38.8 6.4 %collective-permute-start.7 = (bf16[16,1024]{1,0:T(8,128)(2,1)S(1)}, bf16[16,1024]{1,0:T(8,128)(2,1)S(1)}, u32[]{:S(2)}, u32[]{:S(2)}) collective-permute-start(bf16[16,1024]{1,0:T(8,128)(2,1)S(1)} %get-tuple-element.30.refs_2_.refs_0_), channel_id=1, source_target_pairs={{0,1},{1,0},{2,3},{3,2},{4,5},{5,4},{6,7},{7,6},{8,9},{9,8},{10,11... | collective-permute-start | bytes 98312 | tf_op jit(solution)/shard_map/ppermute | solution.py:229
  41.2 4.0 %collective-permute-start.11 = (bf16[16,1024]{1,0:T(8,128)(2,1)S(1)}, bf16[16,1024]{1,0:T(8,128)(2,1)S(1)}, u32[]{:S(2)}, u32[]{:S(2)}) collective-permute-start(bf16[16,1024]{1,0:T(8,128)(2,1)S(1)} %collective-permute-done.8.refs_2_), channel_id=1, source_target_pairs={{0,1},{1,0},{2,3},{3,2},{4,5},{5,4},{6,7},{7,6},{8,9},{9,8},{10,11... | collective-permute-start | bytes 98312 | tf_op jit(solution)/shard_map/ppermute | solution.py:229
  46.6 4.5 %collective-permute-start.14 = (f32[16,1024]{1,0:T(8,128)S(1)}, f32[16,1024]{1,0:T(8,128)S(1)}, u32[]{:S(2)}, u32[]{:S(2)}) collective-permute-start(f32[16,1024]{1,0:T(8,128)S(1)} %partial_logits.1), channel_id=1, source_target_pairs={{0,4},{1,5},{2,6},{3,7},{4,0},{5,1},{6,2},{7,3},{8,12},{9,13},{10,... | collective-permute-start | bytes 196616 | tf_op jit(solution)/shard_map/ppermute | solution.py:229
  51.1 6.4 %collective-permute-start.15 = (f32[16,1024]{1,0:T(8,128)S(1)}, f32[16,1024]{1,0:T(8,128)S(1)}, u32[]{:S(2)}, u32[]{:S(2)}) collective-permute-start(f32[16,1024]{1,0:T(8,128)S(1)} %maximum_add_fusion.sum_ref), channel_id=1, source_target_pairs={{0,8},{1,9},{2,10},{3,11},{4,12},{5,13},{6,14},{7,15},{8,0},{9,1},... | collective-permute-start | bytes 196616 | tf_op jit(solution)/shard_map/ppermute | solution.py:229
  59.9 1.4 %collective-permute-start.16 = (f32[2,16,1024]{2,1,0:T(8,128)S(1)}, f32[2,16,1024]{2,1,0:T(8,128)S(1)}, u32[]{:S(2)}, u32[]{:S(2)}) collective-permute-start(f32[2,16,1024]{2,1,0:T(8,128)S(1)} %get-tuple-element.37), channel_id=1, source_target_pairs={{0,1},{1,0},{2,3},{3,2},{4,5},{5,4},{6,7},{7,6},{8,9},{9,8},{10,11... | collective-permute-start | bytes 393224 | tf_op jit(solution)/shard_map/ppermute | solution.py:229
  61.3 4.3 %collective-permute-start.17 = (f32[16,1024]{1,0:T(8,128)S(1)}, f32[16,1024]{1,0:T(8,128)S(1)}, u32[]{:S(2)}, u32[]{:S(2)}) collective-permute-start(f32[16,1024]{1,0:T(8,128)S(1)} %fusion.4), channel_id=1, source_target_pairs={{0,2},{1,3},{2,0},{3,1},{4,6},{5,7},{6,4},{7,5},{8,10},{9,11},{10,... | collective-permute-start | bytes 196616 | tf_op jit(solution)/shard_map/ppermute | solution.py:229
  66.8 2.9 %collective-permute-start.19 = (f32[4,16,1024]{2,1,0:T(8,128)S(1)}, f32[4,16,1024]{2,1,0:T(8,128)S(1)}, u32[]{:S(2)}, u32[]{:S(2)}) collective-permute-start(f32[4,16,1024]{2,1,0:T(8,128)S(1)} %gradient_terms.7), channel_id=1, source_target_pairs={{0,1},{1,0},{2,3},{3,2},{4,5},{5,4},{6,7},{7,6},{8,9},{9,8},{10,11... | collective-permute-start | bytes 786440 | tf_op jit(solution)/shard_map/ppermute | solution.py:229
  68.0 4.5 %collective-permute-start.18 = (f32[4,16,1024]{2,1,0:T(8,128)S(1)}, f32[4,16,1024]{2,1,0:T(8,128)S(1)}, u32[]{:S(2)}, u32[]{:S(2)}) collective-permute-start(f32[4,16,1024]{2,1,0:T(8,128)S(1)} %gradient_terms.5), channel_id=1, source_target_pairs={{0,1},{1,0},{2,3},{3,2},{4,5},{5,4},{6,7},{7,6},{8,9},{9,8},{10,11... | collective-permute-start | bytes 786440 | tf_op jit(solution)/shard_map/ppermute | solution.py:229
  69.8 8.3 %collective-permute-start.20 = (f32[4,16,1024]{2,1,0:T(8,128)S(1)}, f32[4,16,1024]{2,1,0:T(8,128)S(1)}, u32[]{:S(2)}, u32[]{:S(2)}) collective-permute-start(f32[4,16,1024]{2,1,0:T(8,128)S(1)} %add.43), channel_id=1, source_target_pairs={{0,2},{1,3},{2,0},{3,1},{4,6},{5,7},{6,4},{7,5},{8,10},{9,11},{10,... | collective-permute-start | bytes 786440 | tf_op jit(solution)/shard_map/ppermute | solution.py:229
  78.1 6.9 %collective-permute-start.21 = (f32[16,1024]{1,0:T(8,128)S(1)}, f32[16,1024]{1,0:T(8,128)S(1)}, u32[]{:S(2)}, u32[]{:S(2)}) collective-permute-start(f32[16,1024]{1,0:T(8,128)S(1)} %get-tuple-element.42), channel_id=1, source_target_pairs={{0,8},{1,9},{2,10},{3,11},{4,12},{5,13},{6,14},{7,15},{8,0},{9,1},... | collective-permute-start | bytes 196616 | tf_op jit(solution)/shard_map/ppermute | solution.py:229
  78.2 6.8 %collective-permute-start.22 = (f32[16,1024]{1,0:T(8,128)S(1)}, f32[16,1024]{1,0:T(8,128)S(1)}, u32[]{:S(2)}, u32[]{:S(2)}) collective-permute-start(f32[16,1024]{1,0:T(8,128)S(1)} %get-tuple-element.44), channel_id=1, source_target_pairs={{0,4},{1,5},{2,6},{3,7},{4,0},{5,1},{6,2},{7,3},{8,12},{9,13},{10,... | collective-permute-start | bytes 196616 | tf_op jit(solution)/shard_map/ppermute | solution.py:229
  79.6 6.2 %collective-permute-start.23 = (f32[16,1024]{1,0:T(8,128)S(1)}, f32[16,1024]{1,0:T(8,128)S(1)}, u32[]{:S(2)}, u32[]{:S(2)}) collective-permute-start(f32[16,1024]{1,0:T(8,128)S(1)} %get-tuple-element.43), channel_id=1, source_target_pairs={{0,12},{1,13},{2,14},{3,15},{4,8},{5,9},{6,10},{7,11},{8,4},{9,5},... | collective-permute-start | bytes 196616 | tf_op jit(solution)/shard_map/ppermute | solution.py:229
  (5 other events, 45.6 us)

commit v3 on v2

--- a/solution.py
+++ b/solution.py
@@ -89,23 +89,23 @@
     )(*operands)
 
 
-def gradient_terms(grad, blocks, first, count):
+def gradient_terms(grad, blocks, first, count, step, after):
     classes, rows = grad.shape
     width = blocks.shape[2]
 
-    def body(grad_ref, block_ref, out_ref):
+    def body(after_ref, grad_ref, block_ref, out_ref):
         for at in range(count):
-            out_ref[at] = jnp.dot(grad_ref[...], block_ref[first + at], preferred_element_type=F32)
+            out_ref[at] = jnp.dot(grad_ref[...], block_ref[first + step * at], preferred_element_type=F32)
 
     return pl.pallas_call(
         body,
         out_shape=jax.ShapeDtypeStruct((count, classes, width), F32),
-        in_specs=[in_vmem(), in_vmem()],
+        in_specs=[anywhere(), in_vmem(), in_vmem()],
         out_specs=in_vmem(),
         compiler_params=params(8),
         cost_estimate=cost(2 * rows * count * width * 128, 1024),
         name="gradient_terms",
-    )(grad, pltpu.with_memory_space_constraint(blocks, pltpu.VMEM))
+    )(after, grad, pltpu.with_memory_space_constraint(blocks, pltpu.VMEM))
 
 
 def kernel_tile(block, points, centre_blocks, after):
@@ -172,51 +172,72 @@
     )(*alphas, *flat)
 
 
-def kernel_gradient(logit_sum, received, order, bias, points, tiles):
-    flat = [tile for row in tiles for tile in row]
-    n_parts = len(tiles[0])
-    local = flat[0].shape[1]
-    sizes = [row[0].shape[2] for row in tiles]
+def residual(logit_sum, received, order, bias, points):
     classes, total = logit_sum.shape
     block = total // len(order)
-
-    def body(sum_ref, received_ref, bias_ref, *refs):
-        point_refs, tile_refs = refs[: len(points)], refs[len(points) : len(points) + len(flat)]
-        *out_refs, logits_ref, resid_ref = refs[len(points) + len(flat) :]
+    blocks = [(which, at) for which, array in enumerate(points) for at in range(array.shape[0])]
+
+    def compute(sum_ref, received_ref, bias_ref, point_refs, logits_ref, resid_ref):
         for at, source in enumerate(order):
             here = slice(at * block, (at + 1) * block)
             there = slice(source * block, (source + 1) * block)
             logits = sum_ref[:, here] + received_ref[:, there] + bias_ref[:, :1]
             if at == 0:
                 logits_ref[...] = logits
-            held = point_refs[at // points[0].shape[0]]
-            onehot = held[at % points[0].shape[0], block : block + classes, :block].astype(F32)
+            which, row = blocks[at]
+            onehot = point_refs[which][row, block : block + classes, :block].astype(F32)
             resid_ref[:, here] = (jax.nn.sigmoid(logits) - onehot).astype(BF16)
-        for parity, out_ref in enumerate(out_refs):
-            for which in range(n_parts):
-                acc = None
-                for part, size in enumerate(sizes):
-                    first = sum(sizes[:part])
-                    term = lax.dot_general(
-                        resid_ref[:, first : first + size],
-                        tile_refs[part * n_parts + which][parity],
-                        ROWS_BY_ROWS,
-                        preferred_element_type=F32,
-                    )
-                    acc = term if acc is None else acc + term
-                out_ref[which] = acc
-
-    return pl.pallas_call(
-        body,
-        out_shape=[jax.ShapeDtypeStruct((n_parts, classes, local), F32)] * 2
-        + [jax.ShapeDtypeStruct((classes, block), F32)],
-        in_specs=[in_vmem()] * (3 + len(points) + len(flat)),
-        out_specs=[in_vmem()] * 3,
-        scratch_shapes=[pltpu.VMEM((classes, total), BF16)],
-        compiler_params=params(8),
-        cost_estimate=cost(2 * sum(tile.size for tile in flat) * 128, 1024),
+
+    return compute
+
+
+def kernel_gradient(parity, resid, tiles, residual_of=None):
+    flat = [tile for row in tiles for tile in row]
+    n_parts = len(tiles[0])
+    local = flat[0].shape[1]
+    sizes = [row[0].shape[2] for row in tiles]
+    total = sum(sizes)
+    out_shape = []
+    if residual_of is None:
+        operands = [resid]
+    else:
+        compute, (logit_sum, received, bias, points) = residual_of
+        operands = [logit_sum, received, bias, *points]
+        block = points[0].shape[1] - logit_sum.shape[0]
+        out_shape = [jax.ShapeDtypeStruct((logit_sum.shape[0], block), F32)]
+        out_shape.append(jax.ShapeDtypeStruct(logit_sum.shape, BF16))
+    classes = operands[0].shape[0]
+    n_operands = len(operands)
+
+    def body(*refs):
+        tile_refs = refs[n_operands : n_operands + len(flat)]
+        out_ref, *more_refs = refs[n_operands + len(flat) :]
+        resid_ref = refs[0]
+        if residual_of is not None:
+            logits_ref, resid_ref = more_refs
+            compute(*refs[:3], refs[3:n_operands], logits_ref, resid_ref)
+        for which in range(n_parts):
+            acc = None
+            for part, size in enumerate(sizes):
+                first = sum(sizes[:part])
+                term = lax.dot_general(
+                    resid_ref[:, first : first + size],
+                    tile_refs[part * n_parts + which][parity],
+                    ROWS_BY_ROWS,
+                    preferred_element_type=F32,
+                )
+                acc = term if acc is None else acc + term
+            out_ref[which] = acc
+
+    return pl.pallas_call(
+        body,
+        out_shape=[jax.ShapeDtypeStruct((n_parts, classes, local), F32)] + out_shape,
+        in_specs=[in_vmem()] * (n_operands + len(flat)),
+        out_specs=[in_vmem()] * (1 + len(out_shape)),
+        compiler_params=params(8),
+        cost_estimate=cost(2 * total * n_parts * local * 128, 1024),
         name="kernel_gradient",
-    )(logit_sum, received, bias, *points, *flat)
+    )(*operands, *flat)
 
 
 def on_device(points, labels, centres, tri_inverse, beta, bias):
@@ -236,7 +257,7 @@
 
     block, features = points.shape
     points = jnp.concatenate([points, jnp.pad(onehot, ((0, 0), (0, features - block)))])[None]
-    half = local_centres // 2
+    half = local_centres * 1//2
     centre_halves = [centres[:half], centres[half:]]
     centres_2 = [swap(centre_halves[0], 2)]
     coeffs = beta.T[None]
@@ -248,12 +269,13 @@
             points, coeffs = lax.optimization_barrier((points, coeffs))
             points = jnp.concatenate([points, swap(points, mask)])
     count = len(far)
+    later, coeffs = lax.optimization_barrier((centre_halves[1], coeffs))
     coeffs_2 = swap(coeffs, 2)
+    centres_2.append(swap(later, 2))
     near_2 = [offset ^ 2 for offset in far]
     near_13 = [offset ^ 1 for offset in far + near_2]
     alpha, tri_02 = alpha_sum(me, tri_inverse, (far + near_2, coeffs), None, None, coeffs)
-    later, coeffs_2, alpha, centres_2[0] = lax.optimization_barrier((centre_halves[1], coeffs_2, alpha, centres_2[0]))
-    centres_2.append(swap(later, 2))
+    coeffs_2, alpha, centres_2[0] = lax.optimization_barrier((coeffs_2, alpha, centres_2[0]))
     coeffs_13 = swap(jnp.concatenate([coeffs, coeffs_2]), 1)
     alpha, tri_13 = alpha_sum(me, tri_inverse, (near_13, coeffs_13), (tri_02, count, coeffs_2), alpha, points)
     points = [points, swap(points, outer[0])]
@@ -278,23 +300,39 @@
         if mask != outer[-1]:
             moved = [received[:, source * block : (source + 1) * block] for source in order]
             logit_sum = logit_sum + jnp.concatenate(moved, axis=1)
-    keep, send, logits = kernel_gradient(logit_sum, received, order, bias_column, points, tiles)
-
+    compute = residual(logit_sum, received, order, bias_column, points)
+    send, logits, resid = kernel_gradient(1, None, tiles, (compute, (logit_sum, received, bias_column, points)))
     received = swap(send, 1)
+    (keep,) = kernel_gradient(0, resid, tiles)
+
     received_2 = swap(keep[1] + received[1], 2)
     grad = ((keep[0] + received[0] + received_2) * (1.0 / math.sqrt(total_points))).astype(BF16)
 
-    term_3 = gradient_terms(grad, tri_13, count, count)
-    received_3 = swap(term_3, 1)
-    term_2 = gradient_terms(grad, tri_02, count, count)
-    received_2 = swap(term_2 + received_3, 2)
-    term_1 = gradient_terms(grad, tri_13, 0, count)
-    received_1 = swap(term_1, 1)
-    term_0 = gradient_terms(grad, tri_02, 0, count)
-    total = term_0 + received_1 + received_2
-    gradient = total[0]
-    for at, offset in enumerate(far[1:], 1):
-        gradient = gradient + swap(total[at], offset)
+    half = count // 2
+    position = {offset: at for at, offset in enumerate(far)}
+    near_first = sorted(far, key=lambda offset: (offset & outer[-1], position[offset]))
+    latest = grad
+    sums = {}
+    for offsets in (near_first[half:], near_first[:half]):
+        at = position[offsets[0]]
+        step = position[offsets[1]] - at if half > 1 else 1
+        parts = []
+        for held, first in ((tri_13, count), (tri_02, count), (tri_13, 0), (tri_02, 0)):
+            parts.append((held, first + at))
+        term_3 = gradient_terms(grad, *parts[0], half, step, latest)
+        received_3 = swap(term_3, 1)
+        term_2 = gradient_terms(grad, *parts[1], half, step, term_3)
+        ahead = term_2 + received_3
+        received_2 = swap(ahead, 2)
+        term_1 = gradient_terms(grad, *parts[2], half, step, ahead)
+        received_1 = swap(term_1, 1)
+        latest = gradient_terms(grad, *parts[3], half, step, term_1)
+        total = latest + received_1 + received_2
+        for index, offset in enumerate(offsets):
+            sums[offset] = total[index]
+    gradient = sums[0]
+    for offset in reversed(near_first[1:]):
+        gradient = gradient + swap(sums[offset], offset)
     return (gradient.T, logits.T)
 
 

time: 86.6 us -> 83.7 us (0.967)
  starting transfers between devices: 26.1 us -> 23.1 us
  waiting for transfers between devices: 29 us -> 27.6 us
    ppermute x24 -> x27, starting transfers between devices: 26.1 us -> 23.1 us  [swap(): lax.ppermute(array, 'pts', [(index, index ^ mask) for index in range(devi...]
    ppermute x24 -> x27, waiting for transfers between devices: 29 us -> 27.6 us  [swap(): lax.ppermute(array, 'pts', [(index, index ^ mask) for index in range(devi...]
    pallas_call x4 -> x8, Pallas kernels: 4.79 us -> 5.23 us  [gradient_terms(): pl.pallas_call(body, out_shape=jax.ShapeDtypeStruct((count, classes, widt...]
    pallas_call x1 -> x2, Pallas kernels: 2.29 us -> 2.41 us  [kernel_gradient(): pl.pallas_call(body, out_shape=[jax.ShapeDtypeStruct((n_parts, classes, l...]
  transfers between devices with their start and end apart: 24 -> 27, of which waited for: 11 -> 14; matrix products, arithmetic and copies ran while one was open for 2% -> 3% of each run, Pallas kernels for 27% -> 28%
where the time goes in v3:
time: 83.7 us; the launch traced here: 83.5 us
  Pallas kernels  28.8 us (34%)
  waiting for transfers between devices  27.6 us (33%)
  starting transfers between devices  23.1 us (28%)
  local copies, waits for them, and re-layouts  2.21 us (3%)
  between operations  0.9 us (1%)
  other arithmetic  0.88 us (1%)
    ppermute x27, waiting for transfers between devices, swap(): lax.ppermute(array, 'pts', [(index, index ^ mask) for index in range(devi...  27.6 us
    ppermute x27, starting transfers between devices, swap(): lax.ppermute(array, 'pts', [(index, index ^ mask) for index in range(devi...  23.1 us
    pallas_call x2, Pallas kernels, alpha_sum(): pl.pallas_call(body, out_shape=[jax.ShapeDtypeStruct((classes, rows), BF1...  14.5 us
    pallas_call x4, Pallas kernels, kernel_tile(): pl.pallas_call(body, out_shape=pltpu.VMEM((len(centre_blocks), local, tot...  5.28 us
    pallas_call x8, Pallas kernels, gradient_terms(): pl.pallas_call(body, out_shape=jax.ShapeDtypeStruct((count, classes, widt...  5.23 us
    pallas_call x2, Pallas kernels, kernel_gradient(): pl.pallas_call(body, out_shape=[jax.ShapeDtypeStruct((n_parts, classes, l...  2.41 us
    slice x1, local copies, waits for them, and re-layouts, on_device(): centre_halves = [centres[:half], centres[half:]]  2.06 us
  transfers between devices with their start and end apart: 27, of which 14 were waited for; matrix products, arithmetic and copies ran while one was open for 3% of the time, Pallas kernels for 28%

profile of v3, /device:TPU:0, one launch (start us, length us, event | category | flops | bytes accessed | tf_op | source)
XLA Modules:
  0.0 83.5 jit_solution(478621385759909216)
XLA Ops:
  0.7 4.1 %collective-permute-start = (bf16[1,16,1024]{2,1,0:T(8,128)(2,1)}, bf16[1,16,1024]{2,1,0:T(8,128)(2,1)S(1)}, u32[]{:S(2)}, u32[]{:S(2)}) collective-permute-start(bf16[1,16,1024]{2,1,0:T(8,128)(2,1)} %bitcast.35), channel_id=1, source_target_pairs={{0,8},{1,9},{2,10},{3,11},{4,12},{5,13},{6,14},{7,15},{8,0},{9,1},... | collective-permute-start | bytes 98312 | tf_op jit(solution)/shard_map/ppermute | solution.py:250
  4.8 2.1 %fusion.9 = (bf16[512,512]{1,0:T(8,128)(2,1)}, bf16[512,512]{1,0:T(8,128)(2,1)S(1)}) fusion(bf16[1024,512]{1,0:T(8,128)(2,1)} %refs_0_.3), kind=kLoop, calls=%fused_computation.26 | loop fusion | bytes 2097152 | tf_op jit(solution)/shard_map/slice | solution.py:261
  6.8 1.5 %collective-permute-start.3 = (bf16[512,512]{1,0:T(8,128)(2,1)}, bf16[512,512]{1,0:T(8,128)(2,1)S(1)}, u32[]{:S(2)}, u32[]{:S(2)}) collective-permute-start(bf16[512,512]{1,0:T(8,128)(2,1)} %get-tuple-element.42), channel_id=1, source_target_pairs={{0,2},{1,3},{2,0},{3,1},{4,6},{5,7},{6,4},{7,5},{8,10},{9,11},{10,... | collective-permute-start | bytes 1572872 | tf_op jit(solution)/shard_map/ppermute | solution.py:250
  8.4 1.6 %collective-permute-start.1 = (bf16[2,16,1024]{2,1,0:T(8,128)(2,1)S(1)}, bf16[2,16,1024]{2,1,0:T(8,128)(2,1)S(1)}, u32[]{:S(2)}, u32[]{:S(2)}) collective-permute-start(bf16[2,16,1024]{2,1,0:T(8,128)(2,1)S(1)} %pad_maximum_fusion.2), channel_id=1, source_target_pairs={{0,4},{1,5},{2,6},{3,7},{4,0},{5,1},{6,2},{7,3},{8,12},{9,13},{10,... | collective-permute-start | bytes 196616 | tf_op jit(solution)/shard_map/ppermute | solution.py:250
  10.1 1.6 %collective-permute-start.5 = (bf16[1,272,512]{2,1,0:T(8,128)(2,1)S(1)}, bf16[1,272,512]{2,1,0:T(8,128)(2,1)S(1)}, u32[]{:S(2)}, u32[]{:S(2)}) collective-permute-start(bf16[1,272,512]{2,1,0:T(8,128)(2,1)S(1)} %maximum_bitcast_fusion), channel_id=1, source_target_pairs={{0,8},{1,9},{2,10},{3,11},{4,12},{5,13},{6,14},{7,15},{8,0},{9,1},... | collective-permute-start | bytes 835592 | tf_op jit(solution)/shard_map/ppermute | solution.py:250
  13.4 1.5 %collective-permute-start.4 = (bf16[512,512]{1,0:T(8,128)(2,1)S(1)}, bf16[512,512]{1,0:T(8,128)(2,1)S(1)}, u32[]{:S(2)}, u32[]{:S(2)}) collective-permute-start(bf16[512,512]{1,0:T(8,128)(2,1)S(1)} %get-tuple-element.26), channel_id=1, source_target_pairs={{0,2},{1,3},{2,0},{3,1},{4,6},{5,7},{6,4},{7,5},{8,10},{9,11},{10,... | collective-permute-start | bytes 1572872 | tf_op jit(solution)/shard_map/ppermute | solution.py:250
  14.9 6.5 %alpha_sum.2 = (f32[16,1024]{1,0:T(8,128)S(1)}, bf16[8,1024,1024]{2,1,0:T(8,128)(2,1)S(1)}) custom-call(s32[1]{0:T(128)} %bitcast.4.me_ref, bf16[1024,16384]{1,0:T(8,128)(2,1)} %tri_ref.3, bf16[4,16,1024]{2,1,0:T(8,128)(2,1)S(1)} %pad_maximum_fusion.1.after_ref.beta_ref, bf16[4,16,1024]{2,1,0:T(8,128)(2,1)S(1)} %pad_maximum_fusion.1.after_ref.beta_ref), custom_call_target="tpu_custom_call" | custom-call | flops 2147483648 | bytes 16777216 | tf_op jit(solution)/shard_map/alpha_sum/pallas_call | solution.py:77
  21.4 3.3 %collective-permute-done.2.refs_2_ = bf16[4,16,1024]{2,1,0:T(8,128)(2,1)S(1)} collective-permute-done((bf16[4,16,1024]{2,1,0:T(8,128)(2,1)S(1)}, bf16[4,16,1024]{2,1,0:T(8,128)(2,1)S(1)}, u32[]{:S(2)}, u32[]{:S(2)}) %collective-permute-start.2) | collective-permute-done | bytes 131104 | tf_op jit(solution)/shard_map/ppermute | solution.py:250
  26.5 8.1 %alpha_sum.3 = (bf16[16,1024]{1,0:T(8,128)(2,1)S(1)}, bf16[8,1024,1024]{2,1,0:T(8,128)(2,1)S(1)}) custom-call(s32[1]{0:T(128)} %bitcast.4.me_ref, bf16[1024,16384]{1,0:T(8,128)(2,1)} %tri_ref.3, bf16[2,272,512]{2,1,0:T(8,128)(2,1)S(1)} %constant_dynamic-update-slice_fusion.after_ref.point_ref.refs_3_, ...), custom_call_target="tpu_custom_call" | custom-call | flops 2147483648 | bytes 16777216 | tf_op jit(solution)/shard_map/alpha_sum/pallas_call | solution.py:77
  35.2 1.5 %collective-permute-start.8 = (bf16[16,1024]{1,0:T(8,128)(2,1)S(1)}, bf16[16,1024]{1,0:T(8,128)(2,1)S(1)}, u32[]{:S(2)}, u32[]{:S(2)}) collective-permute-start(bf16[16,1024]{1,0:T(8,128)(2,1)S(1)} %get-tuple-element.32.refs_2_.refs_0_), channel_id=1, source_target_pairs={{0,2},{1,3},{2,0},{3,1},{4,6},{5,7},{6,4},{7,5},{8,10},{9,11},{10,... | collective-permute-start | bytes 98312 | tf_op jit(solution)/shard_map/ppermute | solution.py:250
  36.7 1.3 %kernel_tile.4.refs_4_.refs_5_.refs_1_ = bf16[2,1024,512]{2,1,0:T(8,128)(2,1)S(1)} custom-call(bf16[2,272,512]{2,1,0:T(8,128)(2,1)S(1)} %constant_dynamic-update-slice_fusion.after_ref.point_ref.refs_3_, bf16[1024,512]{1,0:T(8,128)(2,1)S(1)} %copy-done, bf16[1024,512]{1,0:T(8,128)(2,1)S(1)} %collective-permute-done.9.refs_1_, ...), custom_call_target="tpu_custom_call" | custom-call | flops 1073741824 | bytes 1024 | tf_op jit(solution)/shard_map/kernel_tile/pallas_call | solution.py:133
  39.1 1.5 %collective-permute-done.10.point_ref.refs_4_ = bf16[2,272,512]{2,1,0:T(8,128)(2,1)S(1)} collective-permute-done((bf16[2,272,512]{2,1,0:T(8,128)(2,1)S(1)}, bf16[2,272,512]{2,1,0:T(8,128)(2,1)S(1)}, u32[]{:S(2)}, u32[]{:S(2)}) %collective-permute-start.10) | collective-permute-done | bytes 557088 | tf_op jit(solution)/shard_map/ppermute | solution.py:250
  40.6 1.3 %kernel_tile.5.refs_2_.refs_5_.refs_6_ = bf16[2,1024,512]{2,1,0:T(8,128)(2,1)S(1)} custom-call(bf16[2,272,512]{2,1,0:T(8,128)(2,1)S(1)} %constant_dynamic-update-slice_fusion.after_ref.point_ref.refs_3_, bf16[512,512]{1,0:T(8,128)(2,1)S(1)} %collective-permute-done.3.refs_0_, bf16[512,512]{1,0:T(8,128)(2,1)S(1)} %collective-permute-done.4.refs_1_, ...), custom_call_target="tpu_custom_call" | custom-call | flops 1073741824 | bytes 1024 | tf_op jit(solution)/shard_map/kernel_tile/pallas_call | solution.py:133
  42.0 1.3 %kernel_tile.6.refs_4_.refs_6_.refs_7_.refs_3_ = bf16[2,1024,512]{2,1,0:T(8,128)(2,1)S(1)} custom-call(bf16[2,272,512]{2,1,0:T(8,128)(2,1)S(1)} %collective-permute-done.10.point_ref.refs_4_, bf16[1024,512]{1,0:T(8,128)(2,1)S(1)} %copy-done, bf16[1024,512]{1,0:T(8,128)(2,1)S(1)} %collective-permute-done.9.refs_1_, ...), custom_call_target="tpu_custom_call" | custom-call | flops 1073741824 | bytes 1024 | tf_op jit(solution)/shard_map/kernel_tile/pallas_call | solution.py:133
  43.3 1.3 %kernel_tile.7.refs_7_.refs_8_.refs_4_ = bf16[2,1024,512]{2,1,0:T(8,128)(2,1)S(1)} custom-call(bf16[2,272,512]{2,1,0:T(8,128)(2,1)S(1)} %collective-permute-done.10.point_ref.refs_4_, bf16[512,512]{1,0:T(8,128)(2,1)S(1)} %collective-permute-done.3.refs_0_, bf16[512,512]{1,0:T(8,128)(2,1)S(1)} %collective-permute-done.4.refs_1_, ...), custom_call_target="tpu_custom_call" | custom-call | flops 1073741824 | bytes 1024 | tf_op jit(solution)/shard_map/kernel_tile/pallas_call | solution.py:133
  44.6 1.4 %partial_logits.1 = f32[16,1024]{1,0:T(8,128)S(1)} custom-call(bf16[16,1024]{1,0:T(8,128)(2,1)S(1)} %get-tuple-element.32.refs_2_.refs_0_, bf16[16,1024]{1,0:T(8,128)(2,1)S(1)} %collective-permute-done.7.refs_1_, bf16[16,1024]{1,0:T(8,128)(2,1)S(1)} %collective-permute-done.8.refs_2_, bf16[16,1024]{1,0:T(8,128)(2,1)S(1)} %collective-permute-done.11.refs_3_, ...), custom_call_target="tpu_custom_call" | custom-call | flops 1073741824 | bytes 1024 | tf_op jit(solution)/shard_map/partial_logits/pallas_call | solution.py:164
  46.9 3.6 %collective-permute-done.14 = f32[16,1024]{1,0:T(8,128)S(1)} collective-permute-done((f32[16,1024]{1,0:T(8,128)S(1)}, f32[16,1024]{1,0:T(8,128)S(1)}, u32[]{:S(2)}, u32[]{:S(2)}) %collective-permute-start.14) | collective-permute-done | bytes 65568 | tf_op jit(solution)/shard_map/ppermute | solution.py:250
  50.6 6.0 %collective-permute-done.15.refs_1_ = f32[16,1024]{1,0:T(8,128)S(1)} collective-permute-done((f32[16,1024]{1,0:T(8,128)S(1)}, f32[16,1024]{1,0:T(8,128)S(1)}, u32[]{:S(2)}, u32[]{:S(2)}) %collective-permute-start.15) | collective-permute-done | bytes 65568 | tf_op jit(solution)/shard_map/ppermute | solution.py:250
  56.7 1.2 %kernel_gradient.2 = (f32[2,16,1024]{2,1,0:T(8,128)S(1)}, f32[16,256]{1,0:T(8,128)}, bf16[16,1024]{1,0:T(8,128)(2,1)S(1)}) custom-call(f32[16,1024]{1,0:T(8,128)S(1)} %maximum_add_fusion.refs_0_, f32[16,1024]{1,0:T(8,128)S(1)} %collective-permute-done.15.refs_1_, f32[16,128]{1,0:T(8,128)S(1)} %broadcast_in_dim.16.refs_2_, ...), custom_call_target="tpu_custom_call" | custom-call | flops 536870912 | bytes 1024 | tf_op jit(solution)/shard_map/kernel_gradient/pallas_call | solution.py:232
  59.3 1.2 %collective-permute-start.17 = (f32[16,1024]{1,0:T(8,128)S(1)}, f32[16,1024]{1,0:T(8,128)S(1)}, u32[]{:S(2)}, u32[]{:S(2)}) collective-permute-start(f32[16,1024]{1,0:T(8,128)S(1)} %fusion.4), channel_id=1, source_target_pairs={{0,2},{1,3},{2,0},{3,1},{4,6},{5,7},{6,4},{7,5},{8,10},{9,11},{10,... | collective-permute-start | bytes 196616 | tf_op jit(solution)/shard_map/ppermute | solution.py:250
  60.5 3.2 %collective-permute-done.17 = f32[16,1024]{1,0:T(8,128)S(1)} collective-permute-done((f32[16,1024]{1,0:T(8,128)S(1)}, f32[16,1024]{1,0:T(8,128)S(1)}, u32[]{:S(2)}, u32[]{:S(2)}) %collective-permute-start.17) | collective-permute-done | bytes 65568 | tf_op jit(solution)/shard_map/ppermute | solution.py:250
  71.7 2.9 %collective-permute-done.23 = f32[2,16,1024]{2,1,0:T(8,128)S(1)} collective-permute-done((f32[2,16,1024]{2,1,0:T(8,128)S(1)}, f32[2,16,1024]{2,1,0:T(8,128)S(1)}, u32[]{:S(2)}, u32[]{:S(2)}) %collective-permute-start.23) | collective-permute-done | bytes 131104 | tf_op jit(solution)/shard_map/ppermute | solution.py:250
  76.9 3.0 %collective-permute-start.26 = (f32[16,1024]{1,0:T(8,128)S(1)}, f32[16,1024]{1,0:T(8,128)S(1)}, u32[]{:S(2)}, u32[]{:S(2)}) collective-permute-start(f32[16,1024]{1,0:T(8,128)S(1)} %slice_bitcast_fusion), channel_id=1, source_target_pairs={{0,4},{1,5},{2,6},{3,7},{4,0},{5,1},{6,2},{7,3},{8,12},{9,13},{10,... | collective-permute-start | bytes 196616 | tf_op jit(solution)/shard_map/ppermute | solution.py:250
  80.9 1.6 %collective-permute-done.25 = f32[16,1024]{1,0:T(8,128)S(1)} collective-permute-done((f32[16,1024]{1,0:T(8,128)S(1)}, f32[16,1024]{1,0:T(8,128)S(1)}, u32[]{:S(2)}, u32[]{:S(2)}) %collective-permute-start.25) | collective-permute-done | bytes 65568 | tf_op jit(solution)/shard_map/ppermute | solution.py:250
  (78 shorter events, 19.9 us)
Async XLA Ops:
  0.7 7.7 %collective-permute-start = (bf16[1,16,1024]{2,1,0:T(8,128)(2,1)}, bf16[1,16,1024]{2,1,0:T(8,128)(2,1)S(1)}, u32[]{:S(2)}, u32[]{:S(2)}) collective-permute-start(bf16[1,16,1024]{2,1,0:T(8,128)(2,1)} %bitcast.35), channel_id=1, source_target_pairs={{0,8},{1,9},{2,10},{3,11},{4,12},{5,13},{6,14},{7,15},{8,0},{9,1},... | collective-permute-start | bytes 98312 | tf_op jit(solution)/shard_map/ppermute | solution.py:250
  6.8 17.9 %collective-permute-start.3 = (bf16[512,512]{1,0:T(8,128)(2,1)}, bf16[512,512]{1,0:T(8,128)(2,1)S(1)}, u32[]{:S(2)}, u32[]{:S(2)}) collective-permute-start(bf16[512,512]{1,0:T(8,128)(2,1)} %get-tuple-element.42), channel_id=1, source_target_pairs={{0,2},{1,3},{2,0},{3,1},{4,6},{5,7},{6,4},{7,5},{8,10},{9,11},{10,... | collective-permute-start | bytes 1572872 | tf_op jit(solution)/shard_map/ppermute | solution.py:250
  8.4 4.3 %collective-permute-start.1 = (bf16[2,16,1024]{2,1,0:T(8,128)(2,1)S(1)}, bf16[2,16,1024]{2,1,0:T(8,128)(2,1)S(1)}, u32[]{:S(2)}, u32[]{:S(2)}) collective-permute-start(bf16[2,16,1024]{2,1,0:T(8,128)(2,1)S(1)} %pad_maximum_fusion.2), channel_id=1, source_target_pairs={{0,4},{1,5},{2,6},{3,7},{4,0},{5,1},{6,2},{7,3},{8,12},{9,13},{10,... | collective-permute-start | bytes 196616 | tf_op jit(solution)/shard_map/ppermute | solution.py:250
  10.1 26.6 %collective-permute-start.9 = (bf16[1024,512]{1,0:T(8,128)(2,1)S(1)}, bf16[1024,512]{1,0:T(8,128)(2,1)S(1)}, u32[]{:S(2)}, u32[]{:S(2)}) collective-permute-start(bf16[1024,512]{1,0:T(8,128)(2,1)S(1)} %copy-done), channel_id=1, source_target_pairs={{0,1},{1,0},{2,3},{3,2},{4,5},{5,4},{6,7},{7,6},{8,9},{9,8},{10,11... | collective-permute-start | bytes 3145736 | tf_op jit(solution)/shard_map/ppermute | solution.py:250
  10.1 15.8 %collective-permute-start.5 = (bf16[1,272,512]{2,1,0:T(8,128)(2,1)S(1)}, bf16[1,272,512]{2,1,0:T(8,128)(2,1)S(1)}, u32[]{:S(2)}, u32[]{:S(2)}) collective-permute-start(bf16[1,272,512]{2,1,0:T(8,128)(2,1)S(1)} %maximum_bitcast_fusion), channel_id=1, source_target_pairs={{0,8},{1,9},{2,10},{3,11},{4,12},{5,13},{6,14},{7,15},{8,0},{9,1},... | collective-permute-start | bytes 835592 | tf_op jit(solution)/shard_map/ppermute | solution.py:250
  12.8 11.9 %collective-permute-start.2 = (bf16[4,16,1024]{2,1,0:T(8,128)(2,1)S(1)}, bf16[4,16,1024]{2,1,0:T(8,128)(2,1)S(1)}, u32[]{:S(2)}, u32[]{:S(2)}) collective-permute-start(bf16[4,16,1024]{2,1,0:T(8,128)(2,1)S(1)} %pad_maximum_fusion.1.after_ref.beta_ref), channel_id=1, source_target_pairs={{0,2},{1,3},{2,0},{3,1},{4,6},{5,7},{6,4},{7,5},{8,10},{9,11},{10,... | collective-permute-start | bytes 393224 | tf_op jit(solution)/shard_map/ppermute | solution.py:250
  13.4 21.2 %collective-permute-start.4 = (bf16[512,512]{1,0:T(8,128)(2,1)S(1)}, bf16[512,512]{1,0:T(8,128)(2,1)S(1)}, u32[]{:S(2)}, u32[]{:S(2)}) collective-permute-start(bf16[512,512]{1,0:T(8,128)(2,1)S(1)} %get-tuple-element.26), channel_id=1, source_target_pairs={{0,2},{1,3},{2,0},{3,1},{4,6},{5,7},{6,4},{7,5},{8,10},{9,11},{10,... | collective-permute-start | bytes 1572872 | tf_op jit(solution)/shard_map/ppermute | solution.py:250
  25.9 14.7 %collective-permute-start.10 = (bf16[2,272,512]{2,1,0:T(8,128)(2,1)S(1)}, bf16[2,272,512]{2,1,0:T(8,128)(2,1)S(1)}, u32[]{:S(2)}, u32[]{:S(2)}) collective-permute-start(bf16[2,272,512]{2,1,0:T(8,128)(2,1)S(1)} %constant_dynamic-update-slice_fusion.after_ref.point_ref.refs_3_), channel_id=1, source_target_pairs={{0,4},{1,5},{2,6},{3,7},{4,0},{5,1},{6,2},{7,3},{8,12},{9,13},{10,... | collective-permute-start | bytes 1671176 | tf_op jit(solution)/shard_map/ppermute | solution.py:250
  34.6 6.0 %collective-permute-start.12 = (bf16[512,512]{1,0:T(8,128)(2,1)S(1)}, bf16[512,512]{1,0:T(8,128)(2,1)S(1)}, u32[]{:S(2)}, u32[]{:S(2)}) collective-permute-start(bf16[512,512]{1,0:T(8,128)(2,1)S(1)} %collective-permute-done.3.refs_0_), channel_id=1, source_target_pairs={{0,1},{1,0},{2,3},{3,2},{4,5},{5,4},{6,7},{7,6},{8,9},{9,8},{10,11... | collective-permute-start | bytes 1572872 | tf_op jit(solution)/shard_map/ppermute | solution.py:250
  34.9 5.7 %collective-permute-start.13 = (bf16[512,512]{1,0:T(8,128)(2,1)S(1)}, bf16[512,512]{1,0:T(8,128)(2,1)S(1)}, u32[]{:S(2)}, u32[]{:S(2)}) collective-permute-start(bf16[512,512]{1,0:T(8,128)(2,1)S(1)} %collective-permute-done.4.refs_1_), channel_id=1, source_target_pairs={{0,1},{1,0},{2,3},{3,2},{4,5},{5,4},{6,7},{7,6},{8,9},{9,8},{10,11... | collective-permute-start | bytes 1572872 | tf_op jit(solution)/shard_map/ppermute | solution.py:250
  35.2 3.9 %collective-permute-start.8 = (bf16[16,1024]{1,0:T(8,128)(2,1)S(1)}, bf16[16,1024]{1,0:T(8,128)(2,1)S(1)}, u32[]{:S(2)}, u32[]{:S(2)}) collective-permute-start(bf16[16,1024]{1,0:T(8,128)(2,1)S(1)} %get-tuple-element.32.refs_2_.refs_0_), channel_id=1, source_target_pairs={{0,2},{1,3},{2,0},{3,1},{4,6},{5,7},{6,4},{7,5},{8,10},{9,11},{10,... | collective-permute-start | bytes 98312 | tf_op jit(solution)/shard_map/ppermute | solution.py:250
  36.7 7.9 %collective-permute-start.7 = (bf16[16,1024]{1,0:T(8,128)(2,1)S(1)}, bf16[16,1024]{1,0:T(8,128)(2,1)S(1)}, u32[]{:S(2)}, u32[]{:S(2)}) collective-permute-start(bf16[16,1024]{1,0:T(8,128)(2,1)S(1)} %get-tuple-element.32.refs_2_.refs_0_), channel_id=1, source_target_pairs={{0,1},{1,0},{2,3},{3,2},{4,5},{5,4},{6,7},{7,6},{8,9},{9,8},{10,11... | collective-permute-start | bytes 98312 | tf_op jit(solution)/shard_map/ppermute | solution.py:250
  40.6 4.0 %collective-permute-start.11 = (bf16[16,1024]{1,0:T(8,128)(2,1)S(1)}, bf16[16,1024]{1,0:T(8,128)(2,1)S(1)}, u32[]{:S(2)}, u32[]{:S(2)}) collective-permute-start(bf16[16,1024]{1,0:T(8,128)(2,1)S(1)} %collective-permute-done.8.refs_2_), channel_id=1, source_target_pairs={{0,1},{1,0},{2,3},{3,2},{4,5},{5,4},{6,7},{7,6},{8,9},{9,8},{10,11... | collective-permute-start | bytes 98312 | tf_op jit(solution)/shard_map/ppermute | solution.py:250
  46.0 4.5 %collective-permute-start.14 = (f32[16,1024]{1,0:T(8,128)S(1)}, f32[16,1024]{1,0:T(8,128)S(1)}, u32[]{:S(2)}, u32[]{:S(2)}) collective-permute-start(f32[16,1024]{1,0:T(8,128)S(1)} %partial_logits.1), channel_id=1, source_target_pairs={{0,4},{1,5},{2,6},{3,7},{4,0},{5,1},{6,2},{7,3},{8,12},{9,13},{10,... | collective-permute-start | bytes 196616 | tf_op jit(solution)/shard_map/ppermute | solution.py:250
  50.5 6.1 %collective-permute-start.15 = (f32[16,1024]{1,0:T(8,128)S(1)}, f32[16,1024]{1,0:T(8,128)S(1)}, u32[]{:S(2)}, u32[]{:S(2)}) collective-permute-start(f32[16,1024]{1,0:T(8,128)S(1)} %maximum_add_fusion.refs_0_), channel_id=1, source_target_pairs={{0,8},{1,9},{2,10},{3,11},{4,12},{5,13},{6,14},{7,15},{8,0},{9,1},... | collective-permute-start | bytes 196616 | tf_op jit(solution)/shard_map/ppermute | solution.py:250
  59.3 4.4 %collective-permute-start.17 = (f32[16,1024]{1,0:T(8,128)S(1)}, f32[16,1024]{1,0:T(8,128)S(1)}, u32[]{:S(2)}, u32[]{:S(2)}) collective-permute-start(f32[16,1024]{1,0:T(8,128)S(1)} %fusion.4), channel_id=1, source_target_pairs={{0,2},{1,3},{2,0},{3,1},{4,6},{5,7},{6,4},{7,5},{8,10},{9,11},{10,... | collective-permute-start | bytes 196616 | tf_op jit(solution)/shard_map/ppermute | solution.py:250
  67.7 2.3 %collective-permute-start.19 = (f32[2,16,1024]{2,1,0:T(8,128)S(1)}, f32[2,16,1024]{2,1,0:T(8,128)S(1)}, u32[]{:S(2)}, u32[]{:S(2)}) collective-permute-start(f32[2,16,1024]{2,1,0:T(8,128)S(1)} %gradient_terms.12.after_ref), channel_id=1, source_target_pairs={{0,1},{1,0},{2,3},{3,2},{4,5},{5,4},{6,7},{7,6},{8,9},{9,8},{10,11... | collective-permute-start | bytes 393224 | tf_op jit(solution)/shard_map/ppermute | solution.py:250
  67.9 3.8 %collective-permute-start.22 = (f32[2,16,1024]{2,1,0:T(8,128)S(1)}, f32[2,16,1024]{2,1,0:T(8,128)S(1)}, u32[]{:S(2)}, u32[]{:S(2)}) collective-permute-start(f32[2,16,1024]{2,1,0:T(8,128)S(1)} %gradient_terms.10.after_ref), channel_id=1, source_target_pairs={{0,1},{1,0},{2,3},{3,2},{4,5},{5,4},{6,7},{7,6},{8,9},{9,8},{10,11... | collective-permute-start | bytes 393224 | tf_op jit(solution)/shard_map/ppermute | solution.py:250
  68.3 6.3 %collective-permute-start.23 = (f32[2,16,1024]{2,1,0:T(8,128)S(1)}, f32[2,16,1024]{2,1,0:T(8,128)S(1)}, u32[]{:S(2)}, u32[]{:S(2)}) collective-permute-start(f32[2,16,1024]{2,1,0:T(8,128)S(1)} %add.51.after_ref), channel_id=1, source_target_pairs={{0,2},{1,3},{2,0},{3,1},{4,6},{5,7},{6,4},{7,5},{8,10},{9,11},{10,... | collective-permute-start | bytes 393224 | tf_op jit(solution)/shard_map/ppermute | solution.py:250
  70.1 6.7 %collective-permute-start.21 = (f32[2,16,1024]{2,1,0:T(8,128)S(1)}, f32[2,16,1024]{2,1,0:T(8,128)S(1)}, u32[]{:S(2)}, u32[]{:S(2)}) collective-permute-start(f32[2,16,1024]{2,1,0:T(8,128)S(1)} %add.52.after_ref), channel_id=1, source_target_pairs={{0,2},{1,3},{2,0},{3,1},{4,6},{5,7},{6,4},{7,5},{8,10},{9,11},{10,... | collective-permute-start | bytes 393224 | tf_op jit(solution)/shard_map/ppermute | solution.py:250
  71.7 5.1 %collective-permute-start.20 = (f32[2,16,1024]{2,1,0:T(8,128)S(1)}, f32[2,16,1024]{2,1,0:T(8,128)S(1)}, u32[]{:S(2)}, u32[]{:S(2)}) collective-permute-start(f32[2,16,1024]{2,1,0:T(8,128)S(1)} %gradient_terms.14.after_ref), channel_id=1, source_target_pairs={{0,1},{1,0},{2,3},{3,2},{4,5},{5,4},{6,7},{7,6},{8,9},{9,8},{10,11... | collective-permute-start | bytes 393224 | tf_op jit(solution)/shard_map/ppermute | solution.py:250
  74.7 6.3 %collective-permute-start.24 = (f32[16,1024]{1,0:T(8,128)S(1)}, f32[16,1024]{1,0:T(8,128)S(1)}, u32[]{:S(2)}, u32[]{:S(2)}) collective-permute-start(f32[16,1024]{1,0:T(8,128)S(1)} %get-tuple-element.44), channel_id=1, source_target_pairs={{0,12},{1,13},{2,14},{3,15},{4,8},{5,9},{6,10},{7,11},{8,4},{9,5},... | collective-permute-start | bytes 196616 | tf_op jit(solution)/shard_map/ppermute | solution.py:250
  75.8 6.8 %collective-permute-start.25 = (f32[16,1024]{1,0:T(8,128)S(1)}, f32[16,1024]{1,0:T(8,128)S(1)}, u32[]{:S(2)}, u32[]{:S(2)}) collective-permute-start(f32[16,1024]{1,0:T(8,128)S(1)} %get-tuple-element.45), channel_id=1, source_target_pairs={{0,8},{1,9},{2,10},{3,11},{4,12},{5,13},{6,14},{7,15},{8,0},{9,1},... | collective-permute-start | bytes 196616 | tf_op jit(solution)/shard_map/ppermute | solution.py:250
  76.9 6.0 %collective-permute-start.26 = (f32[16,1024]{1,0:T(8,128)S(1)}, f32[16,1024]{1,0:T(8,128)S(1)}, u32[]{:S(2)}, u32[]{:S(2)}) collective-permute-start(f32[16,1024]{1,0:T(8,128)S(1)} %slice_bitcast_fusion), channel_id=1, source_target_pairs={{0,4},{1,5},{2,6},{3,7},{4,0},{5,1},{6,2},{7,3},{8,12},{9,13},{10,... | collective-permute-start | bytes 196616 | tf_op jit(solution)/shard_map/ppermute | solution.py:250
  (8 other events, 49.2 us)

commit v4 on v3

--- a/solution.py
+++ b/solution.py
@@ -16,6 +16,10 @@
 
 def params(mib):
     return pltpu.CompilerParams(vmem_limit_bytes=mib * MIB)
+
+
+def in_hbm(array):
+    return pltpu.with_memory_space_constraint(array, pltpu.HBM)
 
 
 def in_vmem():
@@ -89,13 +93,53 @@
     )(*operands)
 
 
-def gradient_terms(grad, blocks, first, count, step, after):
+def prepare(points, labels, centres, beta):
+    half = centres.shape[0] // 2
+    block, features = points.shape
+    classes = beta.shape[0]
+
+    def body(points_ref, labels_ref, centres_ref, beta_ref, ext_ref, first_ref, second_ref, held_ref, row_ref, sems):
+        moves = (
+            (labels_ref, row_ref),
+            (centres_ref.at[pl.ds(0, half)], first_ref),
+            (points_ref, ext_ref.at[0, pl.ds(0, block)]),
+            (beta_ref, held_ref.at[0]),
+            (centres_ref.at[pl.ds(half, half)], second_ref),
+        )
+        copies = [pltpu.make_async_copy(source, target, sems.at[at]) for at, (source, target) in enumerate(moves)]
+        for copy in copies:
+            copy.start()
+        class_column = lax.broadcasted_iota(jnp.int32, (classes, block), 0)
+        ext_ref[0, block:, :] = jnp.zeros((classes, features), BF16)
+        copies[0].wait()
+        ext_ref[0, block:, :block] = jnp.where(row_ref[...] == class_column, 1.0, 0.0).astype(BF16)
+        for copy in copies[1:]:
+            copy.wait()
+
+    return pl.pallas_call(
+        body,
+        out_shape=[
+            pltpu.VMEM((1, block + classes, features), BF16),
+            pltpu.VMEM((half, features), BF16),
+            pltpu.VMEM((half, features), BF16),
+            pltpu.VMEM((1, *beta.shape), BF16),
+        ],
+        in_specs=[anywhere()] * 4,
+        out_specs=[in_vmem()] * 4,
+        scratch_shapes=[pltpu.VMEM((1, block), jnp.int32), pltpu.SemaphoreType.DMA((5,))],
+        compiler_params=params(8),
+        cost_estimate=cost(1024, 4 * centres.size),
+        name="prepare",
+    )(in_hbm(points), in_hbm(labels[None, :]), in_hbm(centres), in_hbm(beta))
+
+
+def gradient_terms(grad, blocks, first, count, after):
     classes, rows = grad.shape
     width = blocks.shape[2]
 
     def body(after_ref, grad_ref, block_ref, out_ref):
         for at in range(count):
-            out_ref[at] = jnp.dot(grad_ref[...], block_ref[first + step * at], preferred_element_type=F32)
+            out_ref[at] = jnp.dot(grad_ref[...], block_ref[first + at], preferred_element_type=F32)
 
     return pl.pallas_call(
         body,
@@ -136,7 +180,7 @@
         in_specs=[in_vmem()] * (1 + len(pieces)) + [anywhere()],
         out_specs=in_vmem(),
         compiler_params=params(8),
-        cost_estimate=cost(2 * total * len(centre_blocks) * local * features, 1024),
+        cost_estimate=cost(1024, 1024),
         name="kernel_tile",
     )(points, *pieces, after)
 
@@ -172,16 +216,19 @@
     )(*alphas, *flat)
 
 
-def residual(logit_sum, received, order, bias, points):
+def residual(logit_sum, received, orders, bias, points):
     classes, total = logit_sum.shape
-    block = total // len(order)
+    block = total // len(orders[0])
     blocks = [(which, at) for which, array in enumerate(points) for at in range(array.shape[0])]
 
-    def compute(sum_ref, received_ref, bias_ref, point_refs, logits_ref, resid_ref):
-        for at, source in enumerate(order):
+    def compute(sum_ref, bias_ref, received_refs, point_refs, logits_ref, resid_ref):
+        for at in range(len(blocks)):
             here = slice(at * block, (at + 1) * block)
-            there = slice(source * block, (source + 1) * block)
-            logits = sum_ref[:, here] + received_ref[:, there] + bias_ref[:, :1]
+            logits = sum_ref[:, here]
+            for received_ref, order in zip(received_refs, orders):
+                there = slice(order[at] * block, (order[at] + 1) * block)
+                logits = logits + received_ref[:, there].astype(F32)
+            logits = logits + bias_ref[:, :1]
             if at == 0:
                 logits_ref[...] = logits
             which, row = blocks[at]
@@ -202,7 +249,8 @@
         operands = [resid]
     else:
         compute, (logit_sum, received, bias, points) = residual_of
-        operands = [logit_sum, received, bias, *points]
+        operands = [logit_sum, bias, *received, *points]
+        n_first = 2 + len(received)
         block = points[0].shape[1] - logit_sum.shape[0]
         out_shape = [jax.ShapeDtypeStruct((logit_sum.shape[0], block), F32)]
         out_shape.append(jax.ShapeDtypeStruct(logit_sum.shape, BF16))
@@ -215,7 +263,7 @@
         resid_ref = refs[0]
         if residual_of is not None:
             logits_ref, resid_ref = more_refs
-            compute(*refs[:3], refs[3:n_operands], logits_ref, resid_ref)
+            compute(*refs[:2], refs[2:n_first], refs[n_first:n_operands], logits_ref, resid_ref)
         for which in range(n_parts):
             acc = None
             for part, size in enumerate(sizes):
@@ -249,21 +297,18 @@
     def swap(array, mask):
         return lax.ppermute(array, "pts", [(index, index ^ mask) for index in range(devices)])
 
-    tri_inverse = pltpu.with_memory_space_constraint(tri_inverse, pltpu.HBM)
+    tri_inverse = in_hbm(tri_inverse)
     me = lax.axis_index("pts").astype(jnp.int32).reshape(1)
     bias_column = jnp.broadcast_to(bias[:, None], (classes, 128))
-    class_column = jnp.arange(classes, dtype=jnp.int32)[:, None]
-    onehot = (labels[None, :] == class_column).astype(BF16)
-
-    block, features = points.shape
-    points = jnp.concatenate([points, jnp.pad(onehot, ((0, 0), (0, features - block)))])[None]
-    half = local_centres * 1//2
-    centre_halves = [centres[:half], centres[half:]]
+
+    block = points.shape[0]
+    coeffs = beta.T
+    crossed = swap(coeffs[None], outer[-1])
+    points, *centre_halves, coeffs = prepare(points, labels, centres, coeffs)
     centres_2 = [swap(centre_halves[0], 2)]
-    coeffs = beta.T[None]
     far = [0]
     for mask in reversed(outer):
-        coeffs = jnp.concatenate([coeffs, swap(coeffs, mask)])
+        coeffs = jnp.concatenate([coeffs, crossed if mask == outer[-1] else swap(coeffs, mask)])
         far = far + [offset ^ mask for offset in far]
         if mask != outer[0]:
             points, coeffs = lax.optimization_barrier((points, coeffs))
@@ -283,24 +328,21 @@
     alpha_2 = swap(alpha, 2)
     near_centres = [[centres], [swap(centres, 1)]]
     tile_00 = kernel_tile(block, points[0], near_centres, alpha)
-    alpha_2, tile_00, points[1] = lax.optimization_barrier((alpha_2, tile_00, points[1]))
     alpha_1 = swap(alpha, 1)
-    alpha_3 = swap(alpha_2, 1)
     *centres_2, alpha = lax.optimization_barrier((*centres_2, alpha))
     far_centres = [centres_2, [swap(piece, 1) for piece in centres_2]]
     tile_01 = kernel_tile(block, points[0], far_centres, tile_00)
+    alpha_2, tile_01, points[1] = lax.optimization_barrier((alpha_2, tile_01, points[1]))
+    alpha_3 = swap(alpha_2, 1)
     tile_10 = kernel_tile(block, points[1], near_centres, tile_01)
     tile_11 = kernel_tile(block, points[1], far_centres, tile_10)
     tiles = [[tile_00, tile_01], [tile_10, tile_11]]
     logit_sum = partial_logits(tiles, (alpha, alpha_1, alpha_2, alpha_3))
 
-    for mask in outer:
-        received = swap(logit_sum, mask)
-        order = [far.index(offset ^ mask) for offset in far]
-        if mask != outer[-1]:
-            moved = [received[:, source * block : (source + 1) * block] for source in order]
-            logit_sum = logit_sum + jnp.concatenate(moved, axis=1)
-    compute = residual(logit_sum, received, order, bias_column, points)
+    rounded = logit_sum.astype(BF16)
+    received = [swap(rounded, offset) for offset in far[1:]]
+    orders = [[far.index(held ^ offset) for held in far] for offset in far[1:]]
+    compute = residual(logit_sum, received, orders, bias_column, points)
     send, logits, resid = kernel_gradient(1, None, tiles, (compute, (logit_sum, received, bias_column, points)))
     received = swap(send, 1)
     (keep,) = kernel_gradient(0, resid, tiles)
@@ -308,31 +350,18 @@
     received_2 = swap(keep[1] + received[1], 2)
     grad = ((keep[0] + received[0] + received_2) * (1.0 / math.sqrt(total_points))).astype(BF16)
 
-    half = count // 2
-    position = {offset: at for at, offset in enumerate(far)}
-    near_first = sorted(far, key=lambda offset: (offset & outer[-1], position[offset]))
-    latest = grad
-    sums = {}
-    for offsets in (near_first[half:], near_first[:half]):
-        at = position[offsets[0]]
-        step = position[offsets[1]] - at if half > 1 else 1
-        parts = []
-        for held, first in ((tri_13, count), (tri_02, count), (tri_13, 0), (tri_02, 0)):
-            parts.append((held, first + at))
-        term_3 = gradient_terms(grad, *parts[0], half, step, latest)
-        received_3 = swap(term_3, 1)
-        term_2 = gradient_terms(grad, *parts[1], half, step, term_3)
-        ahead = term_2 + received_3
-        received_2 = swap(ahead, 2)
-        term_1 = gradient_terms(grad, *parts[2], half, step, ahead)
-        received_1 = swap(term_1, 1)
-        latest = gradient_terms(grad, *parts[3], half, step, term_1)
-        total = latest + received_1 + received_2
-        for index, offset in enumerate(offsets):
-            sums[offset] = total[index]
-    gradient = sums[0]
-    for offset in reversed(near_first[1:]):
-        gradient = gradient + swap(sums[offset], offset)
+    term_3 = gradient_terms(grad, tri_13, count, count, grad)
+    received_3 = swap(term_3, 1)
+    term_1 = gradient_terms(grad, tri_13, 0, count, term_3)
+    received_1 = swap(term_1, 1)
+    term_2 = gradient_terms(grad, tri_02, count, count, term_1)
+    ahead = (term_2 + received_3).astype(BF16)
+    received_2 = swap(ahead, 2)
+    term_0 = gradient_terms(grad, tri_02, 0, count, ahead)
+    total = term_0 + received_1 + received_2.astype(F32)
+    gradient = total[0]
+    for at, offset in reversed(list(enumerate(far))[1:]):
+        gradient = gradient + swap(total[at].astype(BF16), offset).astype(F32)
     return (gradient.T, logits.T)
 
 

time: 83.7 us -> 76.2 us (0.910)
  waiting for transfers between devices: 27.6 us -> 17.8 us
  starting transfers between devices: 23.1 us -> 26.9 us
  local copies, waits for them, and re-layouts: 2.21 us -> 0.13 us
    ppermute x27 -> x25, waiting for transfers between devices: 27.6 us -> 17.8 us  [swap(): lax.ppermute(array, 'pts', [(index, index ^ mask) for index in range(devi...]
    ppermute x27 -> x25, starting transfers between devices: 23.1 us -> 26.9 us  [swap(): lax.ppermute(array, 'pts', [(index, index ^ mask) for index in range(devi...]
    slice x2 -> x0, local copies, waits for them, and re-layouts: 2.06 us -> none  [the longest x1 2.06 us: on_device(): centre_halves = [centres[:half], centres[half:]]]
    pallas_call x0 -> x1, Pallas kernels: none -> 1.35 us  [prepare(): pl.pallas_call(body, out_shape=[pltpu.VMEM((1, block + classes, features)...]
    pallas_call x8 -> x4, Pallas kernels: 5.23 us -> 4.79 us  [gradient_terms(): pl.pallas_call(body, out_shape=jax.ShapeDtypeStruct((count, classes, widt...]
  transfers between devices with their start and end apart: 27 -> 25, of which waited for: 14 -> 13; matrix products, arithmetic and copies ran while one was open for 3% -> 0% of each run, Pallas kernels for 28% -> 34%
where the time goes in v4:
time: 76.2 us; the launch traced here: 76 us
  Pallas kernels  29.6 us (39%)
  starting transfers between devices  26.9 us (35%)
  waiting for transfers between devices  17.8 us (23%)
  other arithmetic  0.82 us (1%)
  between operations  0.82 us (1%)
    ppermute x25, starting transfers between devices, swap(): lax.ppermute(array, 'pts', [(index, index ^ mask) for index in range(devi...  26.9 us
    ppermute x25, waiting for transfers between devices, swap(): lax.ppermute(array, 'pts', [(index, index ^ mask) for index in range(devi...  17.8 us
    pallas_call x2, Pallas kernels, alpha_sum(): pl.pallas_call(body, out_shape=[jax.ShapeDtypeStruct((classes, rows), BF1...  14.5 us
    pallas_call x4, Pallas kernels, kernel_tile(): pl.pallas_call(body, out_shape=pltpu.VMEM((len(centre_blocks), local, tot...  5.28 us
    pallas_call x4, Pallas kernels, gradient_terms(): pl.pallas_call(body, out_shape=jax.ShapeDtypeStruct((count, classes, widt...  4.79 us
    pallas_call x2, Pallas kernels, kernel_gradient(): pl.pallas_call(body, out_shape=[jax.ShapeDtypeStruct((n_parts, classes, l...  2.41 us
  transfers between devices with their start and end apart: 25, of which 13 were waited for; matrix products, arithmetic and copies ran while one was open for 0% of the time, Pallas kernels for 34%

profile of v4, /device:TPU:0, one launch (start us, length us, event | category | flops | bytes accessed | tf_op | source)
XLA Modules:
  0.0 76.0 jit_solution(14923378633306210390)
XLA Ops:
  0.6 4.1 %collective-permute-start = (bf16[1,16,1024]{2,1,0:T(8,128)(2,1)}, bf16[1,16,1024]{2,1,0:T(8,128)(2,1)S(1)}, u32[]{:S(2)}, u32[]{:S(2)}) collective-permute-start(bf16[1,16,1024]{2,1,0:T(8,128)(2,1)} %bitcast.34), channel_id=1, source_target_pairs={{0,8},{1,9},{2,10},{3,11},{4,12},{5,13},{6,14},{7,15},{8,0},{9,1},... | collective-permute-start | bytes 98312 | tf_op jit(solution)/shard_map/ppermute | solution.py:298
  4.7 1.4 %prepare.1 = (bf16[1,272,512]{2,1,0:T(8,128)(2,1)S(1)}, bf16[512,512]{1,0:T(8,128)(2,1)S(1)}, bf16[512,512]{1,0:T(8,128)(2,1)S(1)}, bf16[1,16,1024]{2,1,0:T(8,128)(2,1)S(1)}) custom-call(bf16[256,512]{1,0:T(8,128)(2,1)} %points_ref.1, s32[1,256]{1,0:T(1,128)} %bitcast.36, bf16[1024,512]{1,0:T(8,128)(2,1)} %refs_0_.3, bf16[16,1024]{1,0:T(8,128)(2,1)} %bitcast.35), custom_call_target="tpu_custom_call" | custom-call | flops 1024 | bytes 2097152 | tf_op jit(solution)/shard_map/prepare/pallas_call | solution.py:119
  6.1 1.6 %collective-permute-start.3 = (bf16[512,512]{1,0:T(8,128)(2,1)S(1)}, bf16[512,512]{1,0:T(8,128)(2,1)S(1)}, u32[]{:S(2)}, u32[]{:S(2)}) collective-permute-start(bf16[512,512]{1,0:T(8,128)(2,1)S(1)} %get-tuple-element.32), channel_id=1, source_target_pairs={{0,2},{1,3},{2,0},{3,1},{4,6},{5,7},{6,4},{7,5},{8,10},{9,11},{10,... | collective-permute-start | bytes 1572872 | tf_op jit(solution)/shard_map/ppermute | solution.py:298
  7.7 1.6 %collective-permute-start.1 = (bf16[2,16,1024]{2,1,0:T(8,128)(2,1)S(1)}, bf16[2,16,1024]{2,1,0:T(8,128)(2,1)S(1)}, u32[]{:S(2)}, u32[]{:S(2)}) collective-permute-start(bf16[2,16,1024]{2,1,0:T(8,128)(2,1)S(1)} %pad_maximum_fusion.2), channel_id=1, source_target_pairs={{0,4},{1,5},{2,6},{3,7},{4,0},{5,1},{6,2},{7,3},{8,12},{9,13},{10,... | collective-permute-start | bytes 196616 | tf_op jit(solution)/shard_map/ppermute | solution.py:298
  9.3 2.3 %collective-permute-start.5 = (bf16[1,272,512]{2,1,0:T(8,128)(2,1)S(1)}, bf16[1,272,512]{2,1,0:T(8,128)(2,1)S(1)}, u32[]{:S(2)}, u32[]{:S(2)}) collective-permute-start(bf16[1,272,512]{2,1,0:T(8,128)(2,1)S(1)} %get-tuple-element.35), channel_id=1, source_target_pairs={{0,8},{1,9},{2,10},{3,11},{4,12},{5,13},{6,14},{7,15},{8,0},{9,1},... | collective-permute-start | bytes 835592 | tf_op jit(solution)/shard_map/ppermute | solution.py:298
  12.0 1.3 %collective-permute-start.2 = (bf16[4,16,1024]{2,1,0:T(8,128)(2,1)S(1)}, bf16[4,16,1024]{2,1,0:T(8,128)(2,1)S(1)}, u32[]{:S(2)}, u32[]{:S(2)}) collective-permute-start(bf16[4,16,1024]{2,1,0:T(8,128)(2,1)S(1)} %pad_maximum_fusion.1.after_ref.beta_ref), channel_id=1, source_target_pairs={{0,2},{1,3},{2,0},{3,1},{4,6},{5,7},{6,4},{7,5},{8,10},{9,11},{10,... | collective-permute-start | bytes 393224 | tf_op jit(solution)/shard_map/ppermute | solution.py:298
  14.1 6.5 %alpha_sum.2 = (f32[16,1024]{1,0:T(8,128)S(1)}, bf16[8,1024,1024]{2,1,0:T(8,128)(2,1)S(1)}) custom-call(s32[1]{0:T(128)} %bitcast.3.me_ref, bf16[1024,16384]{1,0:T(8,128)(2,1)} %tri_ref.3, bf16[4,16,1024]{2,1,0:T(8,128)(2,1)S(1)} %pad_maximum_fusion.1.after_ref.beta_ref, bf16[4,16,1024]{2,1,0:T(8,128)(2,1)S(1)} %pad_maximum_fusion.1.after_ref.beta_ref), custom_call_target="tpu_custom_call" | custom-call | flops 2147483648 | bytes 16777216 | tf_op jit(solution)/shard_map/alpha_sum/pallas_call | solution.py:81
  20.6 3.2 %collective-permute-done.2.refs_2_ = bf16[4,16,1024]{2,1,0:T(8,128)(2,1)S(1)} collective-permute-done((bf16[4,16,1024]{2,1,0:T(8,128)(2,1)S(1)}, bf16[4,16,1024]{2,1,0:T(8,128)(2,1)S(1)}, u32[]{:S(2)}, u32[]{:S(2)}) %collective-permute-start.2) | collective-permute-done | bytes 131104 | tf_op jit(solution)/shard_map/ppermute | solution.py:298
  25.6 8.1 %alpha_sum.3 = (bf16[16,1024]{1,0:T(8,128)(2,1)S(1)}, bf16[8,1024,1024]{2,1,0:T(8,128)(2,1)S(1)}) custom-call(s32[1]{0:T(128)} %bitcast.3.me_ref, bf16[1024,16384]{1,0:T(8,128)(2,1)} %tri_ref.3, bf16[2,272,512]{2,1,0:T(8,128)(2,1)S(1)} %constant_dynamic-update-slice_fusion.after_ref.point_ref.refs_5_, ...), custom_call_target="tpu_custom_call" | custom-call | flops 2147483648 | bytes 16777216 | tf_op jit(solution)/shard_map/alpha_sum/pallas_call | solution.py:81
  34.3 1.5 %collective-permute-start.8 = (bf16[16,1024]{1,0:T(8,128)(2,1)S(1)}, bf16[16,1024]{1,0:T(8,128)(2,1)S(1)}, u32[]{:S(2)}, u32[]{:S(2)}) collective-permute-start(bf16[16,1024]{1,0:T(8,128)(2,1)S(1)} %get-tuple-element.40.refs_2_.refs_0_), channel_id=1, source_target_pairs={{0,2},{1,3},{2,0},{3,1},{4,6},{5,7},{6,4},{7,5},{8,10},{9,11},{10,... | collective-permute-start | bytes 98312 | tf_op jit(solution)/shard_map/ppermute | solution.py:298
  35.8 1.3 %kernel_tile.4.refs_4_.refs_7_.refs_1_ = bf16[2,1024,512]{2,1,0:T(8,128)(2,1)S(1)} custom-call(bf16[2,272,512]{2,1,0:T(8,128)(2,1)S(1)} %constant_dynamic-update-slice_fusion.after_ref.point_ref.refs_5_, bf16[1024,512]{1,0:T(8,128)(2,1)S(1)} %copy-done, bf16[1024,512]{1,0:T(8,128)(2,1)S(1)} %collective-permute-done.11.refs_1_, ...), custom_call_target="tpu_custom_call" | custom-call | flops 1024 | bytes 1024 | tf_op jit(solution)/shard_map/kernel_tile/pallas_call | solution.py:177
  37.2 1.3 %kernel_tile.5.refs_2_.refs_5_.refs_8_ = bf16[2,1024,512]{2,1,0:T(8,128)(2,1)S(1)} custom-call(bf16[2,272,512]{2,1,0:T(8,128)(2,1)S(1)} %constant_dynamic-update-slice_fusion.after_ref.point_ref.refs_5_, bf16[512,512]{1,0:T(8,128)(2,1)S(1)} %collective-permute-done.3.refs_0_, bf16[512,512]{1,0:T(8,128)(2,1)S(1)} %collective-permute-done.4.refs_1_, ...), custom_call_target="tpu_custom_call" | custom-call | flops 1024 | bytes 1024 | tf_op jit(solution)/shard_map/kernel_tile/pallas_call | solution.py:177
  39.7 1.3 %kernel_tile.6.refs_4_.refs_6_.refs_9_.refs_3_ = bf16[2,1024,512]{2,1,0:T(8,128)(2,1)S(1)} custom-call(bf16[2,272,512]{2,1,0:T(8,128)(2,1)S(1)} %collective-permute-done.12.point_ref.refs_6_, bf16[1024,512]{1,0:T(8,128)(2,1)S(1)} %copy-done, bf16[1024,512]{1,0:T(8,128)(2,1)S(1)} %collective-permute-done.11.refs_1_, ...), custom_call_target="tpu_custom_call" | custom-call | flops 1024 | bytes 1024 | tf_op jit(solution)/shard_map/kernel_tile/pallas_call | solution.py:177
  41.0 1.3 %kernel_tile.7.refs_7_.refs_10_.refs_4_ = bf16[2,1024,512]{2,1,0:T(8,128)(2,1)S(1)} custom-call(bf16[2,272,512]{2,1,0:T(8,128)(2,1)S(1)} %collective-permute-done.12.point_ref.refs_6_, bf16[512,512]{1,0:T(8,128)(2,1)S(1)} %collective-permute-done.3.refs_0_, bf16[512,512]{1,0:T(8,128)(2,1)S(1)} %collective-permute-done.4.refs_1_, ...), custom_call_target="tpu_custom_call" | custom-call | flops 1024 | bytes 1024 | tf_op jit(solution)/shard_map/kernel_tile/pallas_call | solution.py:177
  43.6 1.7 %collective-permute-start.14 = (bf16[16,1024]{1,0:T(8,128)(2,1)S(1)}, bf16[16,1024]{1,0:T(8,128)(2,1)S(1)}, u32[]{:S(2)}, u32[]{:S(2)}) collective-permute-start(bf16[16,1024]{1,0:T(8,128)(2,1)S(1)} %convert_element_type.33), channel_id=1, source_target_pairs={{0,8},{1,9},{2,10},{3,11},{4,12},{5,13},{6,14},{7,15},{8,0},{9,1},... | collective-permute-start | bytes 98312 | tf_op jit(solution)/shard_map/ppermute | solution.py:298
  46.1 1.9 %collective-permute-start.16 = (bf16[16,1024]{1,0:T(8,128)(2,1)S(1)}, bf16[16,1024]{1,0:T(8,128)(2,1)S(1)}, u32[]{:S(2)}, u32[]{:S(2)}) collective-permute-start(bf16[16,1024]{1,0:T(8,128)(2,1)S(1)} %convert_element_type.33), channel_id=1, source_target_pairs={{0,12},{1,13},{2,14},{3,15},{4,8},{5,9},{6,10},{7,11},{8,4},{9,5},... | collective-permute-start | bytes 98312 | tf_op jit(solution)/shard_map/ppermute | solution.py:298
  49.4 2.4 %collective-permute-done.16.refs_4_ = bf16[16,1024]{1,0:T(8,128)(2,1)S(1)} collective-permute-done((bf16[16,1024]{1,0:T(8,128)(2,1)S(1)}, bf16[16,1024]{1,0:T(8,128)(2,1)S(1)}, u32[]{:S(2)}, u32[]{:S(2)}) %collective-permute-start.16) | collective-permute-done | bytes 32800 | tf_op jit(solution)/shard_map/ppermute | solution.py:298
  54.4 1.6 %collective-permute-start.18 = (f32[16,1024]{1,0:T(8,128)S(1)}, f32[16,1024]{1,0:T(8,128)S(1)}, u32[]{:S(2)}, u32[]{:S(2)}) collective-permute-start(f32[16,1024]{1,0:T(8,128)S(1)} %fusion.4), channel_id=1, source_target_pairs={{0,2},{1,3},{2,0},{3,1},{4,6},{5,7},{6,4},{7,5},{8,10},{9,11},{10,... | collective-permute-start | bytes 196616 | tf_op jit(solution)/shard_map/ppermute | solution.py:298
  56.0 2.8 %collective-permute-done.18 = f32[16,1024]{1,0:T(8,128)S(1)} collective-permute-done((f32[16,1024]{1,0:T(8,128)S(1)}, f32[16,1024]{1,0:T(8,128)S(1)}, u32[]{:S(2)}, u32[]{:S(2)}) %collective-permute-start.18) | collective-permute-done | bytes 65568 | tf_op jit(solution)/shard_map/ppermute | solution.py:298
  63.1 1.6 %collective-permute-start.21 = (bf16[4,16,1024]{2,1,0:T(8,128)(2,1)S(1)}, bf16[4,16,1024]{2,1,0:T(8,128)(2,1)S(1)}, u32[]{:S(2)}, u32[]{:S(2)}) collective-permute-start(bf16[4,16,1024]{2,1,0:T(8,128)(2,1)S(1)} %add_convert_fusion.after_ref), channel_id=1, source_target_pairs={{0,2},{1,3},{2,0},{3,1},{4,6},{5,7},{6,4},{7,5},{8,10},{9,11},{10,... | collective-permute-start | bytes 393224 | tf_op jit(solution)/shard_map/ppermute | solution.py:298
  65.8 2.7 %collective-permute-done.21 = bf16[4,16,1024]{2,1,0:T(8,128)(2,1)S(1)} collective-permute-done((bf16[4,16,1024]{2,1,0:T(8,128)(2,1)S(1)}, bf16[4,16,1024]{2,1,0:T(8,128)(2,1)S(1)}, u32[]{:S(2)}, u32[]{:S(2)}) %collective-permute-start.21) | collective-permute-done | bytes 131104 | tf_op jit(solution)/shard_map/ppermute | solution.py:298
  68.6 2.0 %collective-permute-start.22 = (bf16[16,1024]{1,0:T(8,128)(2,1)S(1)}, bf16[16,1024]{1,0:T(8,128)(2,1)S(1)}, u32[]{:S(2)}, u32[]{:S(2)}) collective-permute-start(bf16[16,1024]{1,0:T(8,128)(2,1)S(1)} %get-tuple-element.52), channel_id=1, source_target_pairs={{0,12},{1,13},{2,14},{3,15},{4,8},{5,9},{6,10},{7,11},{8,4},{9,5},... | collective-permute-start | bytes 98312 | tf_op jit(solution)/shard_map/ppermute | solution.py:298
  70.6 2.5 %collective-permute-start.24 = (bf16[16,1024]{1,0:T(8,128)(2,1)S(1)}, bf16[16,1024]{1,0:T(8,128)(2,1)S(1)}, u32[]{:S(2)}, u32[]{:S(2)}) collective-permute-start(bf16[16,1024]{1,0:T(8,128)(2,1)S(1)} %get-tuple-element.53), channel_id=1, source_target_pairs={{0,8},{1,9},{2,10},{3,11},{4,12},{5,13},{6,14},{7,15},{8,0},{9,1},... | collective-permute-start | bytes 98312 | tf_op jit(solution)/shard_map/ppermute | solution.py:298
  73.1 1.6 %collective-permute-done.22 = bf16[16,1024]{1,0:T(8,128)(2,1)S(1)} collective-permute-done((bf16[16,1024]{1,0:T(8,128)(2,1)S(1)}, bf16[16,1024]{1,0:T(8,128)(2,1)S(1)}, u32[]{:S(2)}, u32[]{:S(2)}) %collective-permute-start.22) | collective-permute-done | bytes 32800 | tf_op jit(solution)/shard_map/ppermute | solution.py:298
  (57 shorter events, 17.6 us)
Async XLA Ops:
  0.6 7.1 %collective-permute-start = (bf16[1,16,1024]{2,1,0:T(8,128)(2,1)}, bf16[1,16,1024]{2,1,0:T(8,128)(2,1)S(1)}, u32[]{:S(2)}, u32[]{:S(2)}) collective-permute-start(bf16[1,16,1024]{2,1,0:T(8,128)(2,1)} %bitcast.34), channel_id=1, source_target_pairs={{0,8},{1,9},{2,10},{3,11},{4,12},{5,13},{6,14},{7,15},{8,0},{9,1},... | collective-permute-start | bytes 98312 | tf_op jit(solution)/shard_map/ppermute | solution.py:298
  6.1 17.7 %collective-permute-start.3 = (bf16[512,512]{1,0:T(8,128)(2,1)S(1)}, bf16[512,512]{1,0:T(8,128)(2,1)S(1)}, u32[]{:S(2)}, u32[]{:S(2)}) collective-permute-start(bf16[512,512]{1,0:T(8,128)(2,1)S(1)} %get-tuple-element.32), channel_id=1, source_target_pairs={{0,2},{1,3},{2,0},{3,1},{4,6},{5,7},{6,4},{7,5},{8,10},{9,11},{10,... | collective-permute-start | bytes 1572872 | tf_op jit(solution)/shard_map/ppermute | solution.py:298
  7.7 4.3 %collective-permute-start.1 = (bf16[2,16,1024]{2,1,0:T(8,128)(2,1)S(1)}, bf16[2,16,1024]{2,1,0:T(8,128)(2,1)S(1)}, u32[]{:S(2)}, u32[]{:S(2)}) collective-permute-start(bf16[2,16,1024]{2,1,0:T(8,128)(2,1)S(1)} %pad_maximum_fusion.2), channel_id=1, source_target_pairs={{0,4},{1,5},{2,6},{3,7},{4,0},{5,1},{6,2},{7,3},{8,12},{9,13},{10,... | collective-permute-start | bytes 196616 | tf_op jit(solution)/shard_map/ppermute | solution.py:298
  9.3 26.5 %collective-permute-start.11 = (bf16[1024,512]{1,0:T(8,128)(2,1)}, bf16[1024,512]{1,0:T(8,128)(2,1)S(1)}, u32[]{:S(2)}, u32[]{:S(2)}) collective-permute-start(bf16[1024,512]{1,0:T(8,128)(2,1)} %refs_0_.3), channel_id=1, source_target_pairs={{0,1},{1,0},{2,3},{3,2},{4,5},{5,4},{6,7},{7,6},{8,9},{9,8},{10,11... | collective-permute-start | bytes 3145736 | tf_op jit(solution)/shard_map/ppermute | solution.py:298
  9.3 15.8 %collective-permute-start.5 = (bf16[1,272,512]{2,1,0:T(8,128)(2,1)S(1)}, bf16[1,272,512]{2,1,0:T(8,128)(2,1)S(1)}, u32[]{:S(2)}, u32[]{:S(2)}) collective-permute-start(bf16[1,272,512]{2,1,0:T(8,128)(2,1)S(1)} %get-tuple-element.35), channel_id=1, source_target_pairs={{0,8},{1,9},{2,10},{3,11},{4,12},{5,13},{6,14},{7,15},{8,0},{9,1},... | collective-permute-start | bytes 835592 | tf_op jit(solution)/shard_map/ppermute | solution.py:298
  12.0 11.8 %collective-permute-start.2 = (bf16[4,16,1024]{2,1,0:T(8,128)(2,1)S(1)}, bf16[4,16,1024]{2,1,0:T(8,128)(2,1)S(1)}, u32[]{:S(2)}, u32[]{:S(2)}) collective-permute-start(bf16[4,16,1024]{2,1,0:T(8,128)(2,1)S(1)} %pad_maximum_fusion.1.after_ref.beta_ref), channel_id=1, source_target_pairs={{0,2},{1,3},{2,0},{3,1},{4,6},{5,7},{6,4},{7,5},{8,10},{9,11},{10,... | collective-permute-start | bytes 393224 | tf_op jit(solution)/shard_map/ppermute | solution.py:298
  13.4 20.4 %collective-permute-start.4 = (bf16[512,512]{1,0:T(8,128)(2,1)S(1)}, bf16[512,512]{1,0:T(8,128)(2,1)S(1)}, u32[]{:S(2)}, u32[]{:S(2)}) collective-permute-start(bf16[512,512]{1,0:T(8,128)(2,1)S(1)} %get-tuple-element.34), channel_id=1, source_target_pairs={{0,2},{1,3},{2,0},{3,1},{4,6},{5,7},{6,4},{7,5},{8,10},{9,11},{10,... | collective-permute-start | bytes 1572872 | tf_op jit(solution)/shard_map/ppermute | solution.py:298
  23.8 1.8 %collective-permute-start.6 = (bf16[8,16,1024]{2,1,0:T(8,128)(2,1)S(1)}, bf16[8,16,1024]{2,1,0:T(8,128)(2,1)S(1)}, u32[]{:S(2)}, u32[]{:S(2)}) collective-permute-start(bf16[8,16,1024]{2,1,0:T(8,128)(2,1)S(1)} %pad_maximum_fusion), channel_id=1, source_target_pairs={{0,1},{1,0},{2,3},{3,2},{4,5},{5,4},{6,7},{7,6},{8,9},{9,8},{10,11... | collective-permute-start | bytes 786440 | tf_op jit(solution)/shard_map/ppermute | solution.py:298
  25.2 14.5 %collective-permute-start.12 = (bf16[2,272,512]{2,1,0:T(8,128)(2,1)S(1)}, bf16[2,272,512]{2,1,0:T(8,128)(2,1)S(1)}, u32[]{:S(2)}, u32[]{:S(2)}) collective-permute-start(bf16[2,272,512]{2,1,0:T(8,128)(2,1)S(1)} %constant_dynamic-update-slice_fusion.after_ref.point_ref.refs_5_), channel_id=1, source_target_pairs={{0,4},{1,5},{2,6},{3,7},{4,0},{5,1},{6,2},{7,3},{8,12},{9,13},{10,... | collective-permute-start | bytes 1671176 | tf_op jit(solution)/shard_map/ppermute | solution.py:298
  33.7 3.4 %collective-permute-start.10 = (bf16[512,512]{1,0:T(8,128)(2,1)S(1)}, bf16[512,512]{1,0:T(8,128)(2,1)S(1)}, u32[]{:S(2)}, u32[]{:S(2)}) collective-permute-start(bf16[512,512]{1,0:T(8,128)(2,1)S(1)} %collective-permute-done.4.refs_1_), channel_id=1, source_target_pairs={{0,1},{1,0},{2,3},{3,2},{4,5},{5,4},{6,7},{7,6},{8,9},{9,8},{10,11... | collective-permute-start | bytes 1572872 | tf_op jit(solution)/shard_map/ppermute | solution.py:298
  34.0 3.2 %collective-permute-start.9 = (bf16[512,512]{1,0:T(8,128)(2,1)S(1)}, bf16[512,512]{1,0:T(8,128)(2,1)S(1)}, u32[]{:S(2)}, u32[]{:S(2)}) collective-permute-start(bf16[512,512]{1,0:T(8,128)(2,1)S(1)} %collective-permute-done.3.refs_0_), channel_id=1, source_target_pairs={{0,1},{1,0},{2,3},{3,2},{4,5},{5,4},{6,7},{7,6},{8,9},{9,8},{10,11... | collective-permute-start | bytes 1572872 | tf_op jit(solution)/shard_map/ppermute | solution.py:298
  34.3 4.2 %collective-permute-start.8 = (bf16[16,1024]{1,0:T(8,128)(2,1)S(1)}, bf16[16,1024]{1,0:T(8,128)(2,1)S(1)}, u32[]{:S(2)}, u32[]{:S(2)}) collective-permute-start(bf16[16,1024]{1,0:T(8,128)(2,1)S(1)} %get-tuple-element.40.refs_2_.refs_0_), channel_id=1, source_target_pairs={{0,2},{1,3},{2,0},{3,1},{4,6},{5,7},{6,4},{7,5},{8,10},{9,11},{10,... | collective-permute-start | bytes 98312 | tf_op jit(solution)/shard_map/ppermute | solution.py:298
  35.8 6.5 %collective-permute-start.7 = (bf16[16,1024]{1,0:T(8,128)(2,1)S(1)}, bf16[16,1024]{1,0:T(8,128)(2,1)S(1)}, u32[]{:S(2)}, u32[]{:S(2)}) collective-permute-start(bf16[16,1024]{1,0:T(8,128)(2,1)S(1)} %get-tuple-element.40.refs_2_.refs_0_), channel_id=1, source_target_pairs={{0,1},{1,0},{2,3},{3,2},{4,5},{5,4},{6,7},{7,6},{8,9},{9,8},{10,11... | collective-permute-start | bytes 98312 | tf_op jit(solution)/shard_map/ppermute | solution.py:298
  39.7 2.7 %collective-permute-start.13 = (bf16[16,1024]{1,0:T(8,128)(2,1)S(1)}, bf16[16,1024]{1,0:T(8,128)(2,1)S(1)}, u32[]{:S(2)}, u32[]{:S(2)}) collective-permute-start(bf16[16,1024]{1,0:T(8,128)(2,1)S(1)} %collective-permute-done.8.refs_2_), channel_id=1, source_target_pairs={{0,1},{1,0},{2,3},{3,2},{4,5},{5,4},{6,7},{7,6},{8,9},{9,8},{10,11... | collective-permute-start | bytes 98312 | tf_op jit(solution)/shard_map/ppermute | solution.py:298
  43.6 5.7 %collective-permute-start.14 = (bf16[16,1024]{1,0:T(8,128)(2,1)S(1)}, bf16[16,1024]{1,0:T(8,128)(2,1)S(1)}, u32[]{:S(2)}, u32[]{:S(2)}) collective-permute-start(bf16[16,1024]{1,0:T(8,128)(2,1)S(1)} %convert_element_type.33), channel_id=1, source_target_pairs={{0,8},{1,9},{2,10},{3,11},{4,12},{5,13},{6,14},{7,15},{8,0},{9,1},... | collective-permute-start | bytes 98312 | tf_op jit(solution)/shard_map/ppermute | solution.py:298
  45.3 4.1 %collective-permute-start.15 = (bf16[16,1024]{1,0:T(8,128)(2,1)S(1)}, bf16[16,1024]{1,0:T(8,128)(2,1)S(1)}, u32[]{:S(2)}, u32[]{:S(2)}) collective-permute-start(bf16[16,1024]{1,0:T(8,128)(2,1)S(1)} %convert_element_type.33), channel_id=1, source_target_pairs={{0,4},{1,5},{2,6},{3,7},{4,0},{5,1},{6,2},{7,3},{8,12},{9,13},{10,... | collective-permute-start | bytes 98312 | tf_op jit(solution)/shard_map/ppermute | solution.py:298
  46.1 5.7 %collective-permute-start.16 = (bf16[16,1024]{1,0:T(8,128)(2,1)S(1)}, bf16[16,1024]{1,0:T(8,128)(2,1)S(1)}, u32[]{:S(2)}, u32[]{:S(2)}) collective-permute-start(bf16[16,1024]{1,0:T(8,128)(2,1)S(1)} %convert_element_type.33), channel_id=1, source_target_pairs={{0,12},{1,13},{2,14},{3,15},{4,8},{5,9},{6,10},{7,11},{8,4},{9,5},... | collective-permute-start | bytes 98312 | tf_op jit(solution)/shard_map/ppermute | solution.py:298
  54.4 4.4 %collective-permute-start.18 = (f32[16,1024]{1,0:T(8,128)S(1)}, f32[16,1024]{1,0:T(8,128)S(1)}, u32[]{:S(2)}, u32[]{:S(2)}) collective-permute-start(f32[16,1024]{1,0:T(8,128)S(1)} %fusion.4), channel_id=1, source_target_pairs={{0,2},{1,3},{2,0},{3,1},{4,6},{5,7},{6,4},{7,5},{8,10},{9,11},{10,... | collective-permute-start | bytes 196616 | tf_op jit(solution)/shard_map/ppermute | solution.py:298
  60.1 2.9 %collective-permute-start.19 = (f32[4,16,1024]{2,1,0:T(8,128)S(1)}, f32[4,16,1024]{2,1,0:T(8,128)S(1)}, u32[]{:S(2)}, u32[]{:S(2)}) collective-permute-start(f32[4,16,1024]{2,1,0:T(8,128)S(1)} %gradient_terms.4.after_ref), channel_id=1, source_target_pairs={{0,1},{1,0},{2,3},{3,2},{4,5},{5,4},{6,7},{7,6},{8,9},{9,8},{10,11... | collective-permute-start | bytes 786440 | tf_op jit(solution)/shard_map/ppermute | solution.py:298
  61.3 4.5 %collective-permute-start.20 = (f32[4,16,1024]{2,1,0:T(8,128)S(1)}, f32[4,16,1024]{2,1,0:T(8,128)S(1)}, u32[]{:S(2)}, u32[]{:S(2)}) collective-permute-start(f32[4,16,1024]{2,1,0:T(8,128)S(1)} %gradient_terms.5.after_ref), channel_id=1, source_target_pairs={{0,1},{1,0},{2,3},{3,2},{4,5},{5,4},{6,7},{7,6},{8,9},{9,8},{10,11... | collective-permute-start | bytes 786440 | tf_op jit(solution)/shard_map/ppermute | solution.py:298
  63.1 5.5 %collective-permute-start.21 = (bf16[4,16,1024]{2,1,0:T(8,128)(2,1)S(1)}, bf16[4,16,1024]{2,1,0:T(8,128)(2,1)S(1)}, u32[]{:S(2)}, u32[]{:S(2)}) collective-permute-start(bf16[4,16,1024]{2,1,0:T(8,128)(2,1)S(1)} %add_convert_fusion.after_ref), channel_id=1, source_target_pairs={{0,2},{1,3},{2,0},{3,1},{4,6},{5,7},{6,4},{7,5},{8,10},{9,11},{10,... | collective-permute-start | bytes 393224 | tf_op jit(solution)/shard_map/ppermute | solution.py:298
  68.6 6.1 %collective-permute-start.22 = (bf16[16,1024]{1,0:T(8,128)(2,1)S(1)}, bf16[16,1024]{1,0:T(8,128)(2,1)S(1)}, u32[]{:S(2)}, u32[]{:S(2)}) collective-permute-start(bf16[16,1024]{1,0:T(8,128)(2,1)S(1)} %get-tuple-element.52), channel_id=1, source_target_pairs={{0,12},{1,13},{2,14},{3,15},{4,8},{5,9},{6,10},{7,11},{8,4},{9,5},... | collective-permute-start | bytes 98312 | tf_op jit(solution)/shard_map/ppermute | solution.py:298
  70.6 4.2 %collective-permute-start.23 = (bf16[16,1024]{1,0:T(8,128)(2,1)S(1)}, bf16[16,1024]{1,0:T(8,128)(2,1)S(1)}, u32[]{:S(2)}, u32[]{:S(2)}) collective-permute-start(bf16[16,1024]{1,0:T(8,128)(2,1)S(1)} %get-tuple-element.54), channel_id=1, source_target_pairs={{0,4},{1,5},{2,6},{3,7},{4,0},{5,1},{6,2},{7,3},{8,12},{9,13},{10,... | collective-permute-start | bytes 98312 | tf_op jit(solution)/shard_map/ppermute | solution.py:298
  70.6 4.8 %collective-permute-start.24 = (bf16[16,1024]{1,0:T(8,128)(2,1)S(1)}, bf16[16,1024]{1,0:T(8,128)(2,1)S(1)}, u32[]{:S(2)}, u32[]{:S(2)}) collective-permute-start(bf16[16,1024]{1,0:T(8,128)(2,1)S(1)} %get-tuple-element.53), channel_id=1, source_target_pairs={{0,8},{1,9},{2,10},{3,11},{4,12},{5,13},{6,14},{7,15},{8,0},{9,1},... | collective-permute-start | bytes 98312 | tf_op jit(solution)/shard_map/ppermute | solution.py:298
  (3 other events, 21.0 us)

commit v5 on v4

--- a/solution.py
+++ b/solution.py
@@ -340,8 +340,9 @@
     logit_sum = partial_logits(tiles, (alpha, alpha_1, alpha_2, alpha_3))
 
     rounded = logit_sum.astype(BF16)
-    received = [swap(rounded, offset) for offset in far[1:]]
-    orders = [[far.index(held ^ offset) for held in far] for offset in far[1:]]
+    partners = sorted(far[1:], reverse=True)
+    received = [swap(rounded, offset) for offset in partners]
+    orders = [[far.index(held ^ offset) for held in far] for offset in partners]
     compute = residual(logit_sum, received, orders, bias_column, points)
     send, logits, resid = kernel_gradient(1, None, tiles, (compute, (logit_sum, received, bias_column, points)))
     received = swap(send, 1)
@@ -360,8 +361,8 @@
     term_0 = gradient_terms(grad, tri_02, 0, count, ahead)
     total = term_0 + received_1 + received_2.astype(F32)
     gradient = total[0]
-    for at, offset in reversed(list(enumerate(far))[1:]):
-        gradient = gradient + swap(total[at].astype(BF16), offset).astype(F32)
+    for offset in sorted(far[1:], reverse=True):
+        gradient = gradient + swap(total[far.index(offset)].astype(BF16), offset).astype(F32)
     return (gradient.T, logits.T)
 
 

time: 76.2 us -> 75.3 us (0.988)
  waiting for transfers between devices: 17.8 us -> 16.9 us
    ppermute x25, waiting for transfers between devices: 17.8 us -> 16.9 us  [swap(): lax.ppermute(array, 'pts', [(index, index ^ mask) for index in range(devi...]
  transfers between devices with their start and end apart: 25 -> 25, of which waited for: 13 -> 11; matrix products, arithmetic and copies ran while one was open for 0% -> 0% of each run, Pallas kernels for 34% -> 35%
where the time goes in v5:
time: 75.3 us; the launch traced here: 75.2 us
  Pallas kernels  29.6 us (39%)
  starting transfers between devices  26.9 us (36%)
  waiting for transfers between devices  16.9 us (22%)
  other arithmetic  0.82 us (1%)
  between operations  0.82 us (1%)
    ppermute x25, starting transfers between devices, swap(): lax.ppermute(array, 'pts', [(index, index ^ mask) for index in range(devi...  26.9 us
    ppermute x25, waiting for transfers between devices, swap(): lax.ppermute(array, 'pts', [(index, index ^ mask) for index in range(devi...  16.9 us
    pallas_call x2, Pallas kernels, alpha_sum(): pl.pallas_call(body, out_shape=[jax.ShapeDtypeStruct((classes, rows), BF1...  14.5 us
    pallas_call x4, Pallas kernels, kernel_tile(): pl.pallas_call(body, out_shape=pltpu.VMEM((len(centre_blocks), local, tot...  5.28 us
    pallas_call x4, Pallas kernels, gradient_terms(): pl.pallas_call(body, out_shape=jax.ShapeDtypeStruct((count, classes, widt...  4.79 us
    pallas_call x2, Pallas kernels, kernel_gradient(): pl.pallas_call(body, out_shape=[jax.ShapeDtypeStruct((n_parts, classes, l...  2.41 us
  transfers between devices with their start and end apart: 25, of which 11 were waited for; matrix products, arithmetic and copies ran while one was open for 0% of the time, Pallas kernels for 35%

profile of v5, /device:TPU:0, one launch (start us, length us, event | category | flops | bytes accessed | tf_op | source)
XLA Modules:
  0.0 75.2 jit_solution(8240192781477179210)
XLA Ops:
  0.6 4.1 %collective-permute-start = (bf16[1,16,1024]{2,1,0:T(8,128)(2,1)}, bf16[1,16,1024]{2,1,0:T(8,128)(2,1)S(1)}, u32[]{:S(2)}, u32[]{:S(2)}) collective-permute-start(bf16[1,16,1024]{2,1,0:T(8,128)(2,1)} %bitcast.34), channel_id=1, source_target_pairs={{0,8},{1,9},{2,10},{3,11},{4,12},{5,13},{6,14},{7,15},{8,0},{9,1},... | collective-permute-start | bytes 98312 | tf_op jit(solution)/shard_map/ppermute | solution.py:298
  4.7 1.4 %prepare.1 = (bf16[1,272,512]{2,1,0:T(8,128)(2,1)S(1)}, bf16[512,512]{1,0:T(8,128)(2,1)S(1)}, bf16[512,512]{1,0:T(8,128)(2,1)S(1)}, bf16[1,16,1024]{2,1,0:T(8,128)(2,1)S(1)}) custom-call(bf16[256,512]{1,0:T(8,128)(2,1)} %points_ref.1, s32[1,256]{1,0:T(1,128)} %bitcast.36, bf16[1024,512]{1,0:T(8,128)(2,1)} %refs_0_.3, bf16[16,1024]{1,0:T(8,128)(2,1)} %bitcast.35), custom_call_target="tpu_custom_call" | custom-call | flops 1024 | bytes 2097152 | tf_op jit(solution)/shard_map/prepare/pallas_call | solution.py:119
  6.1 1.6 %collective-permute-start.3 = (bf16[512,512]{1,0:T(8,128)(2,1)S(1)}, bf16[512,512]{1,0:T(8,128)(2,1)S(1)}, u32[]{:S(2)}, u32[]{:S(2)}) collective-permute-start(bf16[512,512]{1,0:T(8,128)(2,1)S(1)} %get-tuple-element.32), channel_id=1, source_target_pairs={{0,2},{1,3},{2,0},{3,1},{4,6},{5,7},{6,4},{7,5},{8,10},{9,11},{10,... | collective-permute-start | bytes 1572872 | tf_op jit(solution)/shard_map/ppermute | solution.py:298
  7.7 1.6 %collective-permute-start.1 = (bf16[2,16,1024]{2,1,0:T(8,128)(2,1)S(1)}, bf16[2,16,1024]{2,1,0:T(8,128)(2,1)S(1)}, u32[]{:S(2)}, u32[]{:S(2)}) collective-permute-start(bf16[2,16,1024]{2,1,0:T(8,128)(2,1)S(1)} %pad_maximum_fusion.2), channel_id=1, source_target_pairs={{0,4},{1,5},{2,6},{3,7},{4,0},{5,1},{6,2},{7,3},{8,12},{9,13},{10,... | collective-permute-start | bytes 196616 | tf_op jit(solution)/shard_map/ppermute | solution.py:298
  9.3 2.3 %collective-permute-start.5 = (bf16[1,272,512]{2,1,0:T(8,128)(2,1)S(1)}, bf16[1,272,512]{2,1,0:T(8,128)(2,1)S(1)}, u32[]{:S(2)}, u32[]{:S(2)}) collective-permute-start(bf16[1,272,512]{2,1,0:T(8,128)(2,1)S(1)} %get-tuple-element.35), channel_id=1, source_target_pairs={{0,8},{1,9},{2,10},{3,11},{4,12},{5,13},{6,14},{7,15},{8,0},{9,1},... | collective-permute-start | bytes 835592 | tf_op jit(solution)/shard_map/ppermute | solution.py:298
  12.0 1.3 %collective-permute-start.2 = (bf16[4,16,1024]{2,1,0:T(8,128)(2,1)S(1)}, bf16[4,16,1024]{2,1,0:T(8,128)(2,1)S(1)}, u32[]{:S(2)}, u32[]{:S(2)}) collective-permute-start(bf16[4,16,1024]{2,1,0:T(8,128)(2,1)S(1)} %pad_maximum_fusion.1.after_ref.beta_ref), channel_id=1, source_target_pairs={{0,2},{1,3},{2,0},{3,1},{4,6},{5,7},{6,4},{7,5},{8,10},{9,11},{10,... | collective-permute-start | bytes 393224 | tf_op jit(solution)/shard_map/ppermute | solution.py:298
  14.1 6.5 %alpha_sum.2 = (f32[16,1024]{1,0:T(8,128)S(1)}, bf16[8,1024,1024]{2,1,0:T(8,128)(2,1)S(1)}) custom-call(s32[1]{0:T(128)} %bitcast.3.me_ref, bf16[1024,16384]{1,0:T(8,128)(2,1)} %tri_ref.3, bf16[4,16,1024]{2,1,0:T(8,128)(2,1)S(1)} %pad_maximum_fusion.1.after_ref.beta_ref, bf16[4,16,1024]{2,1,0:T(8,128)(2,1)S(1)} %pad_maximum_fusion.1.after_ref.beta_ref), custom_call_target="tpu_custom_call" | custom-call | flops 2147483648 | bytes 16777216 | tf_op jit(solution)/shard_map/alpha_sum/pallas_call | solution.py:81
  20.6 3.2 %collective-permute-done.2.refs_2_ = bf16[4,16,1024]{2,1,0:T(8,128)(2,1)S(1)} collective-permute-done((bf16[4,16,1024]{2,1,0:T(8,128)(2,1)S(1)}, bf16[4,16,1024]{2,1,0:T(8,128)(2,1)S(1)}, u32[]{:S(2)}, u32[]{:S(2)}) %collective-permute-start.2) | collective-permute-done | bytes 131104 | tf_op jit(solution)/shard_map/ppermute | solution.py:298
  25.6 8.1 %alpha_sum.3 = (bf16[16,1024]{1,0:T(8,128)(2,1)S(1)}, bf16[8,1024,1024]{2,1,0:T(8,128)(2,1)S(1)}) custom-call(s32[1]{0:T(128)} %bitcast.3.me_ref, bf16[1024,16384]{1,0:T(8,128)(2,1)} %tri_ref.3, bf16[2,272,512]{2,1,0:T(8,128)(2,1)S(1)} %constant_dynamic-update-slice_fusion.after_ref.point_ref.refs_5_, ...), custom_call_target="tpu_custom_call" | custom-call | flops 2147483648 | bytes 16777216 | tf_op jit(solution)/shard_map/alpha_sum/pallas_call | solution.py:81
  34.3 1.5 %collective-permute-start.8 = (bf16[16,1024]{1,0:T(8,128)(2,1)S(1)}, bf16[16,1024]{1,0:T(8,128)(2,1)S(1)}, u32[]{:S(2)}, u32[]{:S(2)}) collective-permute-start(bf16[16,1024]{1,0:T(8,128)(2,1)S(1)} %get-tuple-element.40.refs_2_.refs_0_), channel_id=1, source_target_pairs={{0,2},{1,3},{2,0},{3,1},{4,6},{5,7},{6,4},{7,5},{8,10},{9,11},{10,... | collective-permute-start | bytes 98312 | tf_op jit(solution)/shard_map/ppermute | solution.py:298
  35.8 1.3 %kernel_tile.4.refs_4_.refs_7_.refs_1_ = bf16[2,1024,512]{2,1,0:T(8,128)(2,1)S(1)} custom-call(bf16[2,272,512]{2,1,0:T(8,128)(2,1)S(1)} %constant_dynamic-update-slice_fusion.after_ref.point_ref.refs_5_, bf16[1024,512]{1,0:T(8,128)(2,1)S(1)} %copy-done, bf16[1024,512]{1,0:T(8,128)(2,1)S(1)} %collective-permute-done.11.refs_1_, ...), custom_call_target="tpu_custom_call" | custom-call | flops 1024 | bytes 1024 | tf_op jit(solution)/shard_map/kernel_tile/pallas_call | solution.py:177
  37.2 1.3 %kernel_tile.5.refs_2_.refs_5_.refs_8_ = bf16[2,1024,512]{2,1,0:T(8,128)(2,1)S(1)} custom-call(bf16[2,272,512]{2,1,0:T(8,128)(2,1)S(1)} %constant_dynamic-update-slice_fusion.after_ref.point_ref.refs_5_, bf16[512,512]{1,0:T(8,128)(2,1)S(1)} %collective-permute-done.3.refs_0_, bf16[512,512]{1,0:T(8,128)(2,1)S(1)} %collective-permute-done.4.refs_1_, ...), custom_call_target="tpu_custom_call" | custom-call | flops 1024 | bytes 1024 | tf_op jit(solution)/shard_map/kernel_tile/pallas_call | solution.py:177
  39.7 1.3 %kernel_tile.6.refs_4_.refs_6_.refs_9_.refs_3_ = bf16[2,1024,512]{2,1,0:T(8,128)(2,1)S(1)} custom-call(bf16[2,272,512]{2,1,0:T(8,128)(2,1)S(1)} %collective-permute-done.12.point_ref.refs_6_, bf16[1024,512]{1,0:T(8,128)(2,1)S(1)} %copy-done, bf16[1024,512]{1,0:T(8,128)(2,1)S(1)} %collective-permute-done.11.refs_1_, ...), custom_call_target="tpu_custom_call" | custom-call | flops 1024 | bytes 1024 | tf_op jit(solution)/shard_map/kernel_tile/pallas_call | solution.py:177
  41.0 1.3 %kernel_tile.7.refs_7_.refs_10_.refs_4_ = bf16[2,1024,512]{2,1,0:T(8,128)(2,1)S(1)} custom-call(bf16[2,272,512]{2,1,0:T(8,128)(2,1)S(1)} %collective-permute-done.12.point_ref.refs_6_, bf16[512,512]{1,0:T(8,128)(2,1)S(1)} %collective-permute-done.3.refs_0_, bf16[512,512]{1,0:T(8,128)(2,1)S(1)} %collective-permute-done.4.refs_1_, ...), custom_call_target="tpu_custom_call" | custom-call | flops 1024 | bytes 1024 | tf_op jit(solution)/shard_map/kernel_tile/pallas_call | solution.py:177
  43.6 1.9 %collective-permute-start.14 = (bf16[16,1024]{1,0:T(8,128)(2,1)S(1)}, bf16[16,1024]{1,0:T(8,128)(2,1)S(1)}, u32[]{:S(2)}, u32[]{:S(2)}) collective-permute-start(bf16[16,1024]{1,0:T(8,128)(2,1)S(1)} %convert_element_type.33), channel_id=1, source_target_pairs={{0,12},{1,13},{2,14},{3,15},{4,8},{5,9},{6,10},{7,11},{8,4},{9,5},... | collective-permute-start | bytes 98312 | tf_op jit(solution)/shard_map/ppermute | solution.py:298
  46.0 1.9 %collective-permute-start.16 = (bf16[16,1024]{1,0:T(8,128)(2,1)S(1)}, bf16[16,1024]{1,0:T(8,128)(2,1)S(1)}, u32[]{:S(2)}, u32[]{:S(2)}) collective-permute-start(bf16[16,1024]{1,0:T(8,128)(2,1)S(1)} %convert_element_type.33), channel_id=1, source_target_pairs={{0,4},{1,5},{2,6},{3,7},{4,0},{5,1},{6,2},{7,3},{8,12},{9,13},{10,... | collective-permute-start | bytes 98312 | tf_op jit(solution)/shard_map/ppermute | solution.py:298
  48.0 1.6 %collective-permute-done.14.refs_2_ = bf16[16,1024]{1,0:T(8,128)(2,1)S(1)} collective-permute-done((bf16[16,1024]{1,0:T(8,128)(2,1)S(1)}, bf16[16,1024]{1,0:T(8,128)(2,1)S(1)}, u32[]{:S(2)}, u32[]{:S(2)}) %collective-permute-start.14) | collective-permute-done | bytes 32800 | tf_op jit(solution)/shard_map/ppermute | solution.py:298
  53.3 1.6 %collective-permute-start.18 = (f32[16,1024]{1,0:T(8,128)S(1)}, f32[16,1024]{1,0:T(8,128)S(1)}, u32[]{:S(2)}, u32[]{:S(2)}) collective-permute-start(f32[16,1024]{1,0:T(8,128)S(1)} %fusion.4), channel_id=1, source_target_pairs={{0,2},{1,3},{2,0},{3,1},{4,6},{5,7},{6,4},{7,5},{8,10},{9,11},{10,... | collective-permute-start | bytes 196616 | tf_op jit(solution)/shard_map/ppermute | solution.py:298
  54.9 2.8 %collective-permute-done.18 = f32[16,1024]{1,0:T(8,128)S(1)} collective-permute-done((f32[16,1024]{1,0:T(8,128)S(1)}, f32[16,1024]{1,0:T(8,128)S(1)}, u32[]{:S(2)}, u32[]{:S(2)}) %collective-permute-start.18) | collective-permute-done | bytes 65568 | tf_op jit(solution)/shard_map/ppermute | solution.py:298
  61.9 1.6 %collective-permute-start.21 = (bf16[4,16,1024]{2,1,0:T(8,128)(2,1)S(1)}, bf16[4,16,1024]{2,1,0:T(8,128)(2,1)S(1)}, u32[]{:S(2)}, u32[]{:S(2)}) collective-permute-start(bf16[4,16,1024]{2,1,0:T(8,128)(2,1)S(1)} %add_convert_fusion.after_ref), channel_id=1, source_target_pairs={{0,2},{1,3},{2,0},{3,1},{4,6},{5,7},{6,4},{7,5},{8,10},{9,11},{10,... | collective-permute-start | bytes 393224 | tf_op jit(solution)/shard_map/ppermute | solution.py:298
  64.7 2.7 %collective-permute-done.21 = bf16[4,16,1024]{2,1,0:T(8,128)(2,1)S(1)} collective-permute-done((bf16[4,16,1024]{2,1,0:T(8,128)(2,1)S(1)}, bf16[4,16,1024]{2,1,0:T(8,128)(2,1)S(1)}, u32[]{:S(2)}, u32[]{:S(2)}) %collective-permute-start.21) | collective-permute-done | bytes 131104 | tf_op jit(solution)/shard_map/ppermute | solution.py:298
  67.4 2.2 %collective-permute-start.22 = (bf16[16,1024]{1,0:T(8,128)(2,1)S(1)}, bf16[16,1024]{1,0:T(8,128)(2,1)S(1)}, u32[]{:S(2)}, u32[]{:S(2)}) collective-permute-start(bf16[16,1024]{1,0:T(8,128)(2,1)S(1)} %get-tuple-element.52), channel_id=1, source_target_pairs={{0,12},{1,13},{2,14},{3,15},{4,8},{5,9},{6,10},{7,11},{8,4},{9,5},... | collective-permute-start | bytes 98312 | tf_op jit(solution)/shard_map/ppermute | solution.py:298
  70.2 1.6 %collective-permute-start.24 = (bf16[16,1024]{1,0:T(8,128)(2,1)S(1)}, bf16[16,1024]{1,0:T(8,128)(2,1)S(1)}, u32[]{:S(2)}, u32[]{:S(2)}) collective-permute-start(bf16[16,1024]{1,0:T(8,128)(2,1)S(1)} %get-tuple-element.53), channel_id=1, source_target_pairs={{0,4},{1,5},{2,6},{3,7},{4,0},{5,1},{6,2},{7,3},{8,12},{9,13},{10,... | collective-permute-start | bytes 98312 | tf_op jit(solution)/shard_map/ppermute | solution.py:298
  71.9 1.3 %collective-permute-done.22 = bf16[16,1024]{1,0:T(8,128)(2,1)S(1)} collective-permute-done((bf16[16,1024]{1,0:T(8,128)(2,1)S(1)}, bf16[16,1024]{1,0:T(8,128)(2,1)S(1)}, u32[]{:S(2)}, u32[]{:S(2)}) %collective-permute-start.22) | collective-permute-done | bytes 32800 | tf_op jit(solution)/shard_map/ppermute | solution.py:298
  (57 shorter events, 18.1 us)
Async XLA Ops:
  0.6 7.1 %collective-permute-start = (bf16[1,16,1024]{2,1,0:T(8,128)(2,1)}, bf16[1,16,1024]{2,1,0:T(8,128)(2,1)S(1)}, u32[]{:S(2)}, u32[]{:S(2)}) collective-permute-start(bf16[1,16,1024]{2,1,0:T(8,128)(2,1)} %bitcast.34), channel_id=1, source_target_pairs={{0,8},{1,9},{2,10},{3,11},{4,12},{5,13},{6,14},{7,15},{8,0},{9,1},... | collective-permute-start | bytes 98312 | tf_op jit(solution)/shard_map/ppermute | solution.py:298
  6.1 17.7 %collective-permute-start.3 = (bf16[512,512]{1,0:T(8,128)(2,1)S(1)}, bf16[512,512]{1,0:T(8,128)(2,1)S(1)}, u32[]{:S(2)}, u32[]{:S(2)}) collective-permute-start(bf16[512,512]{1,0:T(8,128)(2,1)S(1)} %get-tuple-element.32), channel_id=1, source_target_pairs={{0,2},{1,3},{2,0},{3,1},{4,6},{5,7},{6,4},{7,5},{8,10},{9,11},{10,... | collective-permute-start | bytes 1572872 | tf_op jit(solution)/shard_map/ppermute | solution.py:298
  7.7 4.3 %collective-permute-start.1 = (bf16[2,16,1024]{2,1,0:T(8,128)(2,1)S(1)}, bf16[2,16,1024]{2,1,0:T(8,128)(2,1)S(1)}, u32[]{:S(2)}, u32[]{:S(2)}) collective-permute-start(bf16[2,16,1024]{2,1,0:T(8,128)(2,1)S(1)} %pad_maximum_fusion.2), channel_id=1, source_target_pairs={{0,4},{1,5},{2,6},{3,7},{4,0},{5,1},{6,2},{7,3},{8,12},{9,13},{10,... | collective-permute-start | bytes 196616 | tf_op jit(solution)/shard_map/ppermute | solution.py:298
  9.3 26.5 %collective-permute-start.11 = (bf16[1024,512]{1,0:T(8,128)(2,1)}, bf16[1024,512]{1,0:T(8,128)(2,1)S(1)}, u32[]{:S(2)}, u32[]{:S(2)}) collective-permute-start(bf16[1024,512]{1,0:T(8,128)(2,1)} %refs_0_.3), channel_id=1, source_target_pairs={{0,1},{1,0},{2,3},{3,2},{4,5},{5,4},{6,7},{7,6},{8,9},{9,8},{10,11... | collective-permute-start | bytes 3145736 | tf_op jit(solution)/shard_map/ppermute | solution.py:298
  9.3 15.8 %collective-permute-start.5 = (bf16[1,272,512]{2,1,0:T(8,128)(2,1)S(1)}, bf16[1,272,512]{2,1,0:T(8,128)(2,1)S(1)}, u32[]{:S(2)}, u32[]{:S(2)}) collective-permute-start(bf16[1,272,512]{2,1,0:T(8,128)(2,1)S(1)} %get-tuple-element.35), channel_id=1, source_target_pairs={{0,8},{1,9},{2,10},{3,11},{4,12},{5,13},{6,14},{7,15},{8,0},{9,1},... | collective-permute-start | bytes 835592 | tf_op jit(solution)/shard_map/ppermute | solution.py:298
  12.0 11.8 %collective-permute-start.2 = (bf16[4,16,1024]{2,1,0:T(8,128)(2,1)S(1)}, bf16[4,16,1024]{2,1,0:T(8,128)(2,1)S(1)}, u32[]{:S(2)}, u32[]{:S(2)}) collective-permute-start(bf16[4,16,1024]{2,1,0:T(8,128)(2,1)S(1)} %pad_maximum_fusion.1.after_ref.beta_ref), channel_id=1, source_target_pairs={{0,2},{1,3},{2,0},{3,1},{4,6},{5,7},{6,4},{7,5},{8,10},{9,11},{10,... | collective-permute-start | bytes 393224 | tf_op jit(solution)/shard_map/ppermute | solution.py:298
  13.4 20.4 %collective-permute-start.4 = (bf16[512,512]{1,0:T(8,128)(2,1)S(1)}, bf16[512,512]{1,0:T(8,128)(2,1)S(1)}, u32[]{:S(2)}, u32[]{:S(2)}) collective-permute-start(bf16[512,512]{1,0:T(8,128)(2,1)S(1)} %get-tuple-element.34), channel_id=1, source_target_pairs={{0,2},{1,3},{2,0},{3,1},{4,6},{5,7},{6,4},{7,5},{8,10},{9,11},{10,... | collective-permute-start | bytes 1572872 | tf_op jit(solution)/shard_map/ppermute | solution.py:298
  23.8 1.8 %collective-permute-start.6 = (bf16[8,16,1024]{2,1,0:T(8,128)(2,1)S(1)}, bf16[8,16,1024]{2,1,0:T(8,128)(2,1)S(1)}, u32[]{:S(2)}, u32[]{:S(2)}) collective-permute-start(bf16[8,16,1024]{2,1,0:T(8,128)(2,1)S(1)} %pad_maximum_fusion), channel_id=1, source_target_pairs={{0,1},{1,0},{2,3},{3,2},{4,5},{5,4},{6,7},{7,6},{8,9},{9,8},{10,11... | collective-permute-start | bytes 786440 | tf_op jit(solution)/shard_map/ppermute | solution.py:298
  25.2 14.5 %collective-permute-start.12 = (bf16[2,272,512]{2,1,0:T(8,128)(2,1)S(1)}, bf16[2,272,512]{2,1,0:T(8,128)(2,1)S(1)}, u32[]{:S(2)}, u32[]{:S(2)}) collective-permute-start(bf16[2,272,512]{2,1,0:T(8,128)(2,1)S(1)} %constant_dynamic-update-slice_fusion.after_ref.point_ref.refs_5_), channel_id=1, source_target_pairs={{0,4},{1,5},{2,6},{3,7},{4,0},{5,1},{6,2},{7,3},{8,12},{9,13},{10,... | collective-permute-start | bytes 1671176 | tf_op jit(solution)/shard_map/ppermute | solution.py:298
  33.7 3.4 %collective-permute-start.10 = (bf16[512,512]{1,0:T(8,128)(2,1)S(1)}, bf16[512,512]{1,0:T(8,128)(2,1)S(1)}, u32[]{:S(2)}, u32[]{:S(2)}) collective-permute-start(bf16[512,512]{1,0:T(8,128)(2,1)S(1)} %collective-permute-done.4.refs_1_), channel_id=1, source_target_pairs={{0,1},{1,0},{2,3},{3,2},{4,5},{5,4},{6,7},{7,6},{8,9},{9,8},{10,11... | collective-permute-start | bytes 1572872 | tf_op jit(solution)/shard_map/ppermute | solution.py:298
  34.0 3.2 %collective-permute-start.9 = (bf16[512,512]{1,0:T(8,128)(2,1)S(1)}, bf16[512,512]{1,0:T(8,128)(2,1)S(1)}, u32[]{:S(2)}, u32[]{:S(2)}) collective-permute-start(bf16[512,512]{1,0:T(8,128)(2,1)S(1)} %collective-permute-done.3.refs_0_), channel_id=1, source_target_pairs={{0,1},{1,0},{2,3},{3,2},{4,5},{5,4},{6,7},{7,6},{8,9},{9,8},{10,11... | collective-permute-start | bytes 1572872 | tf_op jit(solution)/shard_map/ppermute | solution.py:298
  34.3 4.2 %collective-permute-start.8 = (bf16[16,1024]{1,0:T(8,128)(2,1)S(1)}, bf16[16,1024]{1,0:T(8,128)(2,1)S(1)}, u32[]{:S(2)}, u32[]{:S(2)}) collective-permute-start(bf16[16,1024]{1,0:T(8,128)(2,1)S(1)} %get-tuple-element.40.refs_2_.refs_0_), channel_id=1, source_target_pairs={{0,2},{1,3},{2,0},{3,1},{4,6},{5,7},{6,4},{7,5},{8,10},{9,11},{10,... | collective-permute-start | bytes 98312 | tf_op jit(solution)/shard_map/ppermute | solution.py:298
  35.8 6.5 %collective-permute-start.7 = (bf16[16,1024]{1,0:T(8,128)(2,1)S(1)}, bf16[16,1024]{1,0:T(8,128)(2,1)S(1)}, u32[]{:S(2)}, u32[]{:S(2)}) collective-permute-start(bf16[16,1024]{1,0:T(8,128)(2,1)S(1)} %get-tuple-element.40.refs_2_.refs_0_), channel_id=1, source_target_pairs={{0,1},{1,0},{2,3},{3,2},{4,5},{5,4},{6,7},{7,6},{8,9},{9,8},{10,11... | collective-permute-start | bytes 98312 | tf_op jit(solution)/shard_map/ppermute | solution.py:298
  39.7 2.7 %collective-permute-start.13 = (bf16[16,1024]{1,0:T(8,128)(2,1)S(1)}, bf16[16,1024]{1,0:T(8,128)(2,1)S(1)}, u32[]{:S(2)}, u32[]{:S(2)}) collective-permute-start(bf16[16,1024]{1,0:T(8,128)(2,1)S(1)} %collective-permute-done.8.refs_2_), channel_id=1, source_target_pairs={{0,1},{1,0},{2,3},{3,2},{4,5},{5,4},{6,7},{7,6},{8,9},{9,8},{10,11... | collective-permute-start | bytes 98312 | tf_op jit(solution)/shard_map/ppermute | solution.py:298
  43.6 6.0 %collective-permute-start.14 = (bf16[16,1024]{1,0:T(8,128)(2,1)S(1)}, bf16[16,1024]{1,0:T(8,128)(2,1)S(1)}, u32[]{:S(2)}, u32[]{:S(2)}) collective-permute-start(bf16[16,1024]{1,0:T(8,128)(2,1)S(1)} %convert_element_type.33), channel_id=1, source_target_pairs={{0,12},{1,13},{2,14},{3,15},{4,8},{5,9},{6,10},{7,11},{8,4},{9,5},... | collective-permute-start | bytes 98312 | tf_op jit(solution)/shard_map/ppermute | solution.py:298
  45.5 5.1 %collective-permute-start.15 = (bf16[16,1024]{1,0:T(8,128)(2,1)S(1)}, bf16[16,1024]{1,0:T(8,128)(2,1)S(1)}, u32[]{:S(2)}, u32[]{:S(2)}) collective-permute-start(bf16[16,1024]{1,0:T(8,128)(2,1)S(1)} %convert_element_type.33), channel_id=1, source_target_pairs={{0,8},{1,9},{2,10},{3,11},{4,12},{5,13},{6,14},{7,15},{8,0},{9,1},... | collective-permute-start | bytes 98312 | tf_op jit(solution)/shard_map/ppermute | solution.py:298
  46.0 4.6 %collective-permute-start.16 = (bf16[16,1024]{1,0:T(8,128)(2,1)S(1)}, bf16[16,1024]{1,0:T(8,128)(2,1)S(1)}, u32[]{:S(2)}, u32[]{:S(2)}) collective-permute-start(bf16[16,1024]{1,0:T(8,128)(2,1)S(1)} %convert_element_type.33), channel_id=1, source_target_pairs={{0,4},{1,5},{2,6},{3,7},{4,0},{5,1},{6,2},{7,3},{8,12},{9,13},{10,... | collective-permute-start | bytes 98312 | tf_op jit(solution)/shard_map/ppermute | solution.py:298
  53.3 4.4 %collective-permute-start.18 = (f32[16,1024]{1,0:T(8,128)S(1)}, f32[16,1024]{1,0:T(8,128)S(1)}, u32[]{:S(2)}, u32[]{:S(2)}) collective-permute-start(f32[16,1024]{1,0:T(8,128)S(1)} %fusion.4), channel_id=1, source_target_pairs={{0,2},{1,3},{2,0},{3,1},{4,6},{5,7},{6,4},{7,5},{8,10},{9,11},{10,... | collective-permute-start | bytes 196616 | tf_op jit(solution)/shard_map/ppermute | solution.py:298
  58.9 2.9 %collective-permute-start.19 = (f32[4,16,1024]{2,1,0:T(8,128)S(1)}, f32[4,16,1024]{2,1,0:T(8,128)S(1)}, u32[]{:S(2)}, u32[]{:S(2)}) collective-permute-start(f32[4,16,1024]{2,1,0:T(8,128)S(1)} %gradient_terms.4.after_ref), channel_id=1, source_target_pairs={{0,1},{1,0},{2,3},{3,2},{4,5},{5,4},{6,7},{7,6},{8,9},{9,8},{10,11... | collective-permute-start | bytes 786440 | tf_op jit(solution)/shard_map/ppermute | solution.py:298
  60.1 4.6 %collective-permute-start.20 = (f32[4,16,1024]{2,1,0:T(8,128)S(1)}, f32[4,16,1024]{2,1,0:T(8,128)S(1)}, u32[]{:S(2)}, u32[]{:S(2)}) collective-permute-start(f32[4,16,1024]{2,1,0:T(8,128)S(1)} %gradient_terms.5.after_ref), channel_id=1, source_target_pairs={{0,1},{1,0},{2,3},{3,2},{4,5},{5,4},{6,7},{7,6},{8,9},{9,8},{10,11... | collective-permute-start | bytes 786440 | tf_op jit(solution)/shard_map/ppermute | solution.py:298
  61.9 5.5 %collective-permute-start.21 = (bf16[4,16,1024]{2,1,0:T(8,128)(2,1)S(1)}, bf16[4,16,1024]{2,1,0:T(8,128)(2,1)S(1)}, u32[]{:S(2)}, u32[]{:S(2)}) collective-permute-start(bf16[4,16,1024]{2,1,0:T(8,128)(2,1)S(1)} %add_convert_fusion.after_ref), channel_id=1, source_target_pairs={{0,2},{1,3},{2,0},{3,1},{4,6},{5,7},{6,4},{7,5},{8,10},{9,11},{10,... | collective-permute-start | bytes 393224 | tf_op jit(solution)/shard_map/ppermute | solution.py:298
  67.4 5.8 %collective-permute-start.22 = (bf16[16,1024]{1,0:T(8,128)(2,1)S(1)}, bf16[16,1024]{1,0:T(8,128)(2,1)S(1)}, u32[]{:S(2)}, u32[]{:S(2)}) collective-permute-start(bf16[16,1024]{1,0:T(8,128)(2,1)S(1)} %get-tuple-element.52), channel_id=1, source_target_pairs={{0,12},{1,13},{2,14},{3,15},{4,8},{5,9},{6,10},{7,11},{8,4},{9,5},... | collective-permute-start | bytes 98312 | tf_op jit(solution)/shard_map/ppermute | solution.py:298
  69.7 4.8 %collective-permute-start.23 = (bf16[16,1024]{1,0:T(8,128)(2,1)S(1)}, bf16[16,1024]{1,0:T(8,128)(2,1)S(1)}, u32[]{:S(2)}, u32[]{:S(2)}) collective-permute-start(bf16[16,1024]{1,0:T(8,128)(2,1)S(1)} %get-tuple-element.54), channel_id=1, source_target_pairs={{0,8},{1,9},{2,10},{3,11},{4,12},{5,13},{6,14},{7,15},{8,0},{9,1},... | collective-permute-start | bytes 98312 | tf_op jit(solution)/shard_map/ppermute | solution.py:298
  70.2 4.3 %collective-permute-start.24 = (bf16[16,1024]{1,0:T(8,128)(2,1)S(1)}, bf16[16,1024]{1,0:T(8,128)(2,1)S(1)}, u32[]{:S(2)}, u32[]{:S(2)}) collective-permute-start(bf16[16,1024]{1,0:T(8,128)(2,1)S(1)} %get-tuple-element.53), channel_id=1, source_target_pairs={{0,4},{1,5},{2,6},{3,7},{4,0},{5,1},{6,2},{7,3},{8,12},{9,13},{10,... | collective-permute-start | bytes 98312 | tf_op jit(solution)/shard_map/ppermute | solution.py:298
  (3 other events, 19.8 us)

commit v6 on v5

--- a/solution.py
+++ b/solution.py
@@ -185,24 +185,28 @@
     )(points, *pieces, after)
 
 
+def place_of(row, index):
+    for which, tile in enumerate(row):
+        if index < tile.shape[0]:
+            return which, index
+        index -= tile.shape[0]
+
+
 def partial_logits(tiles, alphas):
     classes = alphas[0].shape[0]
     sizes = [row[0].shape[2] for row in tiles]
     flat = [tile for row in tiles for tile in row]
-    counts = [tile.shape[0] for tile in tiles[0]]
 
     def body(*refs):
         alpha_refs, tile_refs, out_ref = refs[: len(alphas)], refs[len(alphas) : -1], refs[-1]
         for part, size in enumerate(sizes):
             first = sum(sizes[:part])
+            held = sum(len(row) for row in tiles[:part])
             acc = None
-            index = 0
-            for which, count in enumerate(counts):
-                tile_ref = tile_refs[part * len(counts) + which]
-                for at in range(count):
-                    term = jnp.dot(alpha_refs[index][...], tile_ref[at], preferred_element_type=F32)
-                    acc = term if acc is None else acc + term
-                    index += 1
+            for index in range(len(alphas)):
+                which, at = place_of(tiles[part], index)
+                term = jnp.dot(alpha_refs[index][...], tile_refs[held + which][at], preferred_element_type=F32)
+                acc = term if acc is None else acc + term
             out_ref[:, first : first + size] = acc
 
     return pl.pallas_call(
@@ -268,9 +272,11 @@
             acc = None
             for part, size in enumerate(sizes):
                 first = sum(sizes[:part])
+                held = sum(len(row) for row in tiles[:part])
+                array, at = place_of(tiles[part], 2 * which + parity)
                 term = lax.dot_general(
                     resid_ref[:, first : first + size],
-                    tile_refs[part * n_parts + which][parity],
+                    tile_refs[held + array][at],
                     ROWS_BY_ROWS,
                     preferred_element_type=F32,
                 )
@@ -334,9 +340,8 @@
     tile_01 = kernel_tile(block, points[0], far_centres, tile_00)
     alpha_2, tile_01, points[1] = lax.optimization_barrier((alpha_2, tile_01, points[1]))
     alpha_3 = swap(alpha_2, 1)
-    tile_10 = kernel_tile(block, points[1], near_centres, tile_01)
-    tile_11 = kernel_tile(block, points[1], far_centres, tile_10)
-    tiles = [[tile_00, tile_01], [tile_10, tile_11]]
+    tile_1 = kernel_tile(block, points[1], near_centres + far_centres, tile_01)
+    tiles = [[tile_00, tile_01], [tile_1]]
     logit_sum = partial_logits(tiles, (alpha, alpha_1, alpha_2, alpha_3))
 
     rounded = logit_sum.astype(BF16)

time: 75.3 us -> 75.1 us (level)
    pallas_call x4 -> x3, Pallas kernels: 5.28 us -> 5.05 us  [kernel_tile(): pl.pallas_call(body, out_shape=pltpu.VMEM((len(centre_blocks), local, tot...]
  transfers between devices with their start and end apart: 25 -> 25, of which waited for: 11 -> 11; matrix products, arithmetic and copies ran while one was open for 0% -> 0% of each run, Pallas kernels for 35% -> 34%
where the time goes in v6:
time: 75.1 us; the launch traced here: 74.9 us
  Pallas kernels  29.3 us (39%)
  starting transfers between devices  27 us (36%)
  waiting for transfers between devices  16.9 us (23%)
  other arithmetic  0.82 us (1%)
  between operations  0.82 us (1%)
    ppermute x25, starting transfers between devices, swap(): lax.ppermute(array, 'pts', [(index, index ^ mask) for index in range(devi...  27 us
    ppermute x25, waiting for transfers between devices, swap(): lax.ppermute(array, 'pts', [(index, index ^ mask) for index in range(devi...  16.9 us
    pallas_call x2, Pallas kernels, alpha_sum(): pl.pallas_call(body, out_shape=[jax.ShapeDtypeStruct((classes, rows), BF1...  14.5 us
    pallas_call x3, Pallas kernels, kernel_tile(): pl.pallas_call(body, out_shape=pltpu.VMEM((len(centre_blocks), local, tot...  5.05 us
    pallas_call x4, Pallas kernels, gradient_terms(): pl.pallas_call(body, out_shape=jax.ShapeDtypeStruct((count, classes, widt...  4.79 us
    pallas_call x2, Pallas kernels, kernel_gradient(): pl.pallas_call(body, out_shape=[jax.ShapeDtypeStruct((n_parts, classes, l...  2.41 us
  transfers between devices with their start and end apart: 25, of which 11 were waited for; matrix products, arithmetic and copies ran while one was open for 0% of the time, Pallas kernels for 34%

profile of v6, /device:TPU:0, one launch (start us, length us, event | category | flops | bytes accessed | tf_op | source)
XLA Modules:
  0.0 74.9 jit_solution(1859774230044700016)
XLA Ops:
  0.6 4.1 %collective-permute-start = (bf16[1,16,1024]{2,1,0:T(8,128)(2,1)}, bf16[1,16,1024]{2,1,0:T(8,128)(2,1)S(1)}, u32[]{:S(2)}, u32[]{:S(2)}) collective-permute-start(bf16[1,16,1024]{2,1,0:T(8,128)(2,1)} %bitcast.34), channel_id=1, source_target_pairs={{0,8},{1,9},{2,10},{3,11},{4,12},{5,13},{6,14},{7,15},{8,0},{9,1},... | collective-permute-start | bytes 98312 | tf_op jit(solution)/shard_map/ppermute | solution.py:304
  4.7 1.4 %prepare.1 = (bf16[1,272,512]{2,1,0:T(8,128)(2,1)S(1)}, bf16[512,512]{1,0:T(8,128)(2,1)S(1)}, bf16[512,512]{1,0:T(8,128)(2,1)S(1)}, bf16[1,16,1024]{2,1,0:T(8,128)(2,1)S(1)}) custom-call(bf16[256,512]{1,0:T(8,128)(2,1)} %points_ref.1, s32[1,256]{1,0:T(1,128)} %bitcast.36, bf16[1024,512]{1,0:T(8,128)(2,1)} %refs_0_.3, bf16[16,1024]{1,0:T(8,128)(2,1)} %bitcast.35), custom_call_target="tpu_custom_call" | custom-call | flops 1024 | bytes 2097152 | tf_op jit(solution)/shard_map/prepare/pallas_call | solution.py:119
  6.1 1.6 %collective-permute-start.3 = (bf16[512,512]{1,0:T(8,128)(2,1)S(1)}, bf16[512,512]{1,0:T(8,128)(2,1)S(1)}, u32[]{:S(2)}, u32[]{:S(2)}) collective-permute-start(bf16[512,512]{1,0:T(8,128)(2,1)S(1)} %get-tuple-element.32), channel_id=1, source_target_pairs={{0,2},{1,3},{2,0},{3,1},{4,6},{5,7},{6,4},{7,5},{8,10},{9,11},{10,... | collective-permute-start | bytes 1572872 | tf_op jit(solution)/shard_map/ppermute | solution.py:304
  7.7 1.6 %collective-permute-start.1 = (bf16[2,16,1024]{2,1,0:T(8,128)(2,1)S(1)}, bf16[2,16,1024]{2,1,0:T(8,128)(2,1)S(1)}, u32[]{:S(2)}, u32[]{:S(2)}) collective-permute-start(bf16[2,16,1024]{2,1,0:T(8,128)(2,1)S(1)} %pad_maximum_fusion.2), channel_id=1, source_target_pairs={{0,4},{1,5},{2,6},{3,7},{4,0},{5,1},{6,2},{7,3},{8,12},{9,13},{10,... | collective-permute-start | bytes 196616 | tf_op jit(solution)/shard_map/ppermute | solution.py:304
  9.3 2.3 %collective-permute-start.5 = (bf16[1,272,512]{2,1,0:T(8,128)(2,1)S(1)}, bf16[1,272,512]{2,1,0:T(8,128)(2,1)S(1)}, u32[]{:S(2)}, u32[]{:S(2)}) collective-permute-start(bf16[1,272,512]{2,1,0:T(8,128)(2,1)S(1)} %get-tuple-element.35), channel_id=1, source_target_pairs={{0,8},{1,9},{2,10},{3,11},{4,12},{5,13},{6,14},{7,15},{8,0},{9,1},... | collective-permute-start | bytes 835592 | tf_op jit(solution)/shard_map/ppermute | solution.py:304
  12.0 1.3 %collective-permute-start.2 = (bf16[4,16,1024]{2,1,0:T(8,128)(2,1)S(1)}, bf16[4,16,1024]{2,1,0:T(8,128)(2,1)S(1)}, u32[]{:S(2)}, u32[]{:S(2)}) collective-permute-start(bf16[4,16,1024]{2,1,0:T(8,128)(2,1)S(1)} %pad_maximum_fusion.1.after_ref.beta_ref), channel_id=1, source_target_pairs={{0,2},{1,3},{2,0},{3,1},{4,6},{5,7},{6,4},{7,5},{8,10},{9,11},{10,... | collective-permute-start | bytes 393224 | tf_op jit(solution)/shard_map/ppermute | solution.py:304
  14.1 6.5 %alpha_sum.2 = (f32[16,1024]{1,0:T(8,128)S(1)}, bf16[8,1024,1024]{2,1,0:T(8,128)(2,1)S(1)}) custom-call(s32[1]{0:T(128)} %bitcast.3.me_ref, bf16[1024,16384]{1,0:T(8,128)(2,1)} %tri_ref.3, bf16[4,16,1024]{2,1,0:T(8,128)(2,1)S(1)} %pad_maximum_fusion.1.after_ref.beta_ref, bf16[4,16,1024]{2,1,0:T(8,128)(2,1)S(1)} %pad_maximum_fusion.1.after_ref.beta_ref), custom_call_target="tpu_custom_call" | custom-call | flops 2147483648 | bytes 16777216 | tf_op jit(solution)/shard_map/alpha_sum/pallas_call | solution.py:81
  20.6 3.2 %collective-permute-done.2.refs_2_ = bf16[4,16,1024]{2,1,0:T(8,128)(2,1)S(1)} collective-permute-done((bf16[4,16,1024]{2,1,0:T(8,128)(2,1)S(1)}, bf16[4,16,1024]{2,1,0:T(8,128)(2,1)S(1)}, u32[]{:S(2)}, u32[]{:S(2)}) %collective-permute-start.2) | collective-permute-done | bytes 131104 | tf_op jit(solution)/shard_map/ppermute | solution.py:304
  25.6 8.1 %alpha_sum.3 = (bf16[16,1024]{1,0:T(8,128)(2,1)S(1)}, bf16[8,1024,1024]{2,1,0:T(8,128)(2,1)S(1)}) custom-call(s32[1]{0:T(128)} %bitcast.3.me_ref, bf16[1024,16384]{1,0:T(8,128)(2,1)} %tri_ref.3, bf16[2,272,512]{2,1,0:T(8,128)(2,1)S(1)} %constant_dynamic-update-slice_fusion.after_ref.point_ref.refs_5_, ...), custom_call_target="tpu_custom_call" | custom-call | flops 2147483648 | bytes 16777216 | tf_op jit(solution)/shard_map/alpha_sum/pallas_call | solution.py:81
  34.3 1.5 %collective-permute-start.8 = (bf16[16,1024]{1,0:T(8,128)(2,1)S(1)}, bf16[16,1024]{1,0:T(8,128)(2,1)S(1)}, u32[]{:S(2)}, u32[]{:S(2)}) collective-permute-start(bf16[16,1024]{1,0:T(8,128)(2,1)S(1)} %get-tuple-element.40.refs_2_.refs_0_), channel_id=1, source_target_pairs={{0,2},{1,3},{2,0},{3,1},{4,6},{5,7},{6,4},{7,5},{8,10},{9,11},{10,... | collective-permute-start | bytes 98312 | tf_op jit(solution)/shard_map/ppermute | solution.py:304
  35.9 1.3 %kernel_tile.3.refs_4_.refs_7_.refs_1_ = bf16[2,1024,512]{2,1,0:T(8,128)(2,1)S(1)} custom-call(bf16[2,272,512]{2,1,0:T(8,128)(2,1)S(1)} %constant_dynamic-update-slice_fusion.after_ref.point_ref.refs_5_, bf16[1024,512]{1,0:T(8,128)(2,1)S(1)} %copy-done, bf16[1024,512]{1,0:T(8,128)(2,1)S(1)} %collective-permute-done.11.refs_1_, ...), custom_call_target="tpu_custom_call" | custom-call | flops 1024 | bytes 1024 | tf_op jit(solution)/shard_map/kernel_tile/pallas_call | solution.py:177
  37.2 1.3 %kernel_tile.4.refs_6_.refs_5_.refs_8_.refs_2_ = bf16[2,1024,512]{2,1,0:T(8,128)(2,1)S(1)} custom-call(bf16[2,272,512]{2,1,0:T(8,128)(2,1)S(1)} %constant_dynamic-update-slice_fusion.after_ref.point_ref.refs_5_, bf16[512,512]{1,0:T(8,128)(2,1)S(1)} %collective-permute-done.3.refs_0_.refs_2_, bf16[512,512]{1,0:T(8,128)(2,1)S(1)} %collective-permute-done.4.refs_1_.refs_3_, ...), custom_call_target="tpu_custom_call" | custom-call | flops 1024 | bytes 1024 | tf_op jit(solution)/shard_map/kernel_tile/pallas_call | solution.py:177
  39.7 2.4 %kernel_tile.5.refs_6_.refs_9_.refs_3_ = bf16[4,1024,512]{2,1,0:T(8,128)(2,1)S(1)} custom-call(bf16[2,272,512]{2,1,0:T(8,128)(2,1)S(1)} %collective-permute-done.12.point_ref.refs_6_, bf16[1024,512]{1,0:T(8,128)(2,1)S(1)} %copy-done, bf16[1024,512]{1,0:T(8,128)(2,1)S(1)} %collective-permute-done.11.refs_1_, ...), custom_call_target="tpu_custom_call" | custom-call | flops 1024 | bytes 1024 | tf_op jit(solution)/shard_map/kernel_tile/pallas_call | solution.py:177
  43.3 1.9 %collective-permute-start.14 = (bf16[16,1024]{1,0:T(8,128)(2,1)S(1)}, bf16[16,1024]{1,0:T(8,128)(2,1)S(1)}, u32[]{:S(2)}, u32[]{:S(2)}) collective-permute-start(bf16[16,1024]{1,0:T(8,128)(2,1)S(1)} %convert_element_type.33), channel_id=1, source_target_pairs={{0,12},{1,13},{2,14},{3,15},{4,8},{5,9},{6,10},{7,11},{8,4},{9,5},... | collective-permute-start | bytes 98312 | tf_op jit(solution)/shard_map/ppermute | solution.py:304
  45.8 1.9 %collective-permute-start.16 = (bf16[16,1024]{1,0:T(8,128)(2,1)S(1)}, bf16[16,1024]{1,0:T(8,128)(2,1)S(1)}, u32[]{:S(2)}, u32[]{:S(2)}) collective-permute-start(bf16[16,1024]{1,0:T(8,128)(2,1)S(1)} %convert_element_type.33), channel_id=1, source_target_pairs={{0,4},{1,5},{2,6},{3,7},{4,0},{5,1},{6,2},{7,3},{8,12},{9,13},{10,... | collective-permute-start | bytes 98312 | tf_op jit(solution)/shard_map/ppermute | solution.py:304
  47.7 1.6 %collective-permute-done.14.refs_2_ = bf16[16,1024]{1,0:T(8,128)(2,1)S(1)} collective-permute-done((bf16[16,1024]{1,0:T(8,128)(2,1)S(1)}, bf16[16,1024]{1,0:T(8,128)(2,1)S(1)}, u32[]{:S(2)}, u32[]{:S(2)}) %collective-permute-start.14) | collective-permute-done | bytes 32800 | tf_op jit(solution)/shard_map/ppermute | solution.py:304
  53.0 1.6 %collective-permute-start.18 = (f32[16,1024]{1,0:T(8,128)S(1)}, f32[16,1024]{1,0:T(8,128)S(1)}, u32[]{:S(2)}, u32[]{:S(2)}) collective-permute-start(f32[16,1024]{1,0:T(8,128)S(1)} %fusion.4), channel_id=1, source_target_pairs={{0,2},{1,3},{2,0},{3,1},{4,6},{5,7},{6,4},{7,5},{8,10},{9,11},{10,... | collective-permute-start | bytes 196616 | tf_op jit(solution)/shard_map/ppermute | solution.py:304
  54.6 2.8 %collective-permute-done.18 = f32[16,1024]{1,0:T(8,128)S(1)} collective-permute-done((f32[16,1024]{1,0:T(8,128)S(1)}, f32[16,1024]{1,0:T(8,128)S(1)}, u32[]{:S(2)}, u32[]{:S(2)}) %collective-permute-start.18) | collective-permute-done | bytes 65568 | tf_op jit(solution)/shard_map/ppermute | solution.py:304
  61.6 1.6 %collective-permute-start.21 = (bf16[4,16,1024]{2,1,0:T(8,128)(2,1)S(1)}, bf16[4,16,1024]{2,1,0:T(8,128)(2,1)S(1)}, u32[]{:S(2)}, u32[]{:S(2)}) collective-permute-start(bf16[4,16,1024]{2,1,0:T(8,128)(2,1)S(1)} %add_convert_fusion.after_ref), channel_id=1, source_target_pairs={{0,2},{1,3},{2,0},{3,1},{4,6},{5,7},{6,4},{7,5},{8,10},{9,11},{10,... | collective-permute-start | bytes 393224 | tf_op jit(solution)/shard_map/ppermute | solution.py:304
  64.4 2.7 %collective-permute-done.21 = bf16[4,16,1024]{2,1,0:T(8,128)(2,1)S(1)} collective-permute-done((bf16[4,16,1024]{2,1,0:T(8,128)(2,1)S(1)}, bf16[4,16,1024]{2,1,0:T(8,128)(2,1)S(1)}, u32[]{:S(2)}, u32[]{:S(2)}) %collective-permute-start.21) | collective-permute-done | bytes 131104 | tf_op jit(solution)/shard_map/ppermute | solution.py:304
  67.2 2.3 %collective-permute-start.22 = (bf16[16,1024]{1,0:T(8,128)(2,1)S(1)}, bf16[16,1024]{1,0:T(8,128)(2,1)S(1)}, u32[]{:S(2)}, u32[]{:S(2)}) collective-permute-start(bf16[16,1024]{1,0:T(8,128)(2,1)S(1)} %get-tuple-element.52), channel_id=1, source_target_pairs={{0,12},{1,13},{2,14},{3,15},{4,8},{5,9},{6,10},{7,11},{8,4},{9,5},... | collective-permute-start | bytes 98312 | tf_op jit(solution)/shard_map/ppermute | solution.py:304
  70.0 1.6 %collective-permute-start.24 = (bf16[16,1024]{1,0:T(8,128)(2,1)S(1)}, bf16[16,1024]{1,0:T(8,128)(2,1)S(1)}, u32[]{:S(2)}, u32[]{:S(2)}) collective-permute-start(bf16[16,1024]{1,0:T(8,128)(2,1)S(1)} %get-tuple-element.53), channel_id=1, source_target_pairs={{0,4},{1,5},{2,6},{3,7},{4,0},{5,1},{6,2},{7,3},{8,12},{9,13},{10,... | collective-permute-start | bytes 98312 | tf_op jit(solution)/shard_map/ppermute | solution.py:304
  71.6 1.3 %collective-permute-done.22 = bf16[16,1024]{1,0:T(8,128)(2,1)S(1)} collective-permute-done((bf16[16,1024]{1,0:T(8,128)(2,1)S(1)}, bf16[16,1024]{1,0:T(8,128)(2,1)S(1)}, u32[]{:S(2)}, u32[]{:S(2)}) %collective-permute-start.22) | collective-permute-done | bytes 32800 | tf_op jit(solution)/shard_map/ppermute | solution.py:304
  72.9 1.3 %collective-permute-done.23 = bf16[16,1024]{1,0:T(8,128)(2,1)S(1)} collective-permute-done((bf16[16,1024]{1,0:T(8,128)(2,1)S(1)}, bf16[16,1024]{1,0:T(8,128)(2,1)S(1)}, u32[]{:S(2)}, u32[]{:S(2)}) %collective-permute-start.23) | collective-permute-done | bytes 32800 | tf_op jit(solution)/shard_map/ppermute | solution.py:304
  (56 shorter events, 16.8 us)
Async XLA Ops:
  0.6 7.1 %collective-permute-start = (bf16[1,16,1024]{2,1,0:T(8,128)(2,1)}, bf16[1,16,1024]{2,1,0:T(8,128)(2,1)S(1)}, u32[]{:S(2)}, u32[]{:S(2)}) collective-permute-start(bf16[1,16,1024]{2,1,0:T(8,128)(2,1)} %bitcast.34), channel_id=1, source_target_pairs={{0,8},{1,9},{2,10},{3,11},{4,12},{5,13},{6,14},{7,15},{8,0},{9,1},... | collective-permute-start | bytes 98312 | tf_op jit(solution)/shard_map/ppermute | solution.py:304
  6.1 17.7 %collective-permute-start.3 = (bf16[512,512]{1,0:T(8,128)(2,1)S(1)}, bf16[512,512]{1,0:T(8,128)(2,1)S(1)}, u32[]{:S(2)}, u32[]{:S(2)}) collective-permute-start(bf16[512,512]{1,0:T(8,128)(2,1)S(1)} %get-tuple-element.32), channel_id=1, source_target_pairs={{0,2},{1,3},{2,0},{3,1},{4,6},{5,7},{6,4},{7,5},{8,10},{9,11},{10,... | collective-permute-start | bytes 1572872 | tf_op jit(solution)/shard_map/ppermute | solution.py:304
  7.7 4.3 %collective-permute-start.1 = (bf16[2,16,1024]{2,1,0:T(8,128)(2,1)S(1)}, bf16[2,16,1024]{2,1,0:T(8,128)(2,1)S(1)}, u32[]{:S(2)}, u32[]{:S(2)}) collective-permute-start(bf16[2,16,1024]{2,1,0:T(8,128)(2,1)S(1)} %pad_maximum_fusion.2), channel_id=1, source_target_pairs={{0,4},{1,5},{2,6},{3,7},{4,0},{5,1},{6,2},{7,3},{8,12},{9,13},{10,... | collective-permute-start | bytes 196616 | tf_op jit(solution)/shard_map/ppermute | solution.py:304
  9.3 26.5 %collective-permute-start.11 = (bf16[1024,512]{1,0:T(8,128)(2,1)}, bf16[1024,512]{1,0:T(8,128)(2,1)S(1)}, u32[]{:S(2)}, u32[]{:S(2)}) collective-permute-start(bf16[1024,512]{1,0:T(8,128)(2,1)} %refs_0_.3), channel_id=1, source_target_pairs={{0,1},{1,0},{2,3},{3,2},{4,5},{5,4},{6,7},{7,6},{8,9},{9,8},{10,11... | collective-permute-start | bytes 3145736 | tf_op jit(solution)/shard_map/ppermute | solution.py:304
  9.3 15.8 %collective-permute-start.5 = (bf16[1,272,512]{2,1,0:T(8,128)(2,1)S(1)}, bf16[1,272,512]{2,1,0:T(8,128)(2,1)S(1)}, u32[]{:S(2)}, u32[]{:S(2)}) collective-permute-start(bf16[1,272,512]{2,1,0:T(8,128)(2,1)S(1)} %get-tuple-element.35), channel_id=1, source_target_pairs={{0,8},{1,9},{2,10},{3,11},{4,12},{5,13},{6,14},{7,15},{8,0},{9,1},... | collective-permute-start | bytes 835592 | tf_op jit(solution)/shard_map/ppermute | solution.py:304
  12.0 11.8 %collective-permute-start.2 = (bf16[4,16,1024]{2,1,0:T(8,128)(2,1)S(1)}, bf16[4,16,1024]{2,1,0:T(8,128)(2,1)S(1)}, u32[]{:S(2)}, u32[]{:S(2)}) collective-permute-start(bf16[4,16,1024]{2,1,0:T(8,128)(2,1)S(1)} %pad_maximum_fusion.1.after_ref.beta_ref), channel_id=1, source_target_pairs={{0,2},{1,3},{2,0},{3,1},{4,6},{5,7},{6,4},{7,5},{8,10},{9,11},{10,... | collective-permute-start | bytes 393224 | tf_op jit(solution)/shard_map/ppermute | solution.py:304
  13.4 20.4 %collective-permute-start.4 = (bf16[512,512]{1,0:T(8,128)(2,1)S(1)}, bf16[512,512]{1,0:T(8,128)(2,1)S(1)}, u32[]{:S(2)}, u32[]{:S(2)}) collective-permute-start(bf16[512,512]{1,0:T(8,128)(2,1)S(1)} %get-tuple-element.34), channel_id=1, source_target_pairs={{0,2},{1,3},{2,0},{3,1},{4,6},{5,7},{6,4},{7,5},{8,10},{9,11},{10,... | collective-permute-start | bytes 1572872 | tf_op jit(solution)/shard_map/ppermute | solution.py:304
  23.8 1.8 %collective-permute-start.6 = (bf16[8,16,1024]{2,1,0:T(8,128)(2,1)S(1)}, bf16[8,16,1024]{2,1,0:T(8,128)(2,1)S(1)}, u32[]{:S(2)}, u32[]{:S(2)}) collective-permute-start(bf16[8,16,1024]{2,1,0:T(8,128)(2,1)S(1)} %pad_maximum_fusion), channel_id=1, source_target_pairs={{0,1},{1,0},{2,3},{3,2},{4,5},{5,4},{6,7},{7,6},{8,9},{9,8},{10,11... | collective-permute-start | bytes 786440 | tf_op jit(solution)/shard_map/ppermute | solution.py:304
  25.2 14.5 %collective-permute-start.12 = (bf16[2,272,512]{2,1,0:T(8,128)(2,1)S(1)}, bf16[2,272,512]{2,1,0:T(8,128)(2,1)S(1)}, u32[]{:S(2)}, u32[]{:S(2)}) collective-permute-start(bf16[2,272,512]{2,1,0:T(8,128)(2,1)S(1)} %constant_dynamic-update-slice_fusion.after_ref.point_ref.refs_5_), channel_id=1, source_target_pairs={{0,4},{1,5},{2,6},{3,7},{4,0},{5,1},{6,2},{7,3},{8,12},{9,13},{10,... | collective-permute-start | bytes 1671176 | tf_op jit(solution)/shard_map/ppermute | solution.py:304
  33.8 3.4 %collective-permute-start.10 = (bf16[512,512]{1,0:T(8,128)(2,1)S(1)}, bf16[512,512]{1,0:T(8,128)(2,1)S(1)}, u32[]{:S(2)}, u32[]{:S(2)}) collective-permute-start(bf16[512,512]{1,0:T(8,128)(2,1)S(1)} %collective-permute-done.4.refs_1_.refs_3_), channel_id=1, source_target_pairs={{0,1},{1,0},{2,3},{3,2},{4,5},{5,4},{6,7},{7,6},{8,9},{9,8},{10,11... | collective-permute-start | bytes 1572872 | tf_op jit(solution)/shard_map/ppermute | solution.py:304
  34.0 3.2 %collective-permute-start.9 = (bf16[512,512]{1,0:T(8,128)(2,1)S(1)}, bf16[512,512]{1,0:T(8,128)(2,1)S(1)}, u32[]{:S(2)}, u32[]{:S(2)}) collective-permute-start(bf16[512,512]{1,0:T(8,128)(2,1)S(1)} %collective-permute-done.3.refs_0_.refs_2_), channel_id=1, source_target_pairs={{0,1},{1,0},{2,3},{3,2},{4,5},{5,4},{6,7},{7,6},{8,9},{9,8},{10,11... | collective-permute-start | bytes 1572872 | tf_op jit(solution)/shard_map/ppermute | solution.py:304
  34.3 4.2 %collective-permute-start.8 = (bf16[16,1024]{1,0:T(8,128)(2,1)S(1)}, bf16[16,1024]{1,0:T(8,128)(2,1)S(1)}, u32[]{:S(2)}, u32[]{:S(2)}) collective-permute-start(bf16[16,1024]{1,0:T(8,128)(2,1)S(1)} %get-tuple-element.40.refs_2_.refs_0_), channel_id=1, source_target_pairs={{0,2},{1,3},{2,0},{3,1},{4,6},{5,7},{6,4},{7,5},{8,10},{9,11},{10,... | collective-permute-start | bytes 98312 | tf_op jit(solution)/shard_map/ppermute | solution.py:304
  35.9 6.2 %collective-permute-start.7 = (bf16[16,1024]{1,0:T(8,128)(2,1)S(1)}, bf16[16,1024]{1,0:T(8,128)(2,1)S(1)}, u32[]{:S(2)}, u32[]{:S(2)}) collective-permute-start(bf16[16,1024]{1,0:T(8,128)(2,1)S(1)} %get-tuple-element.40.refs_2_.refs_0_), channel_id=1, source_target_pairs={{0,1},{1,0},{2,3},{3,2},{4,5},{5,4},{6,7},{7,6},{8,9},{9,8},{10,11... | collective-permute-start | bytes 98312 | tf_op jit(solution)/shard_map/ppermute | solution.py:304
  39.7 2.4 %collective-permute-start.13 = (bf16[16,1024]{1,0:T(8,128)(2,1)S(1)}, bf16[16,1024]{1,0:T(8,128)(2,1)S(1)}, u32[]{:S(2)}, u32[]{:S(2)}) collective-permute-start(bf16[16,1024]{1,0:T(8,128)(2,1)S(1)} %collective-permute-done.8.refs_2_), channel_id=1, source_target_pairs={{0,1},{1,0},{2,3},{3,2},{4,5},{5,4},{6,7},{7,6},{8,9},{9,8},{10,11... | collective-permute-start | bytes 98312 | tf_op jit(solution)/shard_map/ppermute | solution.py:304
  43.3 6.0 %collective-permute-start.14 = (bf16[16,1024]{1,0:T(8,128)(2,1)S(1)}, bf16[16,1024]{1,0:T(8,128)(2,1)S(1)}, u32[]{:S(2)}, u32[]{:S(2)}) collective-permute-start(bf16[16,1024]{1,0:T(8,128)(2,1)S(1)} %convert_element_type.33), channel_id=1, source_target_pairs={{0,12},{1,13},{2,14},{3,15},{4,8},{5,9},{6,10},{7,11},{8,4},{9,5},... | collective-permute-start | bytes 98312 | tf_op jit(solution)/shard_map/ppermute | solution.py:304
  45.3 5.1 %collective-permute-start.15 = (bf16[16,1024]{1,0:T(8,128)(2,1)S(1)}, bf16[16,1024]{1,0:T(8,128)(2,1)S(1)}, u32[]{:S(2)}, u32[]{:S(2)}) collective-permute-start(bf16[16,1024]{1,0:T(8,128)(2,1)S(1)} %convert_element_type.33), channel_id=1, source_target_pairs={{0,8},{1,9},{2,10},{3,11},{4,12},{5,13},{6,14},{7,15},{8,0},{9,1},... | collective-permute-start | bytes 98312 | tf_op jit(solution)/shard_map/ppermute | solution.py:304
  45.8 4.6 %collective-permute-start.16 = (bf16[16,1024]{1,0:T(8,128)(2,1)S(1)}, bf16[16,1024]{1,0:T(8,128)(2,1)S(1)}, u32[]{:S(2)}, u32[]{:S(2)}) collective-permute-start(bf16[16,1024]{1,0:T(8,128)(2,1)S(1)} %convert_element_type.33), channel_id=1, source_target_pairs={{0,4},{1,5},{2,6},{3,7},{4,0},{5,1},{6,2},{7,3},{8,12},{9,13},{10,... | collective-permute-start | bytes 98312 | tf_op jit(solution)/shard_map/ppermute | solution.py:304
  53.0 4.4 %collective-permute-start.18 = (f32[16,1024]{1,0:T(8,128)S(1)}, f32[16,1024]{1,0:T(8,128)S(1)}, u32[]{:S(2)}, u32[]{:S(2)}) collective-permute-start(f32[16,1024]{1,0:T(8,128)S(1)} %fusion.4), channel_id=1, source_target_pairs={{0,2},{1,3},{2,0},{3,1},{4,6},{5,7},{6,4},{7,5},{8,10},{9,11},{10,... | collective-permute-start | bytes 196616 | tf_op jit(solution)/shard_map/ppermute | solution.py:304
  58.6 2.9 %collective-permute-start.19 = (f32[4,16,1024]{2,1,0:T(8,128)S(1)}, f32[4,16,1024]{2,1,0:T(8,128)S(1)}, u32[]{:S(2)}, u32[]{:S(2)}) collective-permute-start(f32[4,16,1024]{2,1,0:T(8,128)S(1)} %gradient_terms.4.after_ref), channel_id=1, source_target_pairs={{0,1},{1,0},{2,3},{3,2},{4,5},{5,4},{6,7},{7,6},{8,9},{9,8},{10,11... | collective-permute-start | bytes 786440 | tf_op jit(solution)/shard_map/ppermute | solution.py:304
  59.8 4.6 %collective-permute-start.20 = (f32[4,16,1024]{2,1,0:T(8,128)S(1)}, f32[4,16,1024]{2,1,0:T(8,128)S(1)}, u32[]{:S(2)}, u32[]{:S(2)}) collective-permute-start(f32[4,16,1024]{2,1,0:T(8,128)S(1)} %gradient_terms.5.after_ref), channel_id=1, source_target_pairs={{0,1},{1,0},{2,3},{3,2},{4,5},{5,4},{6,7},{7,6},{8,9},{9,8},{10,11... | collective-permute-start | bytes 786440 | tf_op jit(solution)/shard_map/ppermute | solution.py:304
  61.6 5.5 %collective-permute-start.21 = (bf16[4,16,1024]{2,1,0:T(8,128)(2,1)S(1)}, bf16[4,16,1024]{2,1,0:T(8,128)(2,1)S(1)}, u32[]{:S(2)}, u32[]{:S(2)}) collective-permute-start(bf16[4,16,1024]{2,1,0:T(8,128)(2,1)S(1)} %add_convert_fusion.after_ref), channel_id=1, source_target_pairs={{0,2},{1,3},{2,0},{3,1},{4,6},{5,7},{6,4},{7,5},{8,10},{9,11},{10,... | collective-permute-start | bytes 393224 | tf_op jit(solution)/shard_map/ppermute | solution.py:304
  67.2 5.8 %collective-permute-start.22 = (bf16[16,1024]{1,0:T(8,128)(2,1)S(1)}, bf16[16,1024]{1,0:T(8,128)(2,1)S(1)}, u32[]{:S(2)}, u32[]{:S(2)}) collective-permute-start(bf16[16,1024]{1,0:T(8,128)(2,1)S(1)} %get-tuple-element.52), channel_id=1, source_target_pairs={{0,12},{1,13},{2,14},{3,15},{4,8},{5,9},{6,10},{7,11},{8,4},{9,5},... | collective-permute-start | bytes 98312 | tf_op jit(solution)/shard_map/ppermute | solution.py:304
  69.4 4.8 %collective-permute-start.23 = (bf16[16,1024]{1,0:T(8,128)(2,1)S(1)}, bf16[16,1024]{1,0:T(8,128)(2,1)S(1)}, u32[]{:S(2)}, u32[]{:S(2)}) collective-permute-start(bf16[16,1024]{1,0:T(8,128)(2,1)S(1)} %get-tuple-element.54), channel_id=1, source_target_pairs={{0,8},{1,9},{2,10},{3,11},{4,12},{5,13},{6,14},{7,15},{8,0},{9,1},... | collective-permute-start | bytes 98312 | tf_op jit(solution)/shard_map/ppermute | solution.py:304
  70.0 4.3 %collective-permute-start.24 = (bf16[16,1024]{1,0:T(8,128)(2,1)S(1)}, bf16[16,1024]{1,0:T(8,128)(2,1)S(1)}, u32[]{:S(2)}, u32[]{:S(2)}) collective-permute-start(bf16[16,1024]{1,0:T(8,128)(2,1)S(1)} %get-tuple-element.53), channel_id=1, source_target_pairs={{0,4},{1,5},{2,6},{3,7},{4,0},{5,1},{6,2},{7,3},{8,12},{9,13},{10,... | collective-permute-start | bytes 98312 | tf_op jit(solution)/shard_map/ppermute | solution.py:304
  (3 other events, 28.2 us)

commit v7 on v6

--- a/solution.py
+++ b/solution.py
@@ -11,7 +11,7 @@
 F32 = jnp.float32
 ROWS_BY_ROWS = (((1,), (1,)), ((), ()))
 MIB = 1 << 20
-IN_FLIGHT = 3
+IN_FLIGHT = 4
 
 
 def params(mib):

time: 75.1 us -> 75.5 us (level)
  transfers between devices with their start and end apart: 25 -> 25, of which waited for: 11 -> 12; matrix products, arithmetic and copies ran while one was open for 0% -> 0% of each run, Pallas kernels for 34% -> 35%
where the time goes in v7:
time: 75.5 us; the launch traced here: 75.3 us
  Pallas kernels  29.9 us (40%)
  starting transfers between devices  26.3 us (35%)
  waiting for transfers between devices  17.4 us (23%)
  other arithmetic  0.82 us (1%)
  between operations  0.82 us (1%)
    ppermute x25, starting transfers between devices, swap(): lax.ppermute(array, 'pts', [(index, index ^ mask) for index in range(devi...  26.3 us
    ppermute x25, waiting for transfers between devices, swap(): lax.ppermute(array, 'pts', [(index, index ^ mask) for index in range(devi...  17.4 us
    pallas_call x2, Pallas kernels, alpha_sum(): pl.pallas_call(body, out_shape=[jax.ShapeDtypeStruct((classes, rows), BF1...  15.1 us
    pallas_call x3, Pallas kernels, kernel_tile(): pl.pallas_call(body, out_shape=pltpu.VMEM((len(centre_blocks), local, tot...  5.04 us
    pallas_call x4, Pallas kernels, gradient_terms(): pl.pallas_call(body, out_shape=jax.ShapeDtypeStruct((count, classes, widt...  4.79 us
    pallas_call x2, Pallas kernels, kernel_gradient(): pl.pallas_call(body, out_shape=[jax.ShapeDtypeStruct((n_parts, classes, l...  2.41 us
  transfers between devices with their start and end apart: 25, of which 12 were waited for; matrix products, arithmetic and copies ran while one was open for 0% of the time, Pallas kernels for 35%

profile of v7, /device:TPU:0, one launch (start us, length us, event | category | flops | bytes accessed | tf_op | source)
XLA Modules:
  0.0 75.3 jit_solution(16968090812400760387)
XLA Ops:
  0.6 4.1 %collective-permute-start = (bf16[1,16,1024]{2,1,0:T(8,128)(2,1)}, bf16[1,16,1024]{2,1,0:T(8,128)(2,1)S(1)}, u32[]{:S(2)}, u32[]{:S(2)}) collective-permute-start(bf16[1,16,1024]{2,1,0:T(8,128)(2,1)} %bitcast.34), channel_id=1, source_target_pairs={{0,8},{1,9},{2,10},{3,11},{4,12},{5,13},{6,14},{7,15},{8,0},{9,1},... | collective-permute-start | bytes 98312 | tf_op jit(solution)/shard_map/ppermute | solution.py:304
  4.7 1.4 %prepare.1 = (bf16[1,272,512]{2,1,0:T(8,128)(2,1)S(1)}, bf16[512,512]{1,0:T(8,128)(2,1)S(1)}, bf16[512,512]{1,0:T(8,128)(2,1)S(1)}, bf16[1,16,1024]{2,1,0:T(8,128)(2,1)S(1)}) custom-call(bf16[256,512]{1,0:T(8,128)(2,1)} %points_ref.1, s32[1,256]{1,0:T(1,128)} %bitcast.36, bf16[1024,512]{1,0:T(8,128)(2,1)} %refs_0_.3, bf16[16,1024]{1,0:T(8,128)(2,1)} %bitcast.35), custom_call_target="tpu_custom_call" | custom-call | flops 1024 | bytes 2097152 | tf_op jit(solution)/shard_map/prepare/pallas_call | solution.py:119
  6.1 1.6 %collective-permute-start.3 = (bf16[512,512]{1,0:T(8,128)(2,1)S(1)}, bf16[512,512]{1,0:T(8,128)(2,1)S(1)}, u32[]{:S(2)}, u32[]{:S(2)}) collective-permute-start(bf16[512,512]{1,0:T(8,128)(2,1)S(1)} %get-tuple-element.32), channel_id=1, source_target_pairs={{0,2},{1,3},{2,0},{3,1},{4,6},{5,7},{6,4},{7,5},{8,10},{9,11},{10,... | collective-permute-start | bytes 1572872 | tf_op jit(solution)/shard_map/ppermute | solution.py:304
  7.7 1.6 %collective-permute-start.1 = (bf16[2,16,1024]{2,1,0:T(8,128)(2,1)S(1)}, bf16[2,16,1024]{2,1,0:T(8,128)(2,1)S(1)}, u32[]{:S(2)}, u32[]{:S(2)}) collective-permute-start(bf16[2,16,1024]{2,1,0:T(8,128)(2,1)S(1)} %pad_maximum_fusion.2), channel_id=1, source_target_pairs={{0,4},{1,5},{2,6},{3,7},{4,0},{5,1},{6,2},{7,3},{8,12},{9,13},{10,... | collective-permute-start | bytes 196616 | tf_op jit(solution)/shard_map/ppermute | solution.py:304
  9.3 2.3 %collective-permute-start.5 = (bf16[1,272,512]{2,1,0:T(8,128)(2,1)S(1)}, bf16[1,272,512]{2,1,0:T(8,128)(2,1)S(1)}, u32[]{:S(2)}, u32[]{:S(2)}) collective-permute-start(bf16[1,272,512]{2,1,0:T(8,128)(2,1)S(1)} %get-tuple-element.35), channel_id=1, source_target_pairs={{0,8},{1,9},{2,10},{3,11},{4,12},{5,13},{6,14},{7,15},{8,0},{9,1},... | collective-permute-start | bytes 835592 | tf_op jit(solution)/shard_map/ppermute | solution.py:304
  12.0 1.3 %collective-permute-start.2 = (bf16[4,16,1024]{2,1,0:T(8,128)(2,1)S(1)}, bf16[4,16,1024]{2,1,0:T(8,128)(2,1)S(1)}, u32[]{:S(2)}, u32[]{:S(2)}) collective-permute-start(bf16[4,16,1024]{2,1,0:T(8,128)(2,1)S(1)} %pad_maximum_fusion.1.after_ref.beta_ref), channel_id=1, source_target_pairs={{0,2},{1,3},{2,0},{3,1},{4,6},{5,7},{6,4},{7,5},{8,10},{9,11},{10,... | collective-permute-start | bytes 393224 | tf_op jit(solution)/shard_map/ppermute | solution.py:304
  14.1 6.2 %alpha_sum.2 = (f32[16,1024]{1,0:T(8,128)S(1)}, bf16[8,1024,1024]{2,1,0:T(8,128)(2,1)S(1)}) custom-call(s32[1]{0:T(128)} %bitcast.3.me_ref, bf16[1024,16384]{1,0:T(8,128)(2,1)} %tri_ref.3, bf16[4,16,1024]{2,1,0:T(8,128)(2,1)S(1)} %pad_maximum_fusion.1.after_ref.beta_ref, bf16[4,16,1024]{2,1,0:T(8,128)(2,1)S(1)} %pad_maximum_fusion.1.after_ref.beta_ref), custom_call_target="tpu_custom_call" | custom-call | flops 2147483648 | bytes 16777216 | tf_op jit(solution)/shard_map/alpha_sum/pallas_call | solution.py:81
  20.4 3.5 %collective-permute-done.2.refs_2_ = bf16[4,16,1024]{2,1,0:T(8,128)(2,1)S(1)} collective-permute-done((bf16[4,16,1024]{2,1,0:T(8,128)(2,1)S(1)}, bf16[4,16,1024]{2,1,0:T(8,128)(2,1)S(1)}, u32[]{:S(2)}, u32[]{:S(2)}) %collective-permute-start.2) | collective-permute-done | bytes 131104 | tf_op jit(solution)/shard_map/ppermute | solution.py:304
  24.0 1.2 %collective-permute-done.5 = bf16[1,272,512]{2,1,0:T(8,128)(2,1)S(1)} collective-permute-done((bf16[1,272,512]{2,1,0:T(8,128)(2,1)S(1)}, bf16[1,272,512]{2,1,0:T(8,128)(2,1)S(1)}, u32[]{:S(2)}, u32[]{:S(2)}) %collective-permute-start.5) | collective-permute-done | bytes 278560 | tf_op jit(solution)/shard_map/ppermute | solution.py:304
  25.6 8.9 %alpha_sum.3 = (bf16[16,1024]{1,0:T(8,128)(2,1)S(1)}, bf16[8,1024,1024]{2,1,0:T(8,128)(2,1)S(1)}) custom-call(s32[1]{0:T(128)} %bitcast.3.me_ref, bf16[1024,16384]{1,0:T(8,128)(2,1)} %tri_ref.3, bf16[2,272,512]{2,1,0:T(8,128)(2,1)S(1)} %constant_dynamic-update-slice_fusion.after_ref.point_ref.refs_5_, ...), custom_call_target="tpu_custom_call" | custom-call | flops 2147483648 | bytes 16777216 | tf_op jit(solution)/shard_map/alpha_sum/pallas_call | solution.py:81
  35.1 1.5 %collective-permute-start.8 = (bf16[16,1024]{1,0:T(8,128)(2,1)S(1)}, bf16[16,1024]{1,0:T(8,128)(2,1)S(1)}, u32[]{:S(2)}, u32[]{:S(2)}) collective-permute-start(bf16[16,1024]{1,0:T(8,128)(2,1)S(1)} %get-tuple-element.40.refs_2_.refs_0_), channel_id=1, source_target_pairs={{0,2},{1,3},{2,0},{3,1},{4,6},{5,7},{6,4},{7,5},{8,10},{9,11},{10,... | collective-permute-start | bytes 98312 | tf_op jit(solution)/shard_map/ppermute | solution.py:304
  36.7 1.3 %kernel_tile.3.refs_4_.refs_7_.refs_1_ = bf16[2,1024,512]{2,1,0:T(8,128)(2,1)S(1)} custom-call(bf16[2,272,512]{2,1,0:T(8,128)(2,1)S(1)} %constant_dynamic-update-slice_fusion.after_ref.point_ref.refs_5_, bf16[1024,512]{1,0:T(8,128)(2,1)S(1)} %copy-done, bf16[1024,512]{1,0:T(8,128)(2,1)S(1)} %collective-permute-done.11.refs_1_, ...), custom_call_target="tpu_custom_call" | custom-call | flops 1024 | bytes 1024 | tf_op jit(solution)/shard_map/kernel_tile/pallas_call | solution.py:177
  38.0 1.3 %kernel_tile.4.refs_6_.refs_5_.refs_8_.refs_2_ = bf16[2,1024,512]{2,1,0:T(8,128)(2,1)S(1)} custom-call(bf16[2,272,512]{2,1,0:T(8,128)(2,1)S(1)} %constant_dynamic-update-slice_fusion.after_ref.point_ref.refs_5_, bf16[512,512]{1,0:T(8,128)(2,1)S(1)} %collective-permute-done.3.refs_0_.refs_2_, bf16[512,512]{1,0:T(8,128)(2,1)S(1)} %collective-permute-done.4.refs_1_.refs_3_, ...), custom_call_target="tpu_custom_call" | custom-call | flops 1024 | bytes 1024 | tf_op jit(solution)/shard_map/kernel_tile/pallas_call | solution.py:177
  39.9 2.4 %kernel_tile.5.refs_6_.refs_9_.refs_3_ = bf16[4,1024,512]{2,1,0:T(8,128)(2,1)S(1)} custom-call(bf16[2,272,512]{2,1,0:T(8,128)(2,1)S(1)} %collective-permute-done.12.point_ref.refs_6_, bf16[1024,512]{1,0:T(8,128)(2,1)S(1)} %copy-done, bf16[1024,512]{1,0:T(8,128)(2,1)S(1)} %collective-permute-done.11.refs_1_, ...), custom_call_target="tpu_custom_call" | custom-call | flops 1024 | bytes 1024 | tf_op jit(solution)/shard_map/kernel_tile/pallas_call | solution.py:177
  43.6 1.8 %collective-permute-start.14 = (bf16[16,1024]{1,0:T(8,128)(2,1)S(1)}, bf16[16,1024]{1,0:T(8,128)(2,1)S(1)}, u32[]{:S(2)}, u32[]{:S(2)}) collective-permute-start(bf16[16,1024]{1,0:T(8,128)(2,1)S(1)} %convert_element_type.33), channel_id=1, source_target_pairs={{0,12},{1,13},{2,14},{3,15},{4,8},{5,9},{6,10},{7,11},{8,4},{9,5},... | collective-permute-start | bytes 98312 | tf_op jit(solution)/shard_map/ppermute | solution.py:304
  46.4 1.5 %collective-permute-start.16 = (bf16[16,1024]{1,0:T(8,128)(2,1)S(1)}, bf16[16,1024]{1,0:T(8,128)(2,1)S(1)}, u32[]{:S(2)}, u32[]{:S(2)}) collective-permute-start(bf16[16,1024]{1,0:T(8,128)(2,1)S(1)} %convert_element_type.33), channel_id=1, source_target_pairs={{0,4},{1,5},{2,6},{3,7},{4,0},{5,1},{6,2},{7,3},{8,12},{9,13},{10,... | collective-permute-start | bytes 98312 | tf_op jit(solution)/shard_map/ppermute | solution.py:304
  48.0 1.5 %collective-permute-done.14.refs_2_ = bf16[16,1024]{1,0:T(8,128)(2,1)S(1)} collective-permute-done((bf16[16,1024]{1,0:T(8,128)(2,1)S(1)}, bf16[16,1024]{1,0:T(8,128)(2,1)S(1)}, u32[]{:S(2)}, u32[]{:S(2)}) %collective-permute-start.14) | collective-permute-done | bytes 32800 | tf_op jit(solution)/shard_map/ppermute | solution.py:304
  54.5 3.2 %collective-permute-done.18 = f32[16,1024]{1,0:T(8,128)S(1)} collective-permute-done((f32[16,1024]{1,0:T(8,128)S(1)}, f32[16,1024]{1,0:T(8,128)S(1)}, u32[]{:S(2)}, u32[]{:S(2)}) %collective-permute-start.18) | collective-permute-done | bytes 65568 | tf_op jit(solution)/shard_map/ppermute | solution.py:304
  59.0 1.2 %gradient_terms.5.after_ref = f32[4,16,1024]{2,1,0:T(8,128)S(1)} custom-call(f32[4,16,1024]{2,1,0:T(8,128)S(1)} %gradient_terms.4.after_ref, bf16[16,1024]{1,0:T(8,128)(2,1)S(1)} %fusion.8.after_ref.grad_ref, bf16[8,1024,1024]{2,1,0:T(8,128)(2,1)S(1)} %get-tuple-element.48.block_ref), custom_call_target="tpu_custom_call" | custom-call | flops 1073741824 | bytes 1024 | tf_op jit(solution)/shard_map/gradient_terms/pallas_call | solution.py:144
  64.3 3.1 %collective-permute-done.21 = bf16[4,16,1024]{2,1,0:T(8,128)(2,1)S(1)} collective-permute-done((bf16[4,16,1024]{2,1,0:T(8,128)(2,1)S(1)}, bf16[4,16,1024]{2,1,0:T(8,128)(2,1)S(1)}, u32[]{:S(2)}, u32[]{:S(2)}) %collective-permute-start.21) | collective-permute-done | bytes 131104 | tf_op jit(solution)/shard_map/ppermute | solution.py:304
  67.5 2.3 %collective-permute-start.22 = (bf16[16,1024]{1,0:T(8,128)(2,1)S(1)}, bf16[16,1024]{1,0:T(8,128)(2,1)S(1)}, u32[]{:S(2)}, u32[]{:S(2)}) collective-permute-start(bf16[16,1024]{1,0:T(8,128)(2,1)S(1)} %get-tuple-element.52), channel_id=1, source_target_pairs={{0,12},{1,13},{2,14},{3,15},{4,8},{5,9},{6,10},{7,11},{8,4},{9,5},... | collective-permute-start | bytes 98312 | tf_op jit(solution)/shard_map/ppermute | solution.py:304
  70.2 1.7 %collective-permute-start.24 = (bf16[16,1024]{1,0:T(8,128)(2,1)S(1)}, bf16[16,1024]{1,0:T(8,128)(2,1)S(1)}, u32[]{:S(2)}, u32[]{:S(2)}) collective-permute-start(bf16[16,1024]{1,0:T(8,128)(2,1)S(1)} %get-tuple-element.53), channel_id=1, source_target_pairs={{0,4},{1,5},{2,6},{3,7},{4,0},{5,1},{6,2},{7,3},{8,12},{9,13},{10,... | collective-permute-start | bytes 98312 | tf_op jit(solution)/shard_map/ppermute | solution.py:304
  72.0 1.3 %collective-permute-done.22 = bf16[16,1024]{1,0:T(8,128)(2,1)S(1)} collective-permute-done((bf16[16,1024]{1,0:T(8,128)(2,1)S(1)}, bf16[16,1024]{1,0:T(8,128)(2,1)S(1)}, u32[]{:S(2)}, u32[]{:S(2)}) %collective-permute-start.22) | collective-permute-done | bytes 32800 | tf_op jit(solution)/shard_map/ppermute | solution.py:304
  73.3 1.4 %collective-permute-done.23 = bf16[16,1024]{1,0:T(8,128)(2,1)S(1)} collective-permute-done((bf16[16,1024]{1,0:T(8,128)(2,1)S(1)}, bf16[16,1024]{1,0:T(8,128)(2,1)S(1)}, u32[]{:S(2)}, u32[]{:S(2)}) %collective-permute-start.23) | collective-permute-done | bytes 32800 | tf_op jit(solution)/shard_map/ppermute | solution.py:304
  (56 shorter events, 16.7 us)
Async XLA Ops:
  0.6 7.1 %collective-permute-start = (bf16[1,16,1024]{2,1,0:T(8,128)(2,1)}, bf16[1,16,1024]{2,1,0:T(8,128)(2,1)S(1)}, u32[]{:S(2)}, u32[]{:S(2)}) collective-permute-start(bf16[1,16,1024]{2,1,0:T(8,128)(2,1)} %bitcast.34), channel_id=1, source_target_pairs={{0,8},{1,9},{2,10},{3,11},{4,12},{5,13},{6,14},{7,15},{8,0},{9,1},... | collective-permute-start | bytes 98312 | tf_op jit(solution)/shard_map/ppermute | solution.py:304
  6.1 17.7 %collective-permute-start.3 = (bf16[512,512]{1,0:T(8,128)(2,1)S(1)}, bf16[512,512]{1,0:T(8,128)(2,1)S(1)}, u32[]{:S(2)}, u32[]{:S(2)}) collective-permute-start(bf16[512,512]{1,0:T(8,128)(2,1)S(1)} %get-tuple-element.32), channel_id=1, source_target_pairs={{0,2},{1,3},{2,0},{3,1},{4,6},{5,7},{6,4},{7,5},{8,10},{9,11},{10,... | collective-permute-start | bytes 1572872 | tf_op jit(solution)/shard_map/ppermute | solution.py:304
  7.7 4.3 %collective-permute-start.1 = (bf16[2,16,1024]{2,1,0:T(8,128)(2,1)S(1)}, bf16[2,16,1024]{2,1,0:T(8,128)(2,1)S(1)}, u32[]{:S(2)}, u32[]{:S(2)}) collective-permute-start(bf16[2,16,1024]{2,1,0:T(8,128)(2,1)S(1)} %pad_maximum_fusion.2), channel_id=1, source_target_pairs={{0,4},{1,5},{2,6},{3,7},{4,0},{5,1},{6,2},{7,3},{8,12},{9,13},{10,... | collective-permute-start | bytes 196616 | tf_op jit(solution)/shard_map/ppermute | solution.py:304
  9.3 27.3 %collective-permute-start.11 = (bf16[1024,512]{1,0:T(8,128)(2,1)}, bf16[1024,512]{1,0:T(8,128)(2,1)S(1)}, u32[]{:S(2)}, u32[]{:S(2)}) collective-permute-start(bf16[1024,512]{1,0:T(8,128)(2,1)} %refs_0_.3), channel_id=1, source_target_pairs={{0,1},{1,0},{2,3},{3,2},{4,5},{5,4},{6,7},{7,6},{8,9},{9,8},{10,11... | collective-permute-start | bytes 3145736 | tf_op jit(solution)/shard_map/ppermute | solution.py:304
  9.3 15.8 %collective-permute-start.5 = (bf16[1,272,512]{2,1,0:T(8,128)(2,1)S(1)}, bf16[1,272,512]{2,1,0:T(8,128)(2,1)S(1)}, u32[]{:S(2)}, u32[]{:S(2)}) collective-permute-start(bf16[1,272,512]{2,1,0:T(8,128)(2,1)S(1)} %get-tuple-element.35), channel_id=1, source_target_pairs={{0,8},{1,9},{2,10},{3,11},{4,12},{5,13},{6,14},{7,15},{8,0},{9,1},... | collective-permute-start | bytes 835592 | tf_op jit(solution)/shard_map/ppermute | solution.py:304
  12.0 11.8 %collective-permute-start.2 = (bf16[4,16,1024]{2,1,0:T(8,128)(2,1)S(1)}, bf16[4,16,1024]{2,1,0:T(8,128)(2,1)S(1)}, u32[]{:S(2)}, u32[]{:S(2)}) collective-permute-start(bf16[4,16,1024]{2,1,0:T(8,128)(2,1)S(1)} %pad_maximum_fusion.1.after_ref.beta_ref), channel_id=1, source_target_pairs={{0,2},{1,3},{2,0},{3,1},{4,6},{5,7},{6,4},{7,5},{8,10},{9,11},{10,... | collective-permute-start | bytes 393224 | tf_op jit(solution)/shard_map/ppermute | solution.py:304
  13.4 21.2 %collective-permute-start.4 = (bf16[512,512]{1,0:T(8,128)(2,1)S(1)}, bf16[512,512]{1,0:T(8,128)(2,1)S(1)}, u32[]{:S(2)}, u32[]{:S(2)}) collective-permute-start(bf16[512,512]{1,0:T(8,128)(2,1)S(1)} %get-tuple-element.34), channel_id=1, source_target_pairs={{0,2},{1,3},{2,0},{3,1},{4,6},{5,7},{6,4},{7,5},{8,10},{9,11},{10,... | collective-permute-start | bytes 1572872 | tf_op jit(solution)/shard_map/ppermute | solution.py:304
  23.8 1.8 %collective-permute-start.6 = (bf16[8,16,1024]{2,1,0:T(8,128)(2,1)S(1)}, bf16[8,16,1024]{2,1,0:T(8,128)(2,1)S(1)}, u32[]{:S(2)}, u32[]{:S(2)}) collective-permute-start(bf16[8,16,1024]{2,1,0:T(8,128)(2,1)S(1)} %pad_maximum_fusion), channel_id=1, source_target_pairs={{0,1},{1,0},{2,3},{3,2},{4,5},{5,4},{6,7},{7,6},{8,9},{9,8},{10,11... | collective-permute-start | bytes 786440 | tf_op jit(solution)/shard_map/ppermute | solution.py:304
  25.2 14.5 %collective-permute-start.12 = (bf16[2,272,512]{2,1,0:T(8,128)(2,1)S(1)}, bf16[2,272,512]{2,1,0:T(8,128)(2,1)S(1)}, u32[]{:S(2)}, u32[]{:S(2)}) collective-permute-start(bf16[2,272,512]{2,1,0:T(8,128)(2,1)S(1)} %constant_dynamic-update-slice_fusion.after_ref.point_ref.refs_5_), channel_id=1, source_target_pairs={{0,4},{1,5},{2,6},{3,7},{4,0},{5,1},{6,2},{7,3},{8,12},{9,13},{10,... | collective-permute-start | bytes 1671176 | tf_op jit(solution)/shard_map/ppermute | solution.py:304
  34.6 3.4 %collective-permute-start.10 = (bf16[512,512]{1,0:T(8,128)(2,1)S(1)}, bf16[512,512]{1,0:T(8,128)(2,1)S(1)}, u32[]{:S(2)}, u32[]{:S(2)}) collective-permute-start(bf16[512,512]{1,0:T(8,128)(2,1)S(1)} %collective-permute-done.4.refs_1_.refs_3_), channel_id=1, source_target_pairs={{0,1},{1,0},{2,3},{3,2},{4,5},{5,4},{6,7},{7,6},{8,9},{9,8},{10,11... | collective-permute-start | bytes 1572872 | tf_op jit(solution)/shard_map/ppermute | solution.py:304
  34.8 3.2 %collective-permute-start.9 = (bf16[512,512]{1,0:T(8,128)(2,1)S(1)}, bf16[512,512]{1,0:T(8,128)(2,1)S(1)}, u32[]{:S(2)}, u32[]{:S(2)}) collective-permute-start(bf16[512,512]{1,0:T(8,128)(2,1)S(1)} %collective-permute-done.3.refs_0_.refs_2_), channel_id=1, source_target_pairs={{0,1},{1,0},{2,3},{3,2},{4,5},{5,4},{6,7},{7,6},{8,9},{9,8},{10,11... | collective-permute-start | bytes 1572872 | tf_op jit(solution)/shard_map/ppermute | solution.py:304
  35.1 4.2 %collective-permute-start.8 = (bf16[16,1024]{1,0:T(8,128)(2,1)S(1)}, bf16[16,1024]{1,0:T(8,128)(2,1)S(1)}, u32[]{:S(2)}, u32[]{:S(2)}) collective-permute-start(bf16[16,1024]{1,0:T(8,128)(2,1)S(1)} %get-tuple-element.40.refs_2_.refs_0_), channel_id=1, source_target_pairs={{0,2},{1,3},{2,0},{3,1},{4,6},{5,7},{6,4},{7,5},{8,10},{9,11},{10,... | collective-permute-start | bytes 98312 | tf_op jit(solution)/shard_map/ppermute | solution.py:304
  36.7 5.7 %collective-permute-start.7 = (bf16[16,1024]{1,0:T(8,128)(2,1)S(1)}, bf16[16,1024]{1,0:T(8,128)(2,1)S(1)}, u32[]{:S(2)}, u32[]{:S(2)}) collective-permute-start(bf16[16,1024]{1,0:T(8,128)(2,1)S(1)} %get-tuple-element.40.refs_2_.refs_0_), channel_id=1, source_target_pairs={{0,1},{1,0},{2,3},{3,2},{4,5},{5,4},{6,7},{7,6},{8,9},{9,8},{10,11... | collective-permute-start | bytes 98312 | tf_op jit(solution)/shard_map/ppermute | solution.py:304
  39.7 2.7 %collective-permute-start.13 = (bf16[16,1024]{1,0:T(8,128)(2,1)S(1)}, bf16[16,1024]{1,0:T(8,128)(2,1)S(1)}, u32[]{:S(2)}, u32[]{:S(2)}) collective-permute-start(bf16[16,1024]{1,0:T(8,128)(2,1)S(1)} %collective-permute-done.8.refs_2_), channel_id=1, source_target_pairs={{0,1},{1,0},{2,3},{3,2},{4,5},{5,4},{6,7},{7,6},{8,9},{9,8},{10,11... | collective-permute-start | bytes 98312 | tf_op jit(solution)/shard_map/ppermute | solution.py:304
  43.6 6.0 %collective-permute-start.14 = (bf16[16,1024]{1,0:T(8,128)(2,1)S(1)}, bf16[16,1024]{1,0:T(8,128)(2,1)S(1)}, u32[]{:S(2)}, u32[]{:S(2)}) collective-permute-start(bf16[16,1024]{1,0:T(8,128)(2,1)S(1)} %convert_element_type.33), channel_id=1, source_target_pairs={{0,12},{1,13},{2,14},{3,15},{4,8},{5,9},{6,10},{7,11},{8,4},{9,5},... | collective-permute-start | bytes 98312 | tf_op jit(solution)/shard_map/ppermute | solution.py:304
  45.3 5.1 %collective-permute-start.15 = (bf16[16,1024]{1,0:T(8,128)(2,1)S(1)}, bf16[16,1024]{1,0:T(8,128)(2,1)S(1)}, u32[]{:S(2)}, u32[]{:S(2)}) collective-permute-start(bf16[16,1024]{1,0:T(8,128)(2,1)S(1)} %convert_element_type.33), channel_id=1, source_target_pairs={{0,8},{1,9},{2,10},{3,11},{4,12},{5,13},{6,14},{7,15},{8,0},{9,1},... | collective-permute-start | bytes 98312 | tf_op jit(solution)/shard_map/ppermute | solution.py:304
  46.4 4.3 %collective-permute-start.16 = (bf16[16,1024]{1,0:T(8,128)(2,1)S(1)}, bf16[16,1024]{1,0:T(8,128)(2,1)S(1)}, u32[]{:S(2)}, u32[]{:S(2)}) collective-permute-start(bf16[16,1024]{1,0:T(8,128)(2,1)S(1)} %convert_element_type.33), channel_id=1, source_target_pairs={{0,4},{1,5},{2,6},{3,7},{4,0},{5,1},{6,2},{7,3},{8,12},{9,13},{10,... | collective-permute-start | bytes 98312 | tf_op jit(solution)/shard_map/ppermute | solution.py:304
  53.4 4.4 %collective-permute-start.18 = (f32[16,1024]{1,0:T(8,128)S(1)}, f32[16,1024]{1,0:T(8,128)S(1)}, u32[]{:S(2)}, u32[]{:S(2)}) collective-permute-start(f32[16,1024]{1,0:T(8,128)S(1)} %fusion.4), channel_id=1, source_target_pairs={{0,2},{1,3},{2,0},{3,1},{4,6},{5,7},{6,4},{7,5},{8,10},{9,11},{10,... | collective-permute-start | bytes 196616 | tf_op jit(solution)/shard_map/ppermute | solution.py:304
  59.0 2.9 %collective-permute-start.19 = (f32[4,16,1024]{2,1,0:T(8,128)S(1)}, f32[4,16,1024]{2,1,0:T(8,128)S(1)}, u32[]{:S(2)}, u32[]{:S(2)}) collective-permute-start(f32[4,16,1024]{2,1,0:T(8,128)S(1)} %gradient_terms.4.after_ref), channel_id=1, source_target_pairs={{0,1},{1,0},{2,3},{3,2},{4,5},{5,4},{6,7},{7,6},{8,9},{9,8},{10,11... | collective-permute-start | bytes 786440 | tf_op jit(solution)/shard_map/ppermute | solution.py:304
  60.2 4.1 %collective-permute-start.20 = (f32[4,16,1024]{2,1,0:T(8,128)S(1)}, f32[4,16,1024]{2,1,0:T(8,128)S(1)}, u32[]{:S(2)}, u32[]{:S(2)}) collective-permute-start(f32[4,16,1024]{2,1,0:T(8,128)S(1)} %gradient_terms.5.after_ref), channel_id=1, source_target_pairs={{0,1},{1,0},{2,3},{3,2},{4,5},{5,4},{6,7},{7,6},{8,9},{9,8},{10,11... | collective-permute-start | bytes 786440 | tf_op jit(solution)/shard_map/ppermute | solution.py:304
  62.0 5.5 %collective-permute-start.21 = (bf16[4,16,1024]{2,1,0:T(8,128)(2,1)S(1)}, bf16[4,16,1024]{2,1,0:T(8,128)(2,1)S(1)}, u32[]{:S(2)}, u32[]{:S(2)}) collective-permute-start(bf16[4,16,1024]{2,1,0:T(8,128)(2,1)S(1)} %add_convert_fusion.after_ref), channel_id=1, source_target_pairs={{0,2},{1,3},{2,0},{3,1},{4,6},{5,7},{6,4},{7,5},{8,10},{9,11},{10,... | collective-permute-start | bytes 393224 | tf_op jit(solution)/shard_map/ppermute | solution.py:304
  67.5 5.8 %collective-permute-start.22 = (bf16[16,1024]{1,0:T(8,128)(2,1)S(1)}, bf16[16,1024]{1,0:T(8,128)(2,1)S(1)}, u32[]{:S(2)}, u32[]{:S(2)}) collective-permute-start(bf16[16,1024]{1,0:T(8,128)(2,1)S(1)} %get-tuple-element.52), channel_id=1, source_target_pairs={{0,12},{1,13},{2,14},{3,15},{4,8},{5,9},{6,10},{7,11},{8,4},{9,5},... | collective-permute-start | bytes 98312 | tf_op jit(solution)/shard_map/ppermute | solution.py:304
  69.9 4.8 %collective-permute-start.23 = (bf16[16,1024]{1,0:T(8,128)(2,1)S(1)}, bf16[16,1024]{1,0:T(8,128)(2,1)S(1)}, u32[]{:S(2)}, u32[]{:S(2)}) collective-permute-start(bf16[16,1024]{1,0:T(8,128)(2,1)S(1)} %get-tuple-element.54), channel_id=1, source_target_pairs={{0,8},{1,9},{2,10},{3,11},{4,12},{5,13},{6,14},{7,15},{8,0},{9,1},... | collective-permute-start | bytes 98312 | tf_op jit(solution)/shard_map/ppermute | solution.py:304
  70.2 4.4 %collective-permute-start.24 = (bf16[16,1024]{1,0:T(8,128)(2,1)S(1)}, bf16[16,1024]{1,0:T(8,128)(2,1)S(1)}, u32[]{:S(2)}, u32[]{:S(2)}) collective-permute-start(bf16[16,1024]{1,0:T(8,128)(2,1)S(1)} %get-tuple-element.53), channel_id=1, source_target_pairs={{0,4},{1,5},{2,6},{3,7},{4,0},{5,1},{6,2},{7,3},{8,12},{9,13},{10,... | collective-permute-start | bytes 98312 | tf_op jit(solution)/shard_map/ppermute | solution.py:304
  (3 other events, 28.6 us)
